TPU v7x, 128 devices: a whole 4x4x4 slice. The times are simulated.
128 devices in a mesh: gx: 32 (over y, x, core), gy: 4 (over z).
Axes of the slice: x: 4, y: 4, z: 4, core: 2. Of those that a mesh axis runs over, the one named last changes fastest.
Arguments:
- density: float32 [256, 16384], P('gx', 'gy'), may hold values from 1 to 2
- momentum: float32 [3, 256, 16384], P(None, 'gx', 'gy'), may hold values from -0.03 to 0.03
- energy: float32 [256, 16384], P('gx', 'gy'), may hold values from 4 to 6
- basis: bfloat16 [16, 3, 256, 16384], P(None, None, 'gx', 'gy'), may hold values from -4 to 4
- scales: float32 [16], replicated, may hold values from 1 to 10
- snapshots: bfloat16 [15, 3, 256, 16384], P(None, None, 'gx', 'gy'), may hold values from -720 to 720
Outputs:
- density_out: float32 [256, 16384], P('gx', 'gy')
- momentum_out: float32 [3, 256, 16384], P(None, 'gx', 'gy')
- energy_out: float32 [256, 16384], P('gx', 'gy')
- modes: bfloat16 [32, 3, 256, 16384], P(None, None, 'gx', 'gy')
- factor: float32 [32, 32], replicated
All inputs are finite; a program needn't handle non-finite values.
Results may differ from a plain program's by a relative error of at most 0.001.
Values sent between devices are 32-bit elements; how exact they have to be, the bound alone decides.
No kernel may reach another device: no remote copies, remote signals or barrier semaphores. Data moves between devices by JAX's collectives and lax.ppermute only.
A program may use at most 128 MiB of HBM per device.

v0:
```python
import functools

import jax
import jax.numpy as jnp
from jax import lax
from jax.experimental import pallas as pl
from jax.experimental.pallas import tpu as pltpu
from jax.sharding import PartitionSpec as P

NZ = 64
LANES = 128
STEP_TIME = 0.03
FIRST = (0.8, -0.2, 4.0 / 105.0, -1.0 / 280.0)
SECOND = (8.0 / 5.0, -0.2, 8.0 / 315.0, -1.0 / 560.0)
CENTRAL = -205.0 / 72.0
VMEM_LIMIT = 48 * 1024 * 1024
WHOLE = pl.BlockSpec(memory_space=pltpu.VMEM)


def lanes_at(index):
    return pl.ds(pl.multiple_of(index * LANES, LANES), LANES)


def row_ids():
    return lax.broadcasted_iota(jnp.int32, (8, LANES), 0)


def lane_ids():
    return lax.broadcasted_iota(jnp.int32, (8, LANES), 1)


def primitives(rho, mx, my, mz, energy):
    inv = 1.0 / rho
    u, v, w = mx * inv, my * inv, mz * inv
    p = 0.4 * (energy - 0.5 * (mx * u + my * v + mz * w))
    return u, v, w, p, p * inv


def pack_sends(state, to_below, to_above, first_y, last_y):
    length = state[0].shape[-1]
    half = length // (2 * LANES)
    low = row_ids() < 4

    def body(j, carry):
        for f in range(5):
            here = state[f][:, lanes_at(j)]
            other = pltpu.roll(state[f][:, lanes_at(j + half)], 4, 0)
            to_below[f, :, lanes_at(j)] = jnp.where(low, here, other)
            to_above[f, :, lanes_at(j)] = jnp.where(low, other, here)
        return carry

    lax.fori_loop(0, half, body, 0)
    width = 4 * NZ
    for f in range(5):
        first_y[f] = state[f][:, :width]
        last_y[f] = state[f][:, length - width :]


def state_views(rho, mom, energy):
    return [rho, mom.at[0], mom.at[1], mom.at[2], energy]


def pack_kernel(rho, mom, energy, to_below, to_above, first_y, last_y):
    pack_sends(state_views(rho, mom, energy), to_below, to_above, first_y, last_y)


def stage_kernel(stage, refs):
    if stage == 0:
        rho, mom, energy, above, below, before, after = refs[:7]
        base = None
        rest = refs[7:]
    else:
        rho, mom, energy, rho0, mom0, energy0, above, below, before, after = refs[:10]
        base = state_views(rho0, mom0, energy0)
        rest = refs[10:]
    if stage < 2:
        rho_o, mom_o, energy_o, to_below, to_above, first_y, last_y = rest[:7]
        ys, yh, hx = rest[7:]
    else:
        rho_o, mom_o, energy_o, newest = rest[:4]
        ys, yh, hx = rest[4:]
    state = state_views(rho, mom, energy)
    outs = state_views(rho_o, mom_o, energy_o)
    length = rho.shape[-1]
    blocks = length // LANES
    half = blocks // 2
    row, lane = row_ids(), lane_ids()
    depth = lane % NZ
    low = row < 4

    def fill(fields, block):
        r, mx, my, mz, e = fields
        u, v, w, p, t = primitives(r, mx, my, mz, e)
        at = lanes_at(block)
        for f, value in enumerate(
            (my, mx * v, my * v + p, mz * v, (e + p) * v, u, v, w, t, p)
        ):
            ys[f, :, at] = value

    def fill_own(j, carry):
        fill([s[:, lanes_at(j)] for s in state], j + 2)
        return carry

    lax.fori_loop(0, blocks, fill_own, 0)
    for j in range(2):
        fill([before[f, :, j * LANES : (j + 1) * LANES] for f in range(5)], j)
        fill([after[f, :, j * LANES : (j + 1) * LANES] for f in range(5)], blocks + 2 + j)

    def shift_half(j, carry):
        for f in range(9):
            here, following = ys[f, :, lanes_at(j)], ys[f, :, lanes_at(j + 1)]
            yh[f, :, lanes_at(j)] = pltpu.roll(
                jnp.where(lane < NZ, following, here), NZ, 1
            )
        return carry

    lax.fori_loop(0, blocks + 3, shift_half, 0)

    def unpack(j, carry):
        for f in range(5):
            a, b = above[f, :, lanes_at(j)], below[f, :, lanes_at(j)]
            hx[f, :, lanes_at(j)] = jnp.where(low, a, b)
            hx[f, :, lanes_at(j + half)] = pltpu.roll(jnp.where(low, b, a), 4, 0)
        return carry

    lax.fori_loop(0, half, unpack, 0)

    def main(j, carry):
        at = lanes_at(j)
        own = [s[:, at] for s in state]
        r, mx, my, mz, e = own
        u, v, w, t, p = [ys[5 + f, :, lanes_at(j + 2)] for f in range(5)]
        energy_p = e + p
        hr, hmx, hmy, hmz, he = [hx[f, :, at] for f in range(5)]
        hu, hv, hw, hp, ht = primitives(hr, hmx, hmy, hmz, he)
        fx = (mx, mx * u + p, my * u, mz * u, energy_p * u, u, v, w, t)
        hfx = (hmx, hmx * hu + hp, hmy * hu, hmz * hu, (he + hp) * hu, hu, hv, hw, ht)
        fz = (mz, mx * w, my * w, mz * w + p, energy_p * w, u, v, w, t)
        result = []
        for f in range(9):
            total = None if f < 5 else (3.0 * CENTRAL) * fx[f]
            swapped_half = pltpu.roll(fz[f], NZ, 1)
            for k in range(1, 5):
                pairs = [
                    (
                        pltpu.roll(jnp.where(row < k, hfx[f], fx[f]), 8 - k, 0),
                        pltpu.roll(jnp.where(row >= 8 - k, hfx[f], fx[f]), k, 0),
                    ),
                    (
                        pltpu.roll(
                            jnp.where(depth < k, swapped_half, fz[f]), LANES - k, 1
                        ),
                        pltpu.roll(
                            jnp.where(depth >= NZ - k, swapped_half, fz[f]), k, 1
                        ),
                    ),
                ]
                if k % 2:
                    up, down = (k - 1) // 2, -(k + 1) // 2
                    pairs.append(
                        (yh[f, :, lanes_at(j + 2 + up)], yh[f, :, lanes_at(j + 2 + down)])
                    )
                else:
                    pairs.append(
                        (
                            ys[f, :, lanes_at(j + 2 + k // 2)],
                            ys[f, :, lanes_at(j + 2 - k // 2)],
                        )
                    )
                if f < 5:
                    s = sum(a - b for a, b in pairs)
                    term = FIRST[k - 1] * s
                else:
                    s = sum(a + b for a, b in pairs)
                    term = SECOND[k - 1] * s
                total = term if total is None else total + term
            result.append(total)
        visc = 0.08 * t
        lap = result[5:]
        work = visc * (u * lap[0] + v * lap[1] + w * lap[2] + 4.9 * lap[3])
        rate = [
            -result[0],
            visc * lap[0] - result[1],
            visc * lap[1] - result[2],
            visc * lap[2] - result[3],
            work - result[4],
        ]
        final = []
        for f in range(5):
            step = own[f] + STEP_TIME * rate[f]
            if stage == 1:
                step = 0.75 * base[f][:, at] + 0.25 * step
            elif stage == 2:
                step = base[f][:, at] * (1.0 / 3.0) + (2.0 / 3.0) * step
            outs[f][:, at] = step
            final.append(step)
        if stage == 2:
            inv = 1.0 / final[0]
            for c in range(3):
                newest[c, :, at] = final[1 + c] * inv
        return carry

    lax.fori_loop(0, blocks, main, 0)
    if stage < 2:
        pack_sends(outs, to_below, to_above, first_y, last_y)


def f32(*shape):
    return jax.ShapeDtypeStruct(shape, jnp.float32)


def call(kernel, out_shape, args, scratch=(), flops=0, nbytes=0, **kw):
    return pl.pallas_call(
        kernel,
        out_shape=out_shape,
        scratch_shapes=list(scratch),
        compiler_params=pltpu.CompilerParams(vmem_limit_bytes=VMEM_LIMIT),
        cost_estimate=pl.CostEstimate(
            flops=flops, bytes_accessed=nbytes, transcendentals=0
        ),
        **kw,
    )(*args)


def state_shapes(rows, length):
    return (f32(rows, length), f32(3, rows, length), f32(rows, length))


def send_shapes(rows, length):
    packed = f32(5, rows, length // 2)
    edge = f32(5, rows, 4 * NZ)
    return (packed, packed, edge, edge)


def pack(state):
    rows, length = state[0].shape
    shapes = send_shapes(rows, length)
    return call(
        pack_kernel,
        shapes,
        state,
        in_specs=[WHOLE] * 3,
        out_specs=[WHOLE] * 4,
        nbytes=10**6,
    )


def stage_call(stage, state, base, halo):
    rows, length = state[0].shape
    out = state_shapes(rows, length)
    out += send_shapes(rows, length) if stage < 2 else (f32(3, rows, length),)
    args = tuple(state) + (tuple(base) if stage else ()) + tuple(halo)
    scratch = [
        pltpu.VMEM((10, rows, length + 8 * NZ), jnp.float32),
        pltpu.VMEM((9, rows, length + 8 * NZ), jnp.float32),
        pltpu.VMEM((5, rows, length), jnp.float32),
    ]
    return call(
        lambda *refs: stage_kernel(stage, refs),
        out,
        args,
        scratch,
        in_specs=[WHOLE] * len(args),
        out_specs=[WHOLE] * len(out),
        flops=32768 * 700,
        nbytes=3 * 10**6,
    )


def merged_rows(basis, snaps, c):
    first = basis[:, c].astype(jnp.float32)
    second = snaps[:, c].astype(jnp.float32)
    length = first.shape[-1]
    rows = jnp.concatenate([first, second, jnp.zeros((1, 8, length), jnp.float32)], 0)
    return rows.reshape(256, length).astype(jnp.bfloat16)


def group_matrix(shape, group_dim, dtype):
    g = lax.broadcasted_iota(jnp.int32, shape, group_dim)
    o = lax.broadcasted_iota(jnp.int32, shape, 1 - group_dim)
    return (g // 8 == o).astype(dtype)


def same_layer():
    r = lax.broadcasted_iota(jnp.int32, (256, 256), 0)
    c = lax.broadcasted_iota(jnp.int32, (256, 256), 1)
    return r % 8 == c % 8


def gram_kernel(basis, snaps, gram, total):
    step = pl.program_id(0)

    @pl.when(step == 0)
    def _():
        total[...] = jnp.zeros_like(total)

    for c in range(3):
        rows = merged_rows(basis, snaps, c)
        total[...] += lax.dot_general(
            rows, rows, (((1,), (1,)), ((), ())), preferred_element_type=jnp.float32
        )

    @pl.when(step == pl.num_programs(0) - 1)
    def _():
        kept = jnp.where(same_layer(), total[...], 0.0)
        left = group_matrix((32, 256), 1, jnp.float32)
        right = group_matrix((256, 32), 0, jnp.float32)
        small = jnp.dot(left, kept, precision=lax.Precision.HIGHEST)
        small = jnp.dot(small, right, precision=lax.Precision.HIGHEST)
        for g in range(4):
            gram[:, 32 * g : 32 * g + 32] = small[8 * g : 8 * g + 8]


def column_specs(width):
    return [
        pl.BlockSpec((16, 3, 8, width), lambda i: (0, 0, 0, i)),
        pl.BlockSpec((15, 3, 8, width), lambda i: (0, 0, 0, i)),
    ]


def gram_call(basis, snaps, width=1024):
    length = basis.shape[-1]
    return call(
        gram_kernel,
        f32(8, LANES),
        (basis, snaps),
        [pltpu.VMEM((256, 256), jnp.float32)],
        grid=(length // width,),
        in_specs=column_specs(width),
        out_specs=pl.BlockSpec((8, LANES), lambda i: (0, 0)),
        flops=2 * 256 * 256 * 3 * length,
        nbytes=31 * 3 * 8 * length * 2,
    )


def factor_kernel(weight, gram, scale, upper, lower, high, low):
    row = lax.broadcasted_iota(jnp.int32, (32, 32), 0)
    col = lax.broadcasted_iota(jnp.int32, (32, 32), 1)
    s = jnp.broadcast_to(scale[...], (32, 32))
    s_col = jnp.sum(jnp.where(row == col, s, 0.0), axis=1, keepdims=True)
    g = jnp.concatenate([gram[:, 32 * i : 32 * i + 32] for i in range(4)], 0)
    g = g * (weight * s) * s_col
    inside = (row < 31) & (col < 31)
    eye = (row == col).astype(jnp.float32)
    g = jnp.where(inside, g, eye)
    work = jnp.concatenate([g, eye, jnp.zeros((32, 64), jnp.float32)], 1)
    rows128 = lax.broadcasted_iota(jnp.int32, (32, LANES), 0)
    done = jnp.zeros((32, LANES), jnp.float32)
    for j in range(31):
        column = jnp.broadcast_to(work[:, j : j + 1], (32, LANES))
        pivot_row = jnp.broadcast_to(work[j : j + 1], (32, LANES))
        pivot = jnp.broadcast_to(column[j : j + 1], (32, LANES))
        done = jnp.where(rows128 == j, pivot_row / jnp.sqrt(pivot), done)
        work = work - column * (pivot_row / pivot)
    r = jnp.where((col >= row) & inside, done[:, :32], 0.0)
    l = jnp.where((col <= row) & inside, done[:, 32:64], 0.0)
    upper[...] = r
    lower[...] = l
    scaled = l * s
    hi = scaled.astype(jnp.bfloat16)
    lo = (scaled - hi.astype(jnp.float32)).astype(jnp.bfloat16)
    left = group_matrix((256, 32), 0, jnp.bfloat16)
    right = group_matrix((32, 256), 1, jnp.bfloat16)
    keep = same_layer()
    for part, out in ((hi, high), (lo, low)):
        wide = jnp.dot(left, part, preferred_element_type=jnp.float32)
        wide = jnp.dot(
            wide.astype(jnp.bfloat16), right, preferred_element_type=jnp.float32
        )
        out[...] = jnp.where(keep, wide, 0.0).astype(jnp.bfloat16)


def factor_call(gram, scale, weight):
    square = jax.ShapeDtypeStruct((256, 256), jnp.bfloat16)
    return call(
        functools.partial(factor_kernel, weight),
        (f32(32, 32), f32(32, 32), square, square),
        (gram, scale),
        in_specs=[WHOLE] * 2,
        out_specs=[WHOLE] * 4,
        flops=10**7,
        nbytes=10**6,
    )


def modes_kernel(basis, snaps, high, low, modes):
    for c in range(3):
        rows = merged_rows(basis, snaps, c)
        out = jnp.dot(high[...], rows, preferred_element_type=jnp.float32)
        out = out + jnp.dot(low[...], rows, preferred_element_type=jnp.float32)
        modes[:, c] = out.reshape(32, 8, out.shape[-1]).astype(jnp.bfloat16)


def modes_call(basis, snaps, high, low, width=1024):
    length = basis.shape[-1]
    whole = pl.BlockSpec((256, 256), lambda i: (0, 0))
    return call(
        modes_kernel,
        jax.ShapeDtypeStruct((32, 3, 8, length), jnp.bfloat16),
        (basis, snaps, high, low),
        grid=(length // width,),
        in_specs=column_specs(width) + [whole, whole],
        out_specs=pl.BlockSpec((32, 3, 8, width), lambda i: (0, 0, 0, i)),
        flops=4 * 256 * 256 * 3 * length,
        nbytes=63 * 3 * 8 * length * 2,
    )


def cross_kernel(basis, snaps, newest, cross, total):
    step = pl.program_id(0)
    width = newest.shape[-1]

    @pl.when(step == 0)
    def _():
        total[...] = jnp.zeros_like(total)

    new = [newest[c] for c in range(3)]

    def add(k, value):
        folded = sum(
            value[:, i * LANES : (i + 1) * LANES] for i in range(width // LANES)
        )
        total[k] += folded

    for k in range(31):
        ref, i = (basis, k) if k < 16 else (snaps, k - 16)
        add(k, sum(ref[i, c].astype(jnp.float32) * new[c] for c in range(3)))
    add(31, sum(n * n for n in new))

    @pl.when(step == pl.num_programs(0) - 1)
    def _():
        sums = jnp.sum(total[...], axis=1)
        line = lax.dot_general(
            jnp.ones((8, LANES), jnp.float32),
            sums,
            (((1,), (1,)), ((), ())),
            precision=lax.Precision.HIGHEST,
        )
        line = jnp.concatenate([line, jnp.zeros((8, 96), jnp.float32)], 1)
        cross[...] = jnp.broadcast_to(line[:1], cross.shape)


def cross_call(basis, snaps, newest, copies, width=512):
    length = basis.shape[-1]
    return call(
        cross_kernel,
        f32(copies, LANES),
        (basis, snaps, newest),
        [pltpu.VMEM((32, 8, LANES), jnp.float32)],
        grid=(length // width,),
        in_specs=column_specs(width) + [pl.BlockSpec((3, 8, width), lambda i: (0, 0, i))],
        out_specs=pl.BlockSpec((copies, LANES), lambda i: (0, 0)),
        flops=31 * 6 * 8 * length,
        nbytes=31 * 3 * 8 * length * 2,
    )


def last_kernel(
    weight, parts, scale, upper, lower, basis, snaps, newest, held, modes, factor, coef
):
    @pl.when(pl.program_id(0) == 0)
    def _():
        row = lax.broadcasted_iota(jnp.int32, (32, 32), 0)
        col = lax.broadcasted_iota(jnp.int32, (32, 32), 1)
        line = jnp.sum(parts[...], axis=0, keepdims=True)[:, :32]
        line = line * (weight * scale[...])
        l = lower[...]
        r = jnp.sum(l * line, axis=1, keepdims=True)
        rest = line[:, 31:32] - jnp.sum(r * r, axis=0, keepdims=True)
        diagonal = jnp.sqrt(rest)
        last = jnp.where(row < 31, r, diagonal)
        factor[...] = jnp.where(col == 31, last, upper[...])
        w = -jnp.sum(r * l, axis=0, keepdims=True) * scale[...] / diagonal
        w = jnp.where(col[:1] == 31, 1.0 / diagonal, w)
        for k in range(32):
            coef[k] = jnp.broadcast_to(w[:, k : k + 1], (8, LANES))

    width = newest.shape[-1]
    for i in range(width // LANES):
        at = slice(i * LANES, (i + 1) * LANES)
        totals = [coef[31] * newest[c, :, at] for c in range(3)]
        for k in range(31):
            ref, n = (basis, k) if k < 16 else (snaps, k - 16)
            for c in range(3):
                totals[c] = totals[c] + coef[k] * ref[n, c, :, at].astype(jnp.float32)
        for c in range(3):
            modes[0, c, :, at] = totals[c].astype(jnp.bfloat16)


def last_call(parts, scale, upper, lower, basis, snaps, newest, modes, weight, width=512):
    length = basis.shape[-1]
    small = pl.BlockSpec((32, 32), lambda i: (0, 0))
    return call(
        functools.partial(last_kernel, weight),
        (jax.ShapeDtypeStruct(modes.shape, modes.dtype), f32(32, 32)),
        (parts, scale, upper, lower, basis, snaps, newest, modes),
        [pltpu.VMEM((32, 8, LANES), jnp.float32)],
        grid=(length // width,),
        in_specs=[
            pl.BlockSpec(parts.shape, lambda i: (0, 0)),
            pl.BlockSpec((1, 32), lambda i: (0, 0)),
            small,
            small,
        ]
        + column_specs(width)
        + [
            pl.BlockSpec((3, 8, width), lambda i: (0, 0, i)),
            pl.BlockSpec(memory_space=pl.ANY),
        ],
        out_specs=[pl.BlockSpec((1, 3, 8, width), lambda i: (31, 0, 0, i)), small],
        input_output_aliases={7: 0},
        flops=31 * 6 * 8 * length,
        nbytes=31 * 3 * 8 * length * 2,
    )


def shifted(block, axis, distance):
    count = lax.axis_size(axis)
    route = [(i, (i + distance) % count) for i in range(count)]
    return lax.ppermute(block, axis, route)


def exchange(sends):
    to_below, to_above, first_y, last_y = sends
    above = shifted(to_below, "gx", -1)
    below = shifted(to_above, "gx", 1)
    before = shifted(last_y, "gy", 1)
    after = shifted(first_y, "gy", -1)
    return (above, below, before, after)


def summed(block, axis):
    count = lax.axis_size(axis)
    distance = 1
    while distance < count:
        route = [(i, i ^ distance) for i in range(count)]
        block = block + lax.ppermute(block, axis, route)
        distance *= 2
    return block


def local(density, momentum, energy, basis, scales, snapshots):
    rows, length = density.shape
    devices = lax.axis_size("gx") * lax.axis_size("gy")
    weight = 1.0 / (3 * rows * length * devices)
    fields = (density, momentum, energy)
    scale = jnp.concatenate([scales, jnp.ones((16,), jnp.float32)])[None]

    halo = exchange(pack(fields))
    gram = gram_call(basis, snapshots)
    first = stage_call(0, fields, None, halo)
    gram = summed(summed(gram, "gx"), "gy")
    halo = exchange(first[3:])
    second = stage_call(1, first[:3], fields, halo)
    upper, lower, high, low = factor_call(gram, scale, weight)
    halo = exchange(second[3:])
    modes = modes_call(basis, snapshots, high, low)
    final = stage_call(2, second[:3], fields, halo)
    newest = final[3]
    cross = cross_call(basis, snapshots, newest, devices)
    parts = lax.all_to_all(cross, ("gx", "gy"), 0, 0, tiled=True)
    modes, factor = last_call(
        parts, scale, upper, lower, basis, snapshots, newest, modes, weight
    )
    return (final[0], final[1], final[2], modes, factor)


def solution(mesh):
    field, vector = P("gx", "gy"), P(None, "gx", "gy")
    columns = P(None, None, "gx", "gy")
    return jax.shard_map(
        local,
        mesh=mesh,
        in_specs=(field, vector, field, columns, P(), columns),
        out_specs=(field, vector, field, columns, P()),
        check_vma=False,
    )
```

profile of v0, /device:TPU:1, one launch (start us, length us, event | category | flops | bytes accessed | tf_op | source)
XLA Modules:
  0.0 135.3 jit_solution(15077408668444665449)
XLA Ops:
  6.5 1.6 %collective-permute-start.2 = (f32[5,8,256]{2,1,0:T(8,128)S(1)}, f32[5,8,256]{2,1,0:T(8,128)S(1)}, u32[]{:S(2)}, u32[]{:S(2)}) collective-permute-start(f32[5,8,256]{2,1,0:T(8,128)S(1)} %get-tuple-element.35), channel_id=1, source_target_pairs={{0,1},{1,2},{2,3},{3,0},{4,5},{5,6},{6,7},{7,4},{8,9},{9,10},{10,1... | collective-permute-start | bytes 122888 | tf_op jit(solution)/shard_map/ppermute | solution.py:520
  8.2 2.1 %collective-permute-start.3 = (f32[5,8,256]{2,1,0:T(8,128)S(1)}, f32[5,8,256]{2,1,0:T(8,128)S(1)}, u32[]{:S(2)}, u32[]{:S(2)}) collective-permute-start(f32[5,8,256]{2,1,0:T(8,128)S(1)} %get-tuple-element.36), channel_id=1, source_target_pairs={{0,3},{1,0},{2,1},{3,2},{4,7},{5,4},{6,5},{7,6},{8,11},{9,8},{10,9... | collective-permute-start | bytes 122888 | tf_op jit(solution)/shard_map/ppermute | solution.py:520
  11.7 10.7 %shard_map.102 = (f32[8,4096]{1,0:T(8,128)S(1)}, f32[3,8,4096]{2,1,0:T(8,128)S(1)}, f32[8,4096]{1,0:T(8,128)S(1)}, f32[5,8,2048]{2,1,0:T(8,128)S(1)}, f32[5,8,20...) custom-call(f32[8,4096]{1,0:T(8,128)S(1)} %copy-done.5, f32[3,8,4096]{2,1,0:T(8,128)S(1)} %copy-done.3, ...), custom_call_target="tpu_custom_call" | custom-call | flops 22937600 | bytes 3000000 | tf_op jit(solution)/shard_map/pallas_call | solution.py:213
  22.4 8.2 %collective-permute-start.4 = (f32[5,8,2048]{2,1,0:T(8,128)S(1)}, f32[5,8,2048]{2,1,0:T(8,128)S(1)}, u32[]{:S(2)}, u32[]{:S(2)}) collective-permute-start(f32[5,8,2048]{2,1,0:T(8,128)S(1)} %get-tuple-element.40), channel_id=1, source_target_pairs={{0,124},{4,0},{8,4},{12,8},{16,12},{20,16},{24,20},{28,24},{32,28}... | collective-permute-start | bytes 983048 | tf_op jit(solution)/shard_map/ppermute | solution.py:520
  30.6 1.6 %collective-permute-start.6 = (f32[5,8,256]{2,1,0:T(8,128)S(1)}, f32[5,8,256]{2,1,0:T(8,128)S(1)}, u32[]{:S(2)}, u32[]{:S(2)}) collective-permute-start(f32[5,8,256]{2,1,0:T(8,128)S(1)} %get-tuple-element.42), channel_id=1, source_target_pairs={{0,1},{1,2},{2,3},{3,0},{4,5},{5,6},{6,7},{7,4},{8,9},{9,10},{10,1... | collective-permute-start | bytes 122888 | tf_op jit(solution)/shard_map/ppermute | solution.py:520
  32.3 2.1 %collective-permute-start.7 = (f32[5,8,256]{2,1,0:T(8,128)S(1)}, f32[5,8,256]{2,1,0:T(8,128)S(1)}, u32[]{:S(2)}, u32[]{:S(2)}) collective-permute-start(f32[5,8,256]{2,1,0:T(8,128)S(1)} %get-tuple-element.43), channel_id=1, source_target_pairs={{0,3},{1,0},{2,1},{3,2},{4,7},{5,4},{6,5},{7,6},{8,11},{9,8},{10,9... | collective-permute-start | bytes 122888 | tf_op jit(solution)/shard_map/ppermute | solution.py:520
  35.8 10.9 %shard_map.103 = (f32[8,4096]{1,0:T(8,128)S(1)}, f32[3,8,4096]{2,1,0:T(8,128)S(1)}, f32[8,4096]{1,0:T(8,128)S(1)}, f32[5,8,2048]{2,1,0:T(8,128)S(1)}, f32[5,8,20...) custom-call(f32[8,4096]{1,0:T(8,128)S(1)} %get-tuple-element.37.refs_0_, ...), custom_call_target="tpu_custom_call" | custom-call | flops 22937600 | bytes 3000000 | tf_op jit(solution)/shard_map/pallas_call | solution.py:213
  46.7 5.1 %collective-permute-start.8 = (f32[5,8,2048]{2,1,0:T(8,128)S(1)}, f32[5,8,2048]{2,1,0:T(8,128)S(1)}, u32[]{:S(2)}, u32[]{:S(2)}) collective-permute-start(f32[5,8,2048]{2,1,0:T(8,128)S(1)} %get-tuple-element.47), channel_id=1, source_target_pairs={{0,124},{4,0},{8,4},{12,8},{16,12},{20,16},{24,20},{28,24},{32,28}... | collective-permute-start | bytes 983048 | tf_op jit(solution)/shard_map/ppermute | solution.py:520
  51.8 1.9 %copy-done = bf16[16,3,8,4096]{3,2,1,0:T(8,128)(2,1)S(1)} copy-done((bf16[16,3,8,4096]{3,2,1,0:T(8,128)(2,1)S(1)}, bf16[16,3,8,4096]{3,2,1,0:T(8,128)(2,1)}, u32[]{:S(2)}) %copy-start) | copy-done | bytes 3145752
  53.7 1.8 %copy-done.1 = bf16[15,3,8,4096]{3,2,1,0:T(8,128)(2,1)S(1)} copy-done((bf16[15,3,8,4096]{3,2,1,0:T(8,128)(2,1)S(1)}, bf16[15,3,8,4096]{3,2,1,0:T(8,128)(2,1)}, u32[]{:S(2)}) %copy-start.1) | copy-done | bytes 2949144
  55.5 3.5 %shard_map.106 = f32[8,128]{1,0:T(8,128)S(1)} custom-call(bf16[16,3,8,4096]{3,2,1,0:T(8,128)(2,1)S(1)} %copy-done, bf16[15,3,8,4096]{3,2,1,0:T(8,128)(2,1)S(1)} %copy-done.1), custom_call_target="tpu_custom_call" | custom-call | flops 1610612736 | bytes 6094848 | tf_op jit(solution)/shard_map/pallas_call | solution.py:213
  60.4 2.5 %collective-permute-done.13 = f32[8,128]{1,0:T(8,128)S(1)} collective-permute-done((f32[8,128]{1,0:T(8,128)S(1)}, f32[8,128]{1,0:T(8,128)S(1)}, u32[]{:S(2)}, u32[]{:S(2)}) %collective-permute-start.13) | collective-permute-done | bytes 4128 | tf_op jit(solution)/shard_map/ppermute | solution.py:537
  62.9 4.0 %collective-permute-done.14 = f32[8,128]{1,0:T(8,128)S(1)} collective-permute-done((f32[8,128]{1,0:T(8,128)S(1)}, f32[8,128]{1,0:T(8,128)S(1)}, u32[]{:S(2)}, u32[]{:S(2)}) %collective-permute-start.14) | collective-permute-done | bytes 4128 | tf_op jit(solution)/shard_map/ppermute | solution.py:537
  66.8 2.5 %collective-permute-done.15 = f32[8,128]{1,0:T(8,128)S(1)} collective-permute-done((f32[8,128]{1,0:T(8,128)S(1)}, f32[8,128]{1,0:T(8,128)S(1)}, u32[]{:S(2)}, u32[]{:S(2)}) %collective-permute-start.15) | collective-permute-done | bytes 4128 | tf_op jit(solution)/shard_map/ppermute | solution.py:537
  70.6 2.6 %collective-permute-done.16 = f32[8,128]{1,0:T(8,128)S(1)} collective-permute-done((f32[8,128]{1,0:T(8,128)S(1)}, f32[8,128]{1,0:T(8,128)S(1)}, u32[]{:S(2)}, u32[]{:S(2)}) %collective-permute-start.16) | collective-permute-done | bytes 4128 | tf_op jit(solution)/shard_map/ppermute | solution.py:537
  75.7 3.3 %collective-permute-start.18 = (f32[8,128]{1,0:T(8,128)S(1)}, f32[8,128]{1,0:T(8,128)S(1)}, u32[]{:S(2)}, u32[]{:S(2)}) collective-permute-start(f32[8,128]{1,0:T(8,128)S(1)} %add.28), channel_id=1, source_target_pairs={{0,2},{1,3},{2,0},{3,1},{4,6},{5,7},{6,4},{7,5},{8,10},{9,11},{10,... | collective-permute-start | bytes 12296 | tf_op jit(solution)/shard_map/ppermute | solution.py:537
  79.7 1.9 %collective-permute-start.11 = (f32[5,8,256]{2,1,0:T(8,128)S(1)}, f32[5,8,256]{2,1,0:T(8,128)S(1)}, u32[]{:S(2)}, u32[]{:S(2)}) collective-permute-start(f32[5,8,256]{2,1,0:T(8,128)S(1)} %get-tuple-element.50), channel_id=1, source_target_pairs={{0,3},{1,0},{2,1},{3,2},{4,7},{5,4},{6,5},{7,6},{8,11},{9,8},{10,9... | collective-permute-start | bytes 122888 | tf_op jit(solution)/shard_map/ppermute | solution.py:520
  81.7 4.4 %shard_map.107 = (f32[32,32]{1,0:T(8,128)S(1)}, f32[32,32]{1,0:T(8,128)S(1)}, bf16[256,256]{1,0:T(8,128)(2,1)S(1)}, bf16[256,256]{1,0:T(8,128)(2,1)S(1)}) custom-call(f32[8,128]{1,0:T(8,128)S(1)} %add.29.gram, f32[1,32]{1,0:T(1,128)S(1)} %pad_bitcast_fusion.scale), custom_call_target="tpu_custom_call" | custom-call | flops 10000000 | bytes 1000000 | tf_op jit(solution)/shard_map/pallas_call | solution.py:213
  86.9 11.5 %shard_map.104 = (f32[8,4096]{1,0:T(8,128)}, f32[3,8,4096]{2,1,0:T(8,128)}, f32[8,4096]{1,0:T(8,128)}, f32[3,8,4096]{2,1,0:T(8,128)S(1)}) custom-call(f32[8,4096]{1,0:T(8,128)S(1)} %get-tuple-element.44.refs_0_, f32[3,8,4096]{2,1,0:T(8,128)S(1)} %get-tuple-element.45.refs_1_, f32[8,4096]{1,0:T(8,128)S(1)} %get-tuple-element.46.refs_2_, ...), custom_call_target="tpu_custom_call" | custom-call | flops 22937600 | bytes 3000000 | tf_op jit(solution)/shard_map/pallas_call | solution.py:213
  98.3 5.7 %shard_map.105 = f32[128,128]{1,0:T(8,128)} custom-call(bf16[16,3,8,4096]{3,2,1,0:T(8,128)(2,1)} %basis.7, bf16[15,3,8,4096]{3,2,1,0:T(8,128)(2,1)S(1)} %copy-done.2, f32[3,8,4096]{2,1,0:T(8,128)S(1)} %get-tuple-element.54.newest), custom_call_target="tpu_custom_call" | custom-call | flops 6094848 | bytes 6094848 | tf_op jit(solution)/shard_map/pallas_call | solution.py:213
  104.1 13.9 %all-to-all-start = ((f32[128,1,128]{2,1,0:T(1,128)}), f32[128,1,128]{2,1,0:T(1,128)S(1)}, u32[]{:S(2)}, u32[]{:S(2)}) async-start(f32[128,1,128]{2,1,0:T(1,128)} %bitcast.1), calls=%async_computation | async-start | bytes 131072 | tf_op jit(solution)/shard_map/all_to_all | solution.py:561
  118.9 7.1 %shard_map.108.held = bf16[32,3,8,4096]{3,2,1,0:T(8,128)(2,1)} custom-call(bf16[16,3,8,4096]{3,2,1,0:T(8,128)(2,1)} %basis.7, bf16[15,3,8,4096]{3,2,1,0:T(8,128)(2,1)S(1)} %copy-done.2, bf16[256,256]{1,0:T(8,128)(2,1)S(1)} %get-tuple-element.57.high, bf16[256,256]{1,0:T(8,128)(2,1)S(1)} %copy-done.10), custom_call_target="tpu_custom_call" | custom-call | flops 3221225472 | bytes 12386304 | tf_op jit(solution)/shard_map/pallas_call | solution.py:213
  126.0 1.6 %all-to-all-done = f32[128,1,128]{2,1,0:T(1,128)S(1)} async-done(((f32[128,1,128]{2,1,0:T(1,128)}), f32[128,1,128]{2,1,0:T(1,128)S(1)}, u32[]{:S(2)}, u32[]{:S(2)}) %all-to-all-start) | async-done | bytes 65568 | tf_op jit(solution)/shard_map/all_to_all | solution.py:561
  128.9 6.3 %shard_map.109 = (bf16[32,3,8,4096]{3,2,1,0:T(8,128)(2,1)}, f32[32,32]{1,0:T(8,128)}) custom-call(f32[128,128]{1,0:T(8,128)S(1)} %bitcast.6, f32[1,32]{1,0:T(1,128)S(1)} %copy-done.14, f32[32,32]{1,0:T(8,128)S(1)} %get-tuple-element.55.upper, f32[32,32]{1,0:T(8,128)S(1)} %copy-done.12, ...), custom_call_target="tpu_custom_call", output_to_operand_aliasing={{0}: (7, {})} | custom-call | flops 6094848 | bytes 6094848 | tf_op jit(solution)/shard_map/pallas_call | solution.py:213
  (65 shorter events, 17.5 us)
Async XLA Ops:
  0.6 97.7 %copy-start.2 = (bf16[15,3,8,4096]{3,2,1,0:T(8,128)(2,1)S(1)}, bf16[15,3,8,4096]{3,2,1,0:T(8,128)(2,1)}, u32[]{:S(2)}) copy-start(bf16[15,3,8,4096]{3,2,1,0:T(8,128)(2,1)} %snaps.7) | copy-start | bytes 8847364
  3.6 83.2 %copy-start.4 = (f32[3,8,4096]{2,1,0:T(8,128)S(1)}, f32[3,8,4096]{2,1,0:T(8,128)}, u32[]{:S(2)}) copy-start(f32[3,8,4096]{2,1,0:T(8,128)} %refs_4_.3) | copy-start | bytes 1179652
  3.6 83.2 %copy-start.6 = (f32[8,4096]{1,0:T(8,128)S(1)}, f32[8,4096]{1,0:T(8,128)}, u32[]{:S(2)}) copy-start(f32[8,4096]{1,0:T(8,128)} %refs_3_.3) | copy-start | bytes 393220
  3.6 83.3 %copy-start.8 = (f32[8,4096]{1,0:T(8,128)S(1)}, f32[8,4096]{1,0:T(8,128)}, u32[]{:S(2)}) copy-start(f32[8,4096]{1,0:T(8,128)} %refs_5_.3) | copy-start | bytes 393220
  3.8 7.9 %collective-permute-start = (f32[5,8,2048]{2,1,0:T(8,128)S(1)}, f32[5,8,2048]{2,1,0:T(8,128)S(1)}, u32[]{:S(2)}, u32[]{:S(2)}) collective-permute-start(f32[5,8,2048]{2,1,0:T(8,128)S(1)} %get-tuple-element.33), channel_id=1, source_target_pairs={{0,124},{4,0},{8,4},{12,8},{16,12},{20,16},{24,20},{28,24},{32,28}... | collective-permute-start | bytes 983048 | tf_op jit(solution)/shard_map/ppermute | solution.py:520
  5.3 6.4 %collective-permute-start.1 = (f32[5,8,2048]{2,1,0:T(8,128)S(1)}, f32[5,8,2048]{2,1,0:T(8,128)S(1)}, u32[]{:S(2)}, u32[]{:S(2)}) collective-permute-start(f32[5,8,2048]{2,1,0:T(8,128)S(1)} %get-tuple-element.34), channel_id=1, source_target_pairs={{0,4},{4,8},{8,12},{12,16},{16,20},{20,24},{24,28},{28,32},{32,36}... | collective-permute-start | bytes 983048 | tf_op jit(solution)/shard_map/ppermute | solution.py:520
  6.5 5.1 %collective-permute-start.2 = (f32[5,8,256]{2,1,0:T(8,128)S(1)}, f32[5,8,256]{2,1,0:T(8,128)S(1)}, u32[]{:S(2)}, u32[]{:S(2)}) collective-permute-start(f32[5,8,256]{2,1,0:T(8,128)S(1)} %get-tuple-element.35), channel_id=1, source_target_pairs={{0,1},{1,2},{2,3},{3,0},{4,5},{5,6},{6,7},{7,4},{8,9},{9,10},{10,1... | collective-permute-start | bytes 122888 | tf_op jit(solution)/shard_map/ppermute | solution.py:520
  8.2 3.5 %collective-permute-start.3 = (f32[5,8,256]{2,1,0:T(8,128)S(1)}, f32[5,8,256]{2,1,0:T(8,128)S(1)}, u32[]{:S(2)}, u32[]{:S(2)}) collective-permute-start(f32[5,8,256]{2,1,0:T(8,128)S(1)} %get-tuple-element.36), channel_id=1, source_target_pairs={{0,3},{1,0},{2,1},{3,2},{4,7},{5,4},{6,5},{7,6},{8,11},{9,8},{10,9... | collective-permute-start | bytes 122888 | tf_op jit(solution)/shard_map/ppermute | solution.py:520
  22.4 13.3 %collective-permute-start.4 = (f32[5,8,2048]{2,1,0:T(8,128)S(1)}, f32[5,8,2048]{2,1,0:T(8,128)S(1)}, u32[]{:S(2)}, u32[]{:S(2)}) collective-permute-start(f32[5,8,2048]{2,1,0:T(8,128)S(1)} %get-tuple-element.40), channel_id=1, source_target_pairs={{0,124},{4,0},{8,4},{12,8},{16,12},{20,16},{24,20},{28,24},{32,28}... | collective-permute-start | bytes 983048 | tf_op jit(solution)/shard_map/ppermute | solution.py:520
  30.6 5.2 %collective-permute-start.5 = (f32[5,8,2048]{2,1,0:T(8,128)S(1)}, f32[5,8,2048]{2,1,0:T(8,128)S(1)}, u32[]{:S(2)}, u32[]{:S(2)}) collective-permute-start(f32[5,8,2048]{2,1,0:T(8,128)S(1)} %get-tuple-element.41), channel_id=1, source_target_pairs={{0,4},{4,8},{8,12},{12,16},{16,20},{20,24},{24,28},{28,32},{32,36}... | collective-permute-start | bytes 983048 | tf_op jit(solution)/shard_map/ppermute | solution.py:520
  30.6 5.1 %collective-permute-start.6 = (f32[5,8,256]{2,1,0:T(8,128)S(1)}, f32[5,8,256]{2,1,0:T(8,128)S(1)}, u32[]{:S(2)}, u32[]{:S(2)}) collective-permute-start(f32[5,8,256]{2,1,0:T(8,128)S(1)} %get-tuple-element.42), channel_id=1, source_target_pairs={{0,1},{1,2},{2,3},{3,0},{4,5},{5,6},{6,7},{7,4},{8,9},{9,10},{10,1... | collective-permute-start | bytes 122888 | tf_op jit(solution)/shard_map/ppermute | solution.py:520
  32.3 3.5 %collective-permute-start.7 = (f32[5,8,256]{2,1,0:T(8,128)S(1)}, f32[5,8,256]{2,1,0:T(8,128)S(1)}, u32[]{:S(2)}, u32[]{:S(2)}) collective-permute-start(f32[5,8,256]{2,1,0:T(8,128)S(1)} %get-tuple-element.43), channel_id=1, source_target_pairs={{0,3},{1,0},{2,1},{3,2},{4,7},{5,4},{6,5},{7,6},{8,11},{9,8},{10,9... | collective-permute-start | bytes 122888 | tf_op jit(solution)/shard_map/ppermute | solution.py:520
  46.7 40.2 %collective-permute-start.8 = (f32[5,8,2048]{2,1,0:T(8,128)S(1)}, f32[5,8,2048]{2,1,0:T(8,128)S(1)}, u32[]{:S(2)}, u32[]{:S(2)}) collective-permute-start(f32[5,8,2048]{2,1,0:T(8,128)S(1)} %get-tuple-element.47), channel_id=1, source_target_pairs={{0,124},{4,0},{8,4},{12,8},{16,12},{20,16},{24,20},{28,24},{32,28}... | collective-permute-start | bytes 983048 | tf_op jit(solution)/shard_map/ppermute | solution.py:520
  51.8 35.0 %collective-permute-start.9 = (f32[5,8,2048]{2,1,0:T(8,128)S(1)}, f32[5,8,2048]{2,1,0:T(8,128)S(1)}, u32[]{:S(2)}, u32[]{:S(2)}) collective-permute-start(f32[5,8,2048]{2,1,0:T(8,128)S(1)} %get-tuple-element.48), channel_id=1, source_target_pairs={{0,4},{4,8},{8,12},{12,16},{16,20},{20,24},{24,28},{28,32},{32,36}... | collective-permute-start | bytes 983048 | tf_op jit(solution)/shard_map/ppermute | solution.py:520
  59.0 1.4 %collective-permute-start.12 = (f32[8,128]{1,0:T(8,128)S(1)}, f32[8,128]{1,0:T(8,128)S(1)}, u32[]{:S(2)}, u32[]{:S(2)}) collective-permute-start(f32[8,128]{1,0:T(8,128)S(1)} %shard_map.106), channel_id=1, source_target_pairs={{0,4},{4,0},{8,12},{12,8},{16,20},{20,16},{24,28},{28,24},{32,36},... | collective-permute-start | bytes 12296 | tf_op jit(solution)/shard_map/ppermute | solution.py:537
  60.4 2.5 %collective-permute-start.13 = (f32[8,128]{1,0:T(8,128)S(1)}, f32[8,128]{1,0:T(8,128)S(1)}, u32[]{:S(2)}, u32[]{:S(2)}) collective-permute-start(f32[8,128]{1,0:T(8,128)S(1)} %add.23), channel_id=1, source_target_pairs={{0,8},{4,12},{8,0},{12,4},{16,24},{20,28},{24,16},{28,20},{32,40},... | collective-permute-start | bytes 12296 | tf_op jit(solution)/shard_map/ppermute | solution.py:537
  62.9 4.0 %collective-permute-start.14 = (f32[8,128]{1,0:T(8,128)S(1)}, f32[8,128]{1,0:T(8,128)S(1)}, u32[]{:S(2)}, u32[]{:S(2)}) collective-permute-start(f32[8,128]{1,0:T(8,128)S(1)} %add.24), channel_id=1, source_target_pairs={{0,16},{4,20},{8,24},{12,28},{16,0},{20,4},{24,8},{28,12},{32,48},... | collective-permute-start | bytes 12296 | tf_op jit(solution)/shard_map/ppermute | solution.py:537
  66.8 2.5 %collective-permute-start.15 = (f32[8,128]{1,0:T(8,128)S(1)}, f32[8,128]{1,0:T(8,128)S(1)}, u32[]{:S(2)}, u32[]{:S(2)}) collective-permute-start(f32[8,128]{1,0:T(8,128)S(1)} %add.25), channel_id=1, source_target_pairs={{0,32},{4,36},{8,40},{12,44},{16,48},{20,52},{24,56},{28,60},{32,0... | collective-permute-start | bytes 12296 | tf_op jit(solution)/shard_map/ppermute | solution.py:537
  69.3 4.0 %collective-permute-start.16 = (f32[8,128]{1,0:T(8,128)S(1)}, f32[8,128]{1,0:T(8,128)S(1)}, u32[]{:S(2)}, u32[]{:S(2)}) collective-permute-start(f32[8,128]{1,0:T(8,128)S(1)} %add.26), channel_id=1, source_target_pairs={{0,64},{4,68},{8,72},{12,76},{16,80},{20,84},{24,88},{28,92},{32,9... | collective-permute-start | bytes 12296 | tf_op jit(solution)/shard_map/ppermute | solution.py:537
  73.3 2.5 %collective-permute-start.17 = (f32[8,128]{1,0:T(8,128)S(1)}, f32[8,128]{1,0:T(8,128)S(1)}, u32[]{:S(2)}, u32[]{:S(2)}) collective-permute-start(f32[8,128]{1,0:T(8,128)S(1)} %add.27), channel_id=1, source_target_pairs={{0,1},{1,0},{2,3},{3,2},{4,5},{5,4},{6,7},{7,6},{8,9},{9,8},{10,11... | collective-permute-start | bytes 12296 | tf_op jit(solution)/shard_map/ppermute | solution.py:537
  75.7 6.0 %collective-permute-start.18 = (f32[8,128]{1,0:T(8,128)S(1)}, f32[8,128]{1,0:T(8,128)S(1)}, u32[]{:S(2)}, u32[]{:S(2)}) collective-permute-start(f32[8,128]{1,0:T(8,128)S(1)} %add.28), channel_id=1, source_target_pairs={{0,2},{1,3},{2,0},{3,1},{4,6},{5,7},{6,4},{7,5},{8,10},{9,11},{10,... | collective-permute-start | bytes 12296 | tf_op jit(solution)/shard_map/ppermute | solution.py:537
  79.0 7.8 %collective-permute-start.10 = (f32[5,8,256]{2,1,0:T(8,128)S(1)}, f32[5,8,256]{2,1,0:T(8,128)S(1)}, u32[]{:S(2)}, u32[]{:S(2)}) collective-permute-start(f32[5,8,256]{2,1,0:T(8,128)S(1)} %get-tuple-element.49), channel_id=1, source_target_pairs={{0,1},{1,2},{2,3},{3,0},{4,5},{5,6},{6,7},{7,4},{8,9},{9,10},{10,1... | collective-permute-start | bytes 122888 | tf_op jit(solution)/shard_map/ppermute | solution.py:520
  79.7 7.1 %collective-permute-start.11 = (f32[5,8,256]{2,1,0:T(8,128)S(1)}, f32[5,8,256]{2,1,0:T(8,128)S(1)}, u32[]{:S(2)}, u32[]{:S(2)}) collective-permute-start(f32[5,8,256]{2,1,0:T(8,128)S(1)} %get-tuple-element.50), channel_id=1, source_target_pairs={{0,3},{1,0},{2,1},{3,2},{4,7},{5,4},{6,5},{7,6},{8,11},{9,8},{10,9... | collective-permute-start | bytes 122888 | tf_op jit(solution)/shard_map/ppermute | solution.py:520
  104.1 23.5 %all-to-all-start = ((f32[128,1,128]{2,1,0:T(1,128)}), f32[128,1,128]{2,1,0:T(1,128)S(1)}, u32[]{:S(2)}, u32[]{:S(2)}) async-start(f32[128,1,128]{2,1,0:T(1,128)} %bitcast.1), calls=%async_computation | async-start | bytes 131072 | tf_op jit(solution)/shard_map/all_to_all | solution.py:561
  (12 other events, 127.3 us)
where the time goes:
time: 136 us; the launch traced here: 135 us
  Pallas kernels  60.3 us (44%)
  starting transfers between devices  46.7 us (34%)
  waiting for transfers between devices  17.9 us (13%)
  local copies, waits for them, and re-layouts  9.54 us (7%)
    pallas_call x9, Pallas kernels, call(): pl.pallas_call(kernel, out_shape=out_shape, scratch_shapes=list(scratch),...  60.3 us
    ppermute x12, starting transfers between devices, shifted(): return lax.ppermute(block, axis, route)  26.3 us
    all_to_all x1, starting transfers between devices, local(): parts = lax.all_to_all(cross, ('gx', 'gy'), 0, 0, tiled=True)  13.9 us
    ppermute x7, waiting for transfers between devices, summed(): block = block + lax.ppermute(block, axis, route)  13.5 us
    unnamed x32, local copies, waits for them, and re-layouts  9.54 us
    ppermute x7, starting transfers between devices, summed(): block = block + lax.ppermute(block, axis, route)  6.47 us
    ppermute x12, waiting for transfers between devices, shifted(): return lax.ppermute(block, axis, route)  2.8 us
  transfers between devices with their start and end apart: 20, of which 9 were waited for; matrix products, arithmetic and copies ran while one was open for 0% of the time, Pallas kernels for 11%

commit v1 on v0

v1 whole, which is shorter than its diff:
```python
import functools

import jax
import jax.numpy as jnp
import ml_dtypes
import numpy as np
from jax import lax
from jax.experimental import pallas as pl
from jax.experimental.pallas import tpu as pltpu
from jax.sharding import PartitionSpec as P

NZ = 64
LANES = 128
STEP_TIME = 0.03
FIRST = (0.8, -0.2, 4.0 / 105.0, -1.0 / 280.0)
SECOND = (8.0 / 5.0, -0.2, 8.0 / 315.0, -1.0 / 560.0)
CENTRAL = -205.0 / 72.0
UNROLL = (16, 16, 35, 16, 2)
VMEM_LIMIT = 48 * 1024 * 1024
WHOLE = pl.BlockSpec(memory_space=pltpu.VMEM)


def lanes_at(index):
    return pl.ds(pl.multiple_of(index * LANES, LANES), LANES)


def loop(count, body, unroll=1):
    def group(i, carry):
        for n in range(unroll):
            body(i * unroll + n)
        return carry

    lax.fori_loop(0, count // unroll, group, 0)
    for n in range(count - count % unroll, count):
        body(n)


def row_ids():
    return lax.broadcasted_iota(jnp.int32, (8, LANES), 0)


def lane_ids():
    return lax.broadcasted_iota(jnp.int32, (8, LANES), 1)


def primitives(rho, mx, my, mz, energy):
    inv = 1.0 / rho
    u, v, w = mx * inv, my * inv, mz * inv
    p = 0.4 * (energy - 0.5 * (mx * u + my * v + mz * w))
    return u, v, w, p, p * inv


def pack_sends(state, to_below, to_above, first_y, last_y):
    length = state[0].shape[-1]
    half = length // (2 * LANES)
    low = row_ids() < 4

    def body(j):
        for f in range(5):
            here = state[f][:, lanes_at(j)]
            other = pltpu.roll(state[f][:, lanes_at(j + half)], 4, 0)
            to_below[f, :, lanes_at(j)] = jnp.where(low, here, other)
            to_above[f, :, lanes_at(j)] = jnp.where(low, other, here)

    loop(half, body, UNROLL[0])
    width = 4 * NZ
    for f in range(5):
        first_y[f] = state[f][:, :width]
        last_y[f] = state[f][:, length - width :]


def state_views(rho, mom, energy):
    return [rho, mom.at[0], mom.at[1], mom.at[2], energy]


def pack_kernel(rho, mom, energy, to_below, to_above, first_y, last_y):
    pack_sends(state_views(rho, mom, energy), to_below, to_above, first_y, last_y)


def depth_weights():
    position = np.arange(LANES)
    same = position[:, None] // NZ == position[None, :] // NZ
    result = []
    for sign, coefficients in ((-1.0, FIRST), (1.0, SECOND)):
        full = np.zeros((LANES, LANES), np.float32)
        for k in range(1, 5):
            ahead = (position[None, :] + k - position[:, None]) % NZ == 0
            behind = (position[None, :] - k - position[:, None]) % NZ == 0
            full += coefficients[k - 1] * (same & ahead)
            full += sign * coefficients[k - 1] * (same & behind)
        hi = full.astype(ml_dtypes.bfloat16)
        lo = (full - hi.astype(np.float32)).astype(ml_dtypes.bfloat16)
        result.append(np.block([[hi, lo], [hi, np.zeros_like(lo)]]))
    return jnp.asarray(np.stack(result))


def stage_kernel(stage, refs):
    if stage == 0:
        rho, mom, energy, above, below, before, after, along_z = refs[:8]
        base = None
        rest = refs[8:]
    else:
        rho, mom, energy, rho0, mom0, energy0 = refs[:6]
        above, below, before, after, along_z = refs[6:11]
        base = state_views(rho0, mom0, energy0)
        rest = refs[11:]
    if stage < 2:
        rho_o, mom_o, energy_o, to_below, to_above, first_y, last_y = rest[:7]
        ys, yh, hx, zs, zd = rest[7:]
    else:
        rho_o, mom_o, energy_o, newest = rest[:4]
        ys, yh, hx, zs, zd = rest[4:]
    state = state_views(rho, mom, energy)
    outs = state_views(rho_o, mom_o, energy_o)
    length = rho.shape[-1]
    blocks = length // LANES
    half = blocks // 2
    row, lane = row_ids(), lane_ids()
    low = row < 4

    def fill(fields, at):
        r, mx, my, mz, e = fields
        u, v, w, p, t = primitives(r, mx, my, mz, e)
        for f, value in enumerate(
            (my, mx * v, my * v + p, mz * v, (e + p) * v, u, v, w, t, p)
        ):
            ys[f, :, at] = value
        return (mz, mx * w, my * w, mz * w + p, (e + p) * w, u, v, w, t)

    def fill_own(j):
        both = pl.ds(pl.multiple_of(j * 2 * LANES, 2 * LANES), 2 * LANES)
        at = pl.ds(pl.multiple_of(j * 2 * LANES + 2 * LANES, 2 * LANES), 2 * LANES)
        place = pl.ds(pl.multiple_of(j * 16, 16), 16)
        for f, value in enumerate(fill([s[:, both] for s in state], at)):
            tall = jnp.concatenate([value[:, :LANES], value[:, LANES:]], 0)
            hi = tall.astype(jnp.bfloat16)
            zs[f, place, :LANES] = hi
            zs[f, place, LANES:] = (tall - hi.astype(jnp.float32)).astype(jnp.bfloat16)

    loop(blocks // 2, fill_own, UNROLL[1])
    for f in range(9):
        wide = jnp.dot(
            zs[f], along_z[0 if f < 5 else 1], preferred_element_type=jnp.float32
        )
        zd[f] = wide[:, :LANES] + wide[:, LANES:]
    edge = 2 * LANES
    fill([before[f] for f in range(5)], slice(0, edge))
    fill([after[f] for f in range(5)], slice(length + edge, length + 2 * edge))

    def shift_half(j):
        for f in range(9):
            here, following = ys[f, :, lanes_at(j)], ys[f, :, lanes_at(j + 1)]
            yh[f, :, lanes_at(j)] = pltpu.roll(
                jnp.where(lane < NZ, following, here), NZ, 1
            )

    loop(blocks + 3, shift_half, UNROLL[2])

    def unpack(j):
        for f in range(5):
            a, b = above[f, :, lanes_at(j)], below[f, :, lanes_at(j)]
            hx[f, :, lanes_at(j)] = jnp.where(low, a, b)
            hx[f, :, lanes_at(j + half)] = pltpu.roll(jnp.where(low, b, a), 4, 0)

    loop(half, unpack, UNROLL[3])

    def main(j):
        at = lanes_at(j)
        own = [s[:, at] for s in state]
        r, mx, my, mz, e = own
        u, v, w, t, p = [ys[5 + f, :, lanes_at(j + 2)] for f in range(5)]
        energy_p = e + p
        hr, hmx, hmy, hmz, he = [hx[f, :, at] for f in range(5)]
        hu, hv, hw, hp, ht = primitives(hr, hmx, hmy, hmz, he)
        fx = (mx, mx * u + p, my * u, mz * u, energy_p * u, u, v, w, t)
        hfx = (hmx, hmx * hu + hp, hmy * hu, hmz * hu, (he + hp) * hu, hu, hv, hw, ht)
        here = pl.ds(pl.multiple_of(j * 8, 8), 8)
        result = []
        for f in range(9):
            total = zd[f, here, :]
            if f >= 5:
                total = total + (3.0 * CENTRAL) * fx[f]
            for k in range(1, 5):
                pairs = [
                    (
                        pltpu.roll(jnp.where(row < k, hfx[f], fx[f]), 8 - k, 0),
                        pltpu.roll(jnp.where(row >= 8 - k, hfx[f], fx[f]), k, 0),
                    ),
                ]
                if k % 2:
                    up, down = (k - 1) // 2, -(k + 1) // 2
                    pairs.append(
                        (yh[f, :, lanes_at(j + 2 + up)], yh[f, :, lanes_at(j + 2 + down)])
                    )
                else:
                    pairs.append(
                        (
                            ys[f, :, lanes_at(j + 2 + k // 2)],
                            ys[f, :, lanes_at(j + 2 - k // 2)],
                        )
                    )
                if f < 5:
                    s = sum(a - b for a, b in pairs)
                    term = FIRST[k - 1] * s
                else:
                    s = sum(a + b for a, b in pairs)
                    term = SECOND[k - 1] * s
                total = total + term
            result.append(total)
        visc = 0.08 * t
        lap = result[5:]
        work = visc * (u * lap[0] + v * lap[1] + w * lap[2] + 4.9 * lap[3])
        rate = [
            -result[0],
            visc * lap[0] - result[1],
            visc * lap[1] - result[2],
            visc * lap[2] - result[3],
            work - result[4],
        ]
        final = []
        for f in range(5):
            step = own[f] + STEP_TIME * rate[f]
            if stage == 1:
                step = 0.75 * base[f][:, at] + 0.25 * step
            elif stage == 2:
                step = base[f][:, at] * (1.0 / 3.0) + (2.0 / 3.0) * step
            outs[f][:, at] = step
            final.append(step)
        if stage == 2:
            inv = 1.0 / final[0]
            for c in range(3):
                newest[c, :, at] = final[1 + c] * inv

    loop(blocks, main, UNROLL[4])
    if stage < 2:
        pack_sends(outs, to_below, to_above, first_y, last_y)


def f32(*shape):
    return jax.ShapeDtypeStruct(shape, jnp.float32)


def call(kernel, out_shape, args, scratch=(), flops=0, nbytes=0, **kw):
    return pl.pallas_call(
        kernel,
        out_shape=out_shape,
        scratch_shapes=list(scratch),
        compiler_params=pltpu.CompilerParams(vmem_limit_bytes=VMEM_LIMIT),
        cost_estimate=pl.CostEstimate(
            flops=flops, bytes_accessed=nbytes, transcendentals=0
        ),
        **kw,
    )(*args)


def state_shapes(rows, length):
    return (f32(rows, length), f32(3, rows, length), f32(rows, length))


def send_shapes(rows, length):
    packed = f32(5, rows, length // 2)
    edge = f32(5, rows, 4 * NZ)
    return (packed, packed, edge, edge)


def pack(state):
    rows, length = state[0].shape
    shapes = send_shapes(rows, length)
    return call(
        pack_kernel,
        shapes,
        state,
        in_specs=[WHOLE] * 3,
        out_specs=[WHOLE] * 4,
        nbytes=10**6,
    )


def stage_call(stage, state, base, halo):
    rows, length = state[0].shape
    out = state_shapes(rows, length)
    out += send_shapes(rows, length) if stage < 2 else (f32(3, rows, length),)
    args = tuple(state) + (tuple(base) if stage else ()) + tuple(halo) + (depth_weights(),)
    scratch = [
        pltpu.VMEM((10, rows, length + 8 * NZ), jnp.float32),
        pltpu.VMEM((9, rows, length + 8 * NZ), jnp.float32),
        pltpu.VMEM((5, rows, length), jnp.float32),
        pltpu.VMEM((9, length // 16, 2 * LANES), jnp.bfloat16),
        pltpu.VMEM((9, length // 16, LANES), jnp.float32),
    ]
    return call(
        lambda *refs: stage_kernel(stage, refs),
        out,
        args,
        scratch,
        in_specs=[WHOLE] * len(args),
        out_specs=[WHOLE] * len(out),
        flops=32768 * 700,
        nbytes=3 * 10**6,
    )


def merged_rows(basis, snaps, c, at):
    first = basis[:, c, :, at].astype(jnp.float32)
    second = snaps[:, c, :, at].astype(jnp.float32)
    length = first.shape[-1]
    rows = jnp.concatenate([first, second, jnp.zeros((1, 8, length), jnp.float32)], 0)
    return rows.reshape(256, length).astype(jnp.bfloat16)


def group_matrix(shape, group_dim, dtype):
    g = lax.broadcasted_iota(jnp.int32, shape, group_dim)
    o = lax.broadcasted_iota(jnp.int32, shape, 1 - group_dim)
    return (g // 8 == o).astype(dtype)


def same_layer():
    r = lax.broadcasted_iota(jnp.int32, (256, 256), 0)
    c = lax.broadcasted_iota(jnp.int32, (256, 256), 1)
    return r % 8 == c % 8


def pack_square(small):
    return jnp.concatenate([small[8 * g : 8 * g + 8] for g in range(4)], 1)


def gram_kernel(basis, snaps, gram, total):
    width = 1024
    total[...] = jnp.zeros_like(total)

    def add(i):
        at = pl.ds(pl.multiple_of(i * width, width), width)
        for c in range(3):
            rows = merged_rows(basis, snaps, c, at)
            total[...] += lax.dot_general(
                rows, rows, (((1,), (1,)), ((), ())), preferred_element_type=jnp.float32
            )

    loop(basis.shape[-1] // width, add)
    kept = jnp.where(same_layer(), total[...], 0.0)
    left = group_matrix((32, 256), 1, jnp.float32)
    right = group_matrix((256, 32), 0, jnp.float32)
    small = jnp.dot(left, kept, precision=lax.Precision.HIGHEST)
    gram[...] = pack_square(jnp.dot(small, right, precision=lax.Precision.HIGHEST))


def gram_call(basis, snaps):
    length = basis.shape[-1]
    return call(
        gram_kernel,
        f32(8, LANES),
        (basis, snaps),
        [pltpu.VMEM((256, 256), jnp.float32)],
        in_specs=[WHOLE] * 2,
        out_specs=WHOLE,
        flops=2 * 256 * 256 * 3 * length,
        nbytes=31 * 3 * 8 * length * 2,
    )


def cross_kernel(basis, snaps, newest, gram, parts, total):
    total[...] = jnp.zeros_like(total)

    def add(i):
        at = lanes_at(i)
        new = [newest[c, :, at] for c in range(3)]
        for k in range(31):
            ref, n = (basis, k) if k < 16 else (snaps, k - 16)
            total[k] += sum(ref[n, c, :, at].astype(jnp.float32) * new[c] for c in range(3))
        total[31] += sum(n * n for n in new)

    loop(basis.shape[-1] // LANES, add, 4)
    sums = jnp.sum(total[...], axis=1)
    line = lax.dot_general(
        jnp.ones((8, LANES), jnp.float32),
        sums,
        (((1,), (1,)), ((), ())),
        precision=lax.Precision.HIGHEST,
    )
    line = jnp.concatenate([jnp.zeros((8, 96), jnp.float32), line], 1)
    last = (row_ids() == 7) & (lane_ids() >= 96)
    parts[...] = jnp.broadcast_to(jnp.where(last, line, gram[...])[None], parts.shape)


def cross_call(basis, snaps, newest, gram, copies):
    length = basis.shape[-1]
    return call(
        cross_kernel,
        f32(copies, 8, LANES),
        (basis, snaps, newest, gram),
        [pltpu.VMEM((32, 8, LANES), jnp.float32)],
        in_specs=[WHOLE] * 4,
        out_specs=WHOLE,
        flops=31 * 6 * 8 * length,
        nbytes=31 * 3 * 8 * length * 2,
    )


def weights_of(weight, parts, scale, factor, high, low, diagonal):
    row = lax.broadcasted_iota(jnp.int32, (32, 32), 0)
    col = lax.broadcasted_iota(jnp.int32, (32, 32), 1)
    s = jnp.broadcast_to(scale[...], (32, 32))
    s_col = jnp.sum(jnp.where(row == col, s, 0.0), axis=1, keepdims=True)
    packed = jnp.sum(parts[...], axis=0)
    g = jnp.concatenate([packed[:, 32 * i : 32 * i + 32] for i in range(4)], 0)
    line = jnp.broadcast_to(g[31:32], (32, 32))
    line = jnp.sum(jnp.where(row == col, line, 0.0), axis=1, keepdims=True)
    g = jnp.where(col == 31, line, g)
    g = g * (weight * s) * s_col
    eye = (row == col).astype(jnp.float32)
    work = jnp.concatenate([g, eye, jnp.zeros((32, 64), jnp.float32)], 1)
    rows128 = lax.broadcasted_iota(jnp.int32, (32, LANES), 0)
    done = jnp.zeros((32, LANES), jnp.float32)
    for j in range(32):
        column = jnp.broadcast_to(work[:, j : j + 1], (32, LANES))
        pivot_row = jnp.broadcast_to(work[j : j + 1], (32, LANES))
        pivot = jnp.broadcast_to(column[j : j + 1], (32, LANES))
        done = jnp.where(rows128 == j, pivot_row / jnp.sqrt(pivot), done)
        work = work - column * (pivot_row / pivot)
    factor[...] = jnp.where(col >= row, done[:, :32], 0.0)
    l = jnp.where(col <= row, done[:, 32:64], 0.0)
    diagonal[...] = jnp.broadcast_to(l[31:32, 31:32], diagonal.shape)
    scaled = jnp.where(col < 31, l * s, 0.0)
    hi = scaled.astype(jnp.bfloat16)
    lo = (scaled - hi.astype(jnp.float32)).astype(jnp.bfloat16)
    left = group_matrix((256, 32), 0, jnp.bfloat16)
    right = group_matrix((32, 256), 1, jnp.bfloat16)
    keep = same_layer()
    for part, out in ((hi, high), (lo, low)):
        wide = jnp.dot(left, part, preferred_element_type=jnp.float32)
        wide = jnp.dot(
            wide.astype(jnp.bfloat16), right, preferred_element_type=jnp.float32
        )
        out[...] = jnp.where(keep, wide, 0.0).astype(jnp.bfloat16)


def modes_kernel(
    weight, parts, scale, basis, snaps, newest, modes, factor, high, low, diagonal
):
    step = pl.program_id(0)

    @pl.when(step == 0)
    def _():
        weights_of(weight, parts, scale, factor, high, low, diagonal)

    width = modes.shape[-1]
    at = pl.ds(pl.multiple_of(step * width, width), width)
    for c in range(3):
        rows = merged_rows(basis, snaps, c, at)
        out = jnp.dot(high[...], rows, preferred_element_type=jnp.float32)
        out = out + jnp.dot(low[...], rows, preferred_element_type=jnp.float32)
        out = out.reshape(32, 8, width)
        modes[:31, c] = out[:31].astype(jnp.bfloat16)
        own = diagonal[:, :1] * newest[c, :, at]
        modes[31, c] = (out[31] + own).astype(jnp.bfloat16)


def modes_call(parts, scale, basis, snaps, newest, weight, width=1024):
    length = basis.shape[-1]
    return call(
        functools.partial(modes_kernel, weight),
        (jax.ShapeDtypeStruct((32, 3, 8, length), jnp.bfloat16), f32(32, 32)),
        (parts, scale, basis, snaps, newest),
        [
            pltpu.VMEM((256, 256), jnp.bfloat16),
            pltpu.VMEM((256, 256), jnp.bfloat16),
            pltpu.VMEM((8, LANES), jnp.float32),
        ],
        grid=(length // width,),
        in_specs=[WHOLE] * 5,
        out_specs=[
            pl.BlockSpec((32, 3, 8, width), lambda i: (0, 0, 0, i)),
            pl.BlockSpec((32, 32), lambda i: (0, 0)),
        ],
        flops=4 * 256 * 256 * 3 * length,
        nbytes=63 * 3 * 8 * length * 2,
    )


def shifted(block, axis, distance):
    count = lax.axis_size(axis)
    route = [(i, (i + distance) % count) for i in range(count)]
    return lax.ppermute(block, axis, route)


def exchange(sends):
    to_below, to_above, first_y, last_y = sends
    above = shifted(to_below, "gx", -1)
    below = shifted(to_above, "gx", 1)
    before = shifted(last_y, "gy", 1)
    after = shifted(first_y, "gy", -1)
    return (above, below, before, after)


def local(density, momentum, energy, basis, scales, snapshots):
    rows, length = density.shape
    devices = lax.axis_size("gx") * lax.axis_size("gy")
    weight = 1.0 / (3 * rows * length * devices)
    fields = (density, momentum, energy)
    scale = jnp.concatenate([scales, jnp.ones((16,), jnp.float32)])[None]

    halo = exchange(pack(fields))
    gram = gram_call(basis, snapshots)
    first = stage_call(0, fields, None, halo)
    second = stage_call(1, first[:3], fields, exchange(first[3:]))
    final = stage_call(2, second[:3], fields, exchange(second[3:]))
    newest = final[3]
    parts = cross_call(basis, snapshots, newest, gram, devices)
    parts = lax.all_to_all(parts, ("gx", "gy"), 0, 0, tiled=True)
    modes, factor = modes_call(parts, scale, basis, snapshots, newest, weight)
    return (final[0], final[1], final[2], modes, factor)


def solution(mesh):
    field, vector = P("gx", "gy"), P(None, "gx", "gy")
    columns = P(None, None, "gx", "gy")
    return jax.shard_map(
        local,
        mesh=mesh,
        in_specs=(field, vector, field, columns, P(), columns),
        out_specs=(field, vector, field, columns, P()),
        check_vma=False,
    )
```

time: 136 us -> 89.4 us (0.66)
  Pallas kernels: 60.3 us -> 29 us
  starting transfers between devices: 46.7 us -> 34.2 us
  waiting for transfers between devices: 17.9 us -> 16.5 us
    pallas_call x9 -> x7, Pallas kernels: 60.3 us -> 29 us  [call(): pl.pallas_call(kernel, out_shape=out_shape, scratch_shapes=list(scratch),...]
    ppermute x7 -> x0, waiting for transfers between devices: 13.5 us -> none  [summed(): block = block + lax.ppermute(block, axis, route)]
    all_to_all x1, waiting for transfers between devices: 1.62 us -> 13.7 us  [local(): parts = lax.all_to_all(parts, ('gx', 'gy'), 0, 0, tiled=True)]
    all_to_all x1, starting transfers between devices: 13.9 us -> 7.19 us  [local(): parts = lax.all_to_all(parts, ('gx', 'gy'), 0, 0, tiled=True)]
    ppermute x7 -> x0, starting transfers between devices: 6.47 us -> none  [summed(): block = block + lax.ppermute(block, axis, route)]
  transfers between devices with their start and end apart: 20 -> 13, of which waited for: 9 -> 3; matrix products, arithmetic and copies ran while one was open for 0% -> 0% of each run, Pallas kernels for 11% -> 3%
where the time goes in v1:
time: 89.4 us; the launch traced here: 89 us
  starting transfers between devices  34.2 us (38%)
  Pallas kernels  29 us (32%)
  waiting for transfers between devices  16.5 us (18%)
  local copies, waits for them, and re-layouts  8.44 us (9%)
    pallas_call x7, Pallas kernels, call(): pl.pallas_call(kernel, out_shape=out_shape, scratch_shapes=list(scratch),...  29 us
    ppermute x12, starting transfers between devices, shifted(): return lax.ppermute(block, axis, route)  27 us
    all_to_all x1, waiting for transfers between devices, local(): parts = lax.all_to_all(parts, ('gx', 'gy'), 0, 0, tiled=True)  13.7 us
    unnamed x32, local copies, waits for them, and re-layouts  8.44 us
    all_to_all x1, starting transfers between devices, local(): parts = lax.all_to_all(parts, ('gx', 'gy'), 0, 0, tiled=True)  7.19 us
    ppermute x12, waiting for transfers between devices, shifted(): return lax.ppermute(block, axis, route)  2.81 us
  transfers between devices with their start and end apart: 13, of which 3 were waited for; matrix products, arithmetic and copies ran while one was open for 0% of the time, Pallas kernels for 3%

profile of v1, /device:TPU:1, one launch (start us, length us, event | category | flops | bytes accessed | tf_op | source)
XLA Modules:
  0.0 89.0 jit_solution(12984277698188585666)
XLA Ops:
  0.7 1.1 %copy-done.4 = f32[3,8,4096]{2,1,0:T(8,128)S(1)} copy-done((f32[3,8,4096]{2,1,0:T(8,128)S(1)}, f32[3,8,4096]{2,1,0:T(8,128)}, u32[]{:S(2)}) %copy-start.4) | copy-done | bytes 393240
  3.7 1.5 %collective-permute-start = (f32[5,8,2048]{2,1,0:T(8,128)S(1)}, f32[5,8,2048]{2,1,0:T(8,128)S(1)}, u32[]{:S(2)}, u32[]{:S(2)}) collective-permute-start(f32[5,8,2048]{2,1,0:T(8,128)S(1)} %get-tuple-element.29), channel_id=1, source_target_pairs={{0,124},{4,0},{8,4},{12,8},{16,12},{20,16},{24,20},{28,24},{32,28}... | collective-permute-start | bytes 983048 | tf_op jit(solution)/shard_map/ppermute | solution.py:483
  5.2 1.3 %collective-permute-start.1 = (f32[5,8,2048]{2,1,0:T(8,128)S(1)}, f32[5,8,2048]{2,1,0:T(8,128)S(1)}, u32[]{:S(2)}, u32[]{:S(2)}) collective-permute-start(f32[5,8,2048]{2,1,0:T(8,128)S(1)} %get-tuple-element.30), channel_id=1, source_target_pairs={{0,4},{4,8},{8,12},{12,16},{16,20},{20,24},{24,28},{28,32},{32,36}... | collective-permute-start | bytes 983048 | tf_op jit(solution)/shard_map/ppermute | solution.py:483
  6.4 1.6 %collective-permute-start.2 = (f32[5,8,256]{2,1,0:T(8,128)S(1)}, f32[5,8,256]{2,1,0:T(8,128)S(1)}, u32[]{:S(2)}, u32[]{:S(2)}) collective-permute-start(f32[5,8,256]{2,1,0:T(8,128)S(1)} %get-tuple-element.31), channel_id=1, source_target_pairs={{0,1},{1,2},{2,3},{3,0},{4,5},{5,6},{6,7},{7,4},{8,9},{9,10},{10,1... | collective-permute-start | bytes 122888 | tf_op jit(solution)/shard_map/ppermute | solution.py:483
  8.1 2.1 %collective-permute-start.3 = (f32[5,8,256]{2,1,0:T(8,128)S(1)}, f32[5,8,256]{2,1,0:T(8,128)S(1)}, u32[]{:S(2)}, u32[]{:S(2)}) collective-permute-start(f32[5,8,256]{2,1,0:T(8,128)S(1)} %get-tuple-element.32), channel_id=1, source_target_pairs={{0,3},{1,0},{2,1},{3,2},{4,7},{5,4},{6,5},{7,6},{8,11},{9,8},{10,9... | collective-permute-start | bytes 122888 | tf_op jit(solution)/shard_map/ppermute | solution.py:483
  10.2 1.4 %collective-permute-done.2.refs_5_ = f32[5,8,256]{2,1,0:T(8,128)S(1)} collective-permute-done((f32[5,8,256]{2,1,0:T(8,128)S(1)}, f32[5,8,256]{2,1,0:T(8,128)S(1)}, u32[]{:S(2)}, u32[]{:S(2)}) %collective-permute-start.2) | collective-permute-done | bytes 40992 | tf_op jit(solution)/shard_map/ppermute | solution.py:483
  11.6 0.9 %copy-done.6 = bf16[2,256,256]{2,1,0:T(8,128)(2,1)S(1)} copy-done((bf16[2,256,256]{2,1,0:T(8,128)(2,1)S(1)}, bf16[2,256,256]{2,1,0:T(8,128)(2,1)}, u32[]{:S(2)}) %copy-start.6) | copy-done | bytes 262168
  12.5 2.7 %shard_map.129 = (f32[8,4096]{1,0:T(8,128)S(1)}, f32[3,8,4096]{2,1,0:T(8,128)S(1)}, f32[8,4096]{1,0:T(8,128)S(1)}, f32[5,8,2048]{2,1,0:T(8,128)S(1)}, f32[5,8,20...) custom-call(f32[8,4096]{1,0:T(8,128)S(1)} %copy-done.9, f32[3,8,4096]{2,1,0:T(8,128)S(1)} %copy-done.4, ...), custom_call_target="tpu_custom_call" | custom-call | flops 22937600 | bytes 3000000 | tf_op jit(solution)/shard_map/pallas_call | solution.py:244
  15.3 8.2 %collective-permute-start.4 = (f32[5,8,2048]{2,1,0:T(8,128)S(1)}, f32[5,8,2048]{2,1,0:T(8,128)S(1)}, u32[]{:S(2)}, u32[]{:S(2)}) collective-permute-start(f32[5,8,2048]{2,1,0:T(8,128)S(1)} %get-tuple-element.36), channel_id=1, source_target_pairs={{0,124},{4,0},{8,4},{12,8},{16,12},{20,16},{24,20},{28,24},{32,28}... | collective-permute-start | bytes 983048 | tf_op jit(solution)/shard_map/ppermute | solution.py:483
  23.5 1.6 %collective-permute-start.6 = (f32[5,8,256]{2,1,0:T(8,128)S(1)}, f32[5,8,256]{2,1,0:T(8,128)S(1)}, u32[]{:S(2)}, u32[]{:S(2)}) collective-permute-start(f32[5,8,256]{2,1,0:T(8,128)S(1)} %get-tuple-element.38), channel_id=1, source_target_pairs={{0,1},{1,2},{2,3},{3,0},{4,5},{5,6},{6,7},{7,4},{8,9},{9,10},{10,1... | collective-permute-start | bytes 122888 | tf_op jit(solution)/shard_map/ppermute | solution.py:483
  25.1 2.1 %collective-permute-start.7 = (f32[5,8,256]{2,1,0:T(8,128)S(1)}, f32[5,8,256]{2,1,0:T(8,128)S(1)}, u32[]{:S(2)}, u32[]{:S(2)}) collective-permute-start(f32[5,8,256]{2,1,0:T(8,128)S(1)} %get-tuple-element.39), channel_id=1, source_target_pairs={{0,3},{1,0},{2,1},{3,2},{4,7},{5,4},{6,5},{7,6},{8,11},{9,8},{10,9... | collective-permute-start | bytes 122888 | tf_op jit(solution)/shard_map/ppermute | solution.py:483
  27.2 1.4 %collective-permute-done.6.refs_8_ = f32[5,8,256]{2,1,0:T(8,128)S(1)} collective-permute-done((f32[5,8,256]{2,1,0:T(8,128)S(1)}, f32[5,8,256]{2,1,0:T(8,128)S(1)}, u32[]{:S(2)}, u32[]{:S(2)}) %collective-permute-start.6) | collective-permute-done | bytes 40992 | tf_op jit(solution)/shard_map/ppermute | solution.py:483
  29.6 2.8 %shard_map.130 = (f32[8,4096]{1,0:T(8,128)S(1)}, f32[3,8,4096]{2,1,0:T(8,128)S(1)}, f32[8,4096]{1,0:T(8,128)S(1)}, f32[5,8,2048]{2,1,0:T(8,128)S(1)}, f32[5,8,20...) custom-call(f32[8,4096]{1,0:T(8,128)S(1)} %get-tuple-element.33.refs_0_, ...), custom_call_target="tpu_custom_call" | custom-call | flops 22937600 | bytes 3000000 | tf_op jit(solution)/shard_map/pallas_call | solution.py:244
  32.4 5.1 %collective-permute-start.8 = (f32[5,8,2048]{2,1,0:T(8,128)S(1)}, f32[5,8,2048]{2,1,0:T(8,128)S(1)}, u32[]{:S(2)}, u32[]{:S(2)}) collective-permute-start(f32[5,8,2048]{2,1,0:T(8,128)S(1)} %get-tuple-element.43), channel_id=1, source_target_pairs={{0,124},{4,0},{8,4},{12,8},{16,12},{20,16},{24,20},{28,24},{32,28}... | collective-permute-start | bytes 983048 | tf_op jit(solution)/shard_map/ppermute | solution.py:483
  37.6 1.3 %collective-permute-start.10 = (f32[5,8,256]{2,1,0:T(8,128)S(1)}, f32[5,8,256]{2,1,0:T(8,128)S(1)}, u32[]{:S(2)}, u32[]{:S(2)}) collective-permute-start(f32[5,8,256]{2,1,0:T(8,128)S(1)} %get-tuple-element.45), channel_id=1, source_target_pairs={{0,1},{1,2},{2,3},{3,0},{4,5},{5,6},{6,7},{7,4},{8,9},{9,10},{10,1... | collective-permute-start | bytes 122888 | tf_op jit(solution)/shard_map/ppermute | solution.py:483
  38.9 2.1 %collective-permute-start.11 = (f32[5,8,256]{2,1,0:T(8,128)S(1)}, f32[5,8,256]{2,1,0:T(8,128)S(1)}, u32[]{:S(2)}, u32[]{:S(2)}) collective-permute-start(f32[5,8,256]{2,1,0:T(8,128)S(1)} %get-tuple-element.46), channel_id=1, source_target_pairs={{0,3},{1,0},{2,1},{3,2},{4,7},{5,4},{6,5},{7,6},{8,11},{9,8},{10,9... | collective-permute-start | bytes 122888 | tf_op jit(solution)/shard_map/ppermute | solution.py:483
  41.0 1.8 %copy-done.1 = bf16[15,3,8,4096]{3,2,1,0:T(8,128)(2,1)S(1)} copy-done((bf16[15,3,8,4096]{3,2,1,0:T(8,128)(2,1)S(1)}, bf16[15,3,8,4096]{3,2,1,0:T(8,128)(2,1)}, u32[]{:S(2)}) %copy-start.1) | copy-done | bytes 2949144
  42.8 3.0 %shard_map.132.gram = f32[8,128]{1,0:T(8,128)S(1)} custom-call(bf16[16,3,8,4096]{3,2,1,0:T(8,128)(2,1)S(1)} %copy-done, bf16[15,3,8,4096]{3,2,1,0:T(8,128)(2,1)S(1)} %copy-done.1), custom_call_target="tpu_custom_call" | custom-call | flops 1610612736 | bytes 6094848 | tf_op jit(solution)/shard_map/pallas_call | solution.py:244
  46.0 3.6 %shard_map.131 = (f32[8,4096]{1,0:T(8,128)}, f32[3,8,4096]{2,1,0:T(8,128)}, f32[8,4096]{1,0:T(8,128)}, f32[3,8,4096]{2,1,0:T(8,128)S(1)}) custom-call(f32[8,4096]{1,0:T(8,128)S(1)} %get-tuple-element.40.refs_0_, f32[3,8,4096]{2,1,0:T(8,128)S(1)} %get-tuple-element.41.refs_1_, f32[8,4096]{1,0:T(8,128)S(1)} %get-tuple-element.42.refs_2_, ...), custom_call_target="tpu_custom_call" | custom-call | flops 22937600 | bytes 3000000 | tf_op jit(solution)/shard_map/pallas_call | solution.py:244
  49.6 4.8 %shard_map.133 = f32[128,8,128]{2,1,0:T(8,128)} custom-call(bf16[16,3,8,4096]{3,2,1,0:T(8,128)(2,1)} %basis.5, bf16[15,3,8,4096]{3,2,1,0:T(8,128)(2,1)S(1)} %copy-done.2, f32[3,8,4096]{2,1,0:T(8,128)S(1)} %get-tuple-element.50.newest, f32[8,128]{1,0:T(8,128)S(1)} %shard_map.132.gram), custom_call_target="tpu_custom_call" | custom-call | flops 6094848 | bytes 6094848 | tf_op jit(solution)/shard_map/pallas_call | solution.py:244
  55.1 7.2 %all-to-all-start = ((f32[128,8,128]{2,1,0:T(8,128)}), f32[128,8,128]{2,1,0:T(8,128)S(1)}, u32[]{:S(2)}, u32[]{:S(2)}) async-start(f32[128,8,128]{2,1,0:T(8,128)} %shard_map.133), calls=%async_computation | async-start | bytes 1048576 | tf_op jit(solution)/shard_map/all_to_all | solution.py:509
  62.3 13.7 %all-to-all-done.parts = f32[128,8,128]{2,1,0:T(8,128)S(1)} async-done(((f32[128,8,128]{2,1,0:T(8,128)}), f32[128,8,128]{2,1,0:T(8,128)S(1)}, u32[]{:S(2)}, u32[]{:S(2)}) %all-to-all-start) | async-done | bytes 524320 | tf_op jit(solution)/shard_map/all_to_all | solution.py:509
  76.1 1.0 %copy-done.14 = f32[3,8,4096]{2,1,0:T(8,128)S(1)} copy-done((f32[3,8,4096]{2,1,0:T(8,128)S(1)}, f32[3,8,4096]{2,1,0:T(8,128)}, u32[]{:S(2)}) %copy-start.14) | copy-done | bytes 393240
  77.1 11.9 %shard_map.134 = (bf16[32,3,8,4096]{3,2,1,0:T(8,128)(2,1)}, f32[32,32]{1,0:T(8,128)}) custom-call(f32[128,8,128]{2,1,0:T(8,128)S(1)} %all-to-all-done.parts, f32[1,32]{1,0:T(1,128)S(1)} %pad_bitcast_fusion.scale, bf16[16,3,8,4096]{3,2,1,0:T(8,128)(2,1)} %basis.5, bf16[15,3,8,4096]{3,2,1,0:T(8,128)(2,1)S(1)} %copy-done.3, f32[3,8,4096]{2,1,0:T(8,128)S(1)} %copy-done.14), custom_call_target="tpu_custom_call" | custom-call | flops 3221225472 | bytes 12386304 | tf_op jit(solution)/shard_map/pallas_call | solution.py:244
  (42 shorter events, 3.6 us)
Async XLA Ops:
  0.6 40.4 %copy-start = (bf16[16,3,8,4096]{3,2,1,0:T(8,128)(2,1)S(1)}, bf16[16,3,8,4096]{3,2,1,0:T(8,128)(2,1)}, u32[]{:S(2)}) copy-start(bf16[16,3,8,4096]{3,2,1,0:T(8,128)(2,1)} %basis.5) | copy-start | bytes 9437188
  0.6 1.1 %copy-start.4 = (f32[3,8,4096]{2,1,0:T(8,128)S(1)}, f32[3,8,4096]{2,1,0:T(8,128)}, u32[]{:S(2)}) copy-start(f32[3,8,4096]{2,1,0:T(8,128)} %refs_4_.3) | copy-start | bytes 1179652
  3.7 7.9 %collective-permute-start = (f32[5,8,2048]{2,1,0:T(8,128)S(1)}, f32[5,8,2048]{2,1,0:T(8,128)S(1)}, u32[]{:S(2)}, u32[]{:S(2)}) collective-permute-start(f32[5,8,2048]{2,1,0:T(8,128)S(1)} %get-tuple-element.29), channel_id=1, source_target_pairs={{0,124},{4,0},{8,4},{12,8},{16,12},{20,16},{24,20},{28,24},{32,28}... | collective-permute-start | bytes 983048 | tf_op jit(solution)/shard_map/ppermute | solution.py:483
  5.2 6.4 %collective-permute-start.1 = (f32[5,8,2048]{2,1,0:T(8,128)S(1)}, f32[5,8,2048]{2,1,0:T(8,128)S(1)}, u32[]{:S(2)}, u32[]{:S(2)}) collective-permute-start(f32[5,8,2048]{2,1,0:T(8,128)S(1)} %get-tuple-element.30), channel_id=1, source_target_pairs={{0,4},{4,8},{8,12},{12,16},{16,20},{20,24},{24,28},{28,32},{32,36}... | collective-permute-start | bytes 983048 | tf_op jit(solution)/shard_map/ppermute | solution.py:483
  6.4 5.1 %collective-permute-start.2 = (f32[5,8,256]{2,1,0:T(8,128)S(1)}, f32[5,8,256]{2,1,0:T(8,128)S(1)}, u32[]{:S(2)}, u32[]{:S(2)}) collective-permute-start(f32[5,8,256]{2,1,0:T(8,128)S(1)} %get-tuple-element.31), channel_id=1, source_target_pairs={{0,1},{1,2},{2,3},{3,0},{4,5},{5,6},{6,7},{7,4},{8,9},{9,10},{10,1... | collective-permute-start | bytes 122888 | tf_op jit(solution)/shard_map/ppermute | solution.py:483
  8.1 3.5 %collective-permute-start.3 = (f32[5,8,256]{2,1,0:T(8,128)S(1)}, f32[5,8,256]{2,1,0:T(8,128)S(1)}, u32[]{:S(2)}, u32[]{:S(2)}) collective-permute-start(f32[5,8,256]{2,1,0:T(8,128)S(1)} %get-tuple-element.32), channel_id=1, source_target_pairs={{0,3},{1,0},{2,1},{3,2},{4,7},{5,4},{6,5},{7,6},{8,11},{9,8},{10,9... | collective-permute-start | bytes 122888 | tf_op jit(solution)/shard_map/ppermute | solution.py:483
  15.3 13.4 %collective-permute-start.4 = (f32[5,8,2048]{2,1,0:T(8,128)S(1)}, f32[5,8,2048]{2,1,0:T(8,128)S(1)}, u32[]{:S(2)}, u32[]{:S(2)}) collective-permute-start(f32[5,8,2048]{2,1,0:T(8,128)S(1)} %get-tuple-element.36), channel_id=1, source_target_pairs={{0,124},{4,0},{8,4},{12,8},{16,12},{20,16},{24,20},{28,24},{32,28}... | collective-permute-start | bytes 983048 | tf_op jit(solution)/shard_map/ppermute | solution.py:483
  23.5 5.2 %collective-permute-start.5 = (f32[5,8,2048]{2,1,0:T(8,128)S(1)}, f32[5,8,2048]{2,1,0:T(8,128)S(1)}, u32[]{:S(2)}, u32[]{:S(2)}) collective-permute-start(f32[5,8,2048]{2,1,0:T(8,128)S(1)} %get-tuple-element.37), channel_id=1, source_target_pairs={{0,4},{4,8},{8,12},{12,16},{16,20},{20,24},{24,28},{28,32},{32,36}... | collective-permute-start | bytes 983048 | tf_op jit(solution)/shard_map/ppermute | solution.py:483
  23.5 5.1 %collective-permute-start.6 = (f32[5,8,256]{2,1,0:T(8,128)S(1)}, f32[5,8,256]{2,1,0:T(8,128)S(1)}, u32[]{:S(2)}, u32[]{:S(2)}) collective-permute-start(f32[5,8,256]{2,1,0:T(8,128)S(1)} %get-tuple-element.38), channel_id=1, source_target_pairs={{0,1},{1,2},{2,3},{3,0},{4,5},{5,6},{6,7},{7,4},{8,9},{9,10},{10,1... | collective-permute-start | bytes 122888 | tf_op jit(solution)/shard_map/ppermute | solution.py:483
  25.1 3.5 %collective-permute-start.7 = (f32[5,8,256]{2,1,0:T(8,128)S(1)}, f32[5,8,256]{2,1,0:T(8,128)S(1)}, u32[]{:S(2)}, u32[]{:S(2)}) collective-permute-start(f32[5,8,256]{2,1,0:T(8,128)S(1)} %get-tuple-element.39), channel_id=1, source_target_pairs={{0,3},{1,0},{2,1},{3,2},{4,7},{5,4},{6,5},{7,6},{8,11},{9,8},{10,9... | collective-permute-start | bytes 122888 | tf_op jit(solution)/shard_map/ppermute | solution.py:483
  29.6 16.3 %copy-start.5 = (f32[3,8,4096]{2,1,0:T(8,128)S(1)}, f32[3,8,4096]{2,1,0:T(8,128)}, u32[]{:S(2)}) copy-start(f32[3,8,4096]{2,1,0:T(8,128)} %refs_4_.3) | copy-start | bytes 1179652
  29.6 16.3 %copy-start.8 = (bf16[2,256,256]{2,1,0:T(8,128)(2,1)S(1)}, bf16[2,256,256]{2,1,0:T(8,128)(2,1)}, u32[]{:S(2)}) copy-start(bf16[2,256,256]{2,1,0:T(8,128)(2,1)} %constant.4.clone.refs_7_.refs_10_) | copy-start | bytes 786436
  29.6 16.3 %copy-start.10 = (f32[8,4096]{1,0:T(8,128)S(1)}, f32[8,4096]{1,0:T(8,128)}, u32[]{:S(2)}) copy-start(f32[8,4096]{1,0:T(8,128)} %refs_3_.3) | copy-start | bytes 393220
  29.6 16.4 %copy-start.12 = (f32[8,4096]{1,0:T(8,128)S(1)}, f32[8,4096]{1,0:T(8,128)}, u32[]{:S(2)}) copy-start(f32[8,4096]{1,0:T(8,128)} %refs_5_.3) | copy-start | bytes 393220
  32.4 13.5 %collective-permute-start.8 = (f32[5,8,2048]{2,1,0:T(8,128)S(1)}, f32[5,8,2048]{2,1,0:T(8,128)S(1)}, u32[]{:S(2)}, u32[]{:S(2)}) collective-permute-start(f32[5,8,2048]{2,1,0:T(8,128)S(1)} %get-tuple-element.43), channel_id=1, source_target_pairs={{0,124},{4,0},{8,4},{12,8},{16,12},{20,16},{24,20},{28,24},{32,28}... | collective-permute-start | bytes 983048 | tf_op jit(solution)/shard_map/ppermute | solution.py:483
  37.6 8.3 %collective-permute-start.9 = (f32[5,8,2048]{2,1,0:T(8,128)S(1)}, f32[5,8,2048]{2,1,0:T(8,128)S(1)}, u32[]{:S(2)}, u32[]{:S(2)}) collective-permute-start(f32[5,8,2048]{2,1,0:T(8,128)S(1)} %get-tuple-element.44), channel_id=1, source_target_pairs={{0,4},{4,8},{8,12},{12,16},{16,20},{20,24},{24,28},{28,32},{32,36}... | collective-permute-start | bytes 983048 | tf_op jit(solution)/shard_map/ppermute | solution.py:483
  37.6 8.3 %collective-permute-start.10 = (f32[5,8,256]{2,1,0:T(8,128)S(1)}, f32[5,8,256]{2,1,0:T(8,128)S(1)}, u32[]{:S(2)}, u32[]{:S(2)}) collective-permute-start(f32[5,8,256]{2,1,0:T(8,128)S(1)} %get-tuple-element.45), channel_id=1, source_target_pairs={{0,1},{1,2},{2,3},{3,0},{4,5},{5,6},{6,7},{7,4},{8,9},{9,10},{10,1... | collective-permute-start | bytes 122888 | tf_op jit(solution)/shard_map/ppermute | solution.py:483
  38.9 7.0 %collective-permute-start.11 = (f32[5,8,256]{2,1,0:T(8,128)S(1)}, f32[5,8,256]{2,1,0:T(8,128)S(1)}, u32[]{:S(2)}, u32[]{:S(2)}) collective-permute-start(f32[5,8,256]{2,1,0:T(8,128)S(1)} %get-tuple-element.46), channel_id=1, source_target_pairs={{0,3},{1,0},{2,1},{3,2},{4,7},{5,4},{6,5},{7,6},{8,11},{9,8},{10,9... | collective-permute-start | bytes 122888 | tf_op jit(solution)/shard_map/ppermute | solution.py:483
  41.0 1.8 %copy-start.1 = (bf16[15,3,8,4096]{3,2,1,0:T(8,128)(2,1)S(1)}, bf16[15,3,8,4096]{3,2,1,0:T(8,128)(2,1)}, u32[]{:S(2)}) copy-start(bf16[15,3,8,4096]{3,2,1,0:T(8,128)(2,1)} %snaps.5) | copy-start | bytes 8847364
  42.8 6.7 %copy-start.2 = (bf16[15,3,8,4096]{3,2,1,0:T(8,128)(2,1)S(1)}, bf16[15,3,8,4096]{3,2,1,0:T(8,128)(2,1)}, u32[]{:S(2)}) copy-start(bf16[15,3,8,4096]{3,2,1,0:T(8,128)(2,1)} %snaps.5) | copy-start | bytes 8847364
  49.6 12.8 %copy-start.15 = (f32[16]{0:T(128)S(1)}, f32[16]{0:T(128)}, u32[]{:S(2)}) copy-start(f32[16]{0:T(128)} %param.13) | copy-start | bytes 196
  49.6 26.5 %copy-start.3 = (bf16[15,3,8,4096]{3,2,1,0:T(8,128)(2,1)S(1)}, bf16[15,3,8,4096]{3,2,1,0:T(8,128)(2,1)}, u32[]{:S(2)}) copy-start(bf16[15,3,8,4096]{3,2,1,0:T(8,128)(2,1)} %snaps.5) | copy-start | bytes 8847364
  55.1 21.0 %all-to-all-start = ((f32[128,8,128]{2,1,0:T(8,128)}), f32[128,8,128]{2,1,0:T(8,128)S(1)}, u32[]{:S(2)}, u32[]{:S(2)}) async-start(f32[128,8,128]{2,1,0:T(8,128)} %shard_map.133), calls=%async_computation | async-start | bytes 1048576 | tf_op jit(solution)/shard_map/all_to_all | solution.py:509
  76.1 1.0 %copy-start.14 = (f32[3,8,4096]{2,1,0:T(8,128)S(1)}, f32[3,8,4096]{2,1,0:T(8,128)}, u32[]{:S(2)}) copy-start(f32[3,8,4096]{2,1,0:T(8,128)} %copy-done.13) | copy-start | bytes 1179652
  (5 other events, 4.5 us)

commit v2 on v1

--- a/solution.py
+++ b/solution.py
@@ -16,8 +16,9 @@
 SECOND = (8.0 / 5.0, -0.2, 8.0 / 315.0, -1.0 / 560.0)
 CENTRAL = -205.0 / 72.0
 UNROLL = (16, 16, 35, 16, 2)
-VMEM_LIMIT = 48 * 1024 * 1024
+VMEM_LIMIT = 20 * 1024 * 1024
 WHOLE = pl.BlockSpec(memory_space=pltpu.VMEM)
+SCALAR = pl.BlockSpec(memory_space=pltpu.SMEM)
 
 
 def lanes_at(index):
@@ -50,17 +51,21 @@
     return u, v, w, p, p * inv
 
 
-def pack_sends(state, to_below, to_above, first_y, last_y):
+def low_rows(odd):
+    return (row_ids() ^ (4 * odd[0])) < 4
+
+
+def pack_sends(state, odd, to_far, to_near, first_y, last_y):
     length = state[0].shape[-1]
     half = length // (2 * LANES)
-    low = row_ids() < 4
+    low = low_rows(odd)
 
     def body(j):
         for f in range(5):
             here = state[f][:, lanes_at(j)]
             other = pltpu.roll(state[f][:, lanes_at(j + half)], 4, 0)
-            to_below[f, :, lanes_at(j)] = jnp.where(low, here, other)
-            to_above[f, :, lanes_at(j)] = jnp.where(low, other, here)
+            to_far[f, :, lanes_at(j)] = jnp.where(low, here, other)
+            to_near[f, :, lanes_at(j)] = jnp.where(low, other, here)
 
     loop(half, body, UNROLL[0])
     width = 4 * NZ
@@ -73,8 +78,15 @@
     return [rho, mom.at[0], mom.at[1], mom.at[2], energy]
 
 
-def pack_kernel(rho, mom, energy, to_below, to_above, first_y, last_y):
-    pack_sends(state_views(rho, mom, energy), to_below, to_above, first_y, last_y)
+def pack_kernel(odd, rho_h, mom_h, energy_h, z_h, rho, mom, energy, along_z, *rest):
+    *sends, sems = rest
+    pairs = ((rho_h, rho), (mom_h, mom), (energy_h, energy), (z_h, along_z))
+    copies = [pltpu.make_async_copy(a, b, sems.at[i]) for i, (a, b) in enumerate(pairs)]
+    for copy in copies:
+        copy.start()
+    for copy in copies:
+        copy.wait()
+    pack_sends(state_views(rho, mom, energy), odd, *sends)
 
 
 def depth_weights():
@@ -95,17 +107,12 @@
 
 
 def stage_kernel(stage, refs):
-    if stage == 0:
-        rho, mom, energy, above, below, before, after, along_z = refs[:8]
-        base = None
-        rest = refs[8:]
-    else:
-        rho, mom, energy, rho0, mom0, energy0 = refs[:6]
-        above, below, before, after, along_z = refs[6:11]
-        base = state_views(rho0, mom0, energy0)
-        rest = refs[11:]
+    odd, along_z, far, near, before, after, rho, mom, energy = refs[:9]
+    base = state_views(*refs[9:12]) if stage else None
+    rest = refs[12:] if stage else refs[9:]
     if stage < 2:
-        rho_o, mom_o, energy_o, to_below, to_above, first_y, last_y = rest[:7]
+        rho_o, mom_o, energy_o = rest[:3]
+        sends = rest[3:7]
         ys, yh, hx, zs, zd = rest[7:]
     else:
         rho_o, mom_o, energy_o, newest = rest[:4]
@@ -116,7 +123,7 @@
     blocks = length // LANES
     half = blocks // 2
     row, lane = row_ids(), lane_ids()
-    low = row < 4
+    low = low_rows(odd)
 
     def fill(fields, at):
         r, mx, my, mz, e = fields
@@ -158,7 +165,7 @@
 
     def unpack(j):
         for f in range(5):
-            a, b = above[f, :, lanes_at(j)], below[f, :, lanes_at(j)]
+            a, b = near[f, :, lanes_at(j)], far[f, :, lanes_at(j)]
             hx[f, :, lanes_at(j)] = jnp.where(low, a, b)
             hx[f, :, lanes_at(j + half)] = pltpu.roll(jnp.where(low, b, a), 4, 0)
 
@@ -233,19 +240,19 @@
 
     loop(blocks, main, UNROLL[4])
     if stage < 2:
-        pack_sends(outs, to_below, to_above, first_y, last_y)
+        pack_sends(outs, odd, *sends)
 
 
 def f32(*shape):
     return jax.ShapeDtypeStruct(shape, jnp.float32)
 
 
-def call(kernel, out_shape, args, scratch=(), flops=0, nbytes=0, **kw):
+def call(kernel, out_shape, args, scratch=(), flops=0, nbytes=0, vmem=VMEM_LIMIT, **kw):
     return pl.pallas_call(
         kernel,
         out_shape=out_shape,
         scratch_shapes=list(scratch),
-        compiler_params=pltpu.CompilerParams(vmem_limit_bytes=VMEM_LIMIT),
+        compiler_params=pltpu.CompilerParams(vmem_limit_bytes=vmem),
         cost_estimate=pl.CostEstimate(
             flops=flops, bytes_accessed=nbytes, transcendentals=0
         ),
@@ -253,6 +260,10 @@
     )(*args)
 
 
+def in_hbm(*arrays):
+    return tuple(pltpu.with_memory_space_constraint(a, pltpu.HBM) for a in arrays)
+
+
 def state_shapes(rows, length):
     return (f32(rows, length), f32(3, rows, length), f32(rows, length))
 
@@ -263,24 +274,29 @@
     return (packed, packed, edge, edge)
 
 
-def pack(state):
+def pack(odd, state):
     rows, length = state[0].shape
-    shapes = send_shapes(rows, length)
-    return call(
+    weights = depth_weights()
+    shapes = state_shapes(rows, length)
+    shapes += (jax.ShapeDtypeStruct(weights.shape, weights.dtype),)
+    shapes += send_shapes(rows, length)
+    out = call(
         pack_kernel,
         shapes,
-        state,
-        in_specs=[WHOLE] * 3,
-        out_specs=[WHOLE] * 4,
+        (odd, *in_hbm(*state, weights)),
+        [pltpu.SemaphoreType.DMA((4,))],
+        in_specs=[SCALAR] + [pl.BlockSpec(memory_space=pltpu.HBM)] * 4,
+        out_specs=[WHOLE] * 8,
         nbytes=10**6,
     )
-
-
-def stage_call(stage, state, base, halo):
+    return out[:3], out[3], out[4:]
+
+
+def stage_call(stage, odd, along_z, halo, state, base):
     rows, length = state[0].shape
     out = state_shapes(rows, length)
     out += send_shapes(rows, length) if stage < 2 else (f32(3, rows, length),)
-    args = tuple(state) + (tuple(base) if stage else ()) + tuple(halo) + (depth_weights(),)
+    args = (odd, along_z, *halo, *state) + (tuple(base) if stage else ())
     scratch = [
         pltpu.VMEM((10, rows, length + 8 * NZ), jnp.float32),
         pltpu.VMEM((9, rows, length + 8 * NZ), jnp.float32),
@@ -293,7 +309,7 @@
         out,
         args,
         scratch,
-        in_specs=[WHOLE] * len(args),
+        in_specs=[SCALAR] + [WHOLE] * (len(args) - 1),
         out_specs=[WHOLE] * len(out),
         flops=32768 * 700,
         nbytes=3 * 10**6,
@@ -324,52 +340,77 @@
     return jnp.concatenate([small[8 * g : 8 * g + 8] for g in range(4)], 1)
 
 
-def gram_kernel(basis, snaps, gram, total):
-    width = 1024
+GRAM_WIDTH = 1024
+
+
+def gram_kernel(basis_h, snaps_h, gram, merged, basis, snaps, total, sems):
+    width = GRAM_WIDTH
+    places = [slice(i, i + width) for i in range(0, basis_h.shape[-1], width)]
+    loads = []
+    for n, at in enumerate(places):
+        for m, (source, held) in enumerate(((basis_h, basis), (snaps_h, snaps))):
+            loads.append(
+                pltpu.make_async_copy(
+                    source.at[:, :, :, at], held.at[:, :, :, at], sems.at[n, m]
+                )
+            )
+            loads[-1].start()
     total[...] = jnp.zeros_like(total)
-
-    def add(i):
-        at = pl.ds(pl.multiple_of(i * width, width), width)
+    for n, at in enumerate(places):
+        loads[2 * n].wait()
+        loads[2 * n + 1].wait()
         for c in range(3):
             rows = merged_rows(basis, snaps, c, at)
+            merged[c, :, at] = rows
             total[...] += lax.dot_general(
                 rows, rows, (((1,), (1,)), ((), ())), preferred_element_type=jnp.float32
             )
-
-    loop(basis.shape[-1] // width, add)
     kept = jnp.where(same_layer(), total[...], 0.0)
     left = group_matrix((32, 256), 1, jnp.float32)
     right = group_matrix((256, 32), 0, jnp.float32)
     small = jnp.dot(left, kept, precision=lax.Precision.HIGHEST)
-    gram[...] = pack_square(jnp.dot(small, right, precision=lax.Precision.HIGHEST))
+    small = jnp.dot(small, right, precision=lax.Precision.HIGHEST)
+    gram[...] = pack_square(small)
 
 
 def gram_call(basis, snaps):
     length = basis.shape[-1]
+    hbm = pl.BlockSpec(memory_space=pltpu.HBM)
     return call(
         gram_kernel,
-        f32(8, LANES),
-        (basis, snaps),
-        [pltpu.VMEM((256, 256), jnp.float32)],
-        in_specs=[WHOLE] * 2,
-        out_specs=WHOLE,
+        (f32(8, LANES), pltpu.VMEM((3, 256, length), jnp.bfloat16)),
+        in_hbm(basis, snaps),
+        [
+            pltpu.VMEM(basis.shape, jnp.bfloat16),
+            pltpu.VMEM(snaps.shape, jnp.bfloat16),
+            pltpu.VMEM((256, 256), jnp.float32),
+            pltpu.SemaphoreType.DMA((length // GRAM_WIDTH, 2)),
+        ],
+        in_specs=[hbm, hbm],
+        out_specs=[WHOLE] * 2,
         flops=2 * 256 * 256 * 3 * length,
         nbytes=31 * 3 * 8 * length * 2,
     )
 
 
-def cross_kernel(basis, snaps, newest, gram, parts, total):
-    total[...] = jnp.zeros_like(total)
+def cross_kernel(merged, newest, gram, parts, total):
+    blocks = newest.shape[-1] // LANES
 
     def add(i):
-        at = lanes_at(i)
-        new = [newest[c, :, at] for c in range(3)]
-        for k in range(31):
-            ref, n = (basis, k) if k < 16 else (snaps, k - 16)
-            total[k] += sum(ref[n, c, :, at].astype(jnp.float32) * new[c] for c in range(3))
-        total[31] += sum(n * n for n in new)
-
-    loop(basis.shape[-1] // LANES, add, 4)
+        pair = pl.ds(pl.multiple_of(i * 16, 16), 16)
+        sums = [jnp.zeros((2, 8, LANES), jnp.float32) for _ in range(4)]
+        for n in range(3 * blocks):
+            c, at = n % 3, slice(n // 3 * LANES, (n // 3 + 1) * LANES)
+            rows = merged[c, pair, at].astype(jnp.float32).reshape(2, 8, LANES)
+            sums[n % 4] = sums[n % 4] + rows * newest[c, :, at]
+        total[pl.ds(i * 2, 2)] = (sums[0] + sums[1]) + (sums[2] + sums[3])
+
+    loop(16, add)
+    own = [jnp.zeros((8, LANES), jnp.float32) for _ in range(4)]
+    for n in range(3 * blocks):
+        value = newest[n % 3, :, n // 3 * LANES : (n // 3 + 1) * LANES]
+        own[n % 4] = own[n % 4] + value * value
+    total[31] = (own[0] + own[1]) + (own[2] + own[3])
     sums = jnp.sum(total[...], axis=1)
     line = lax.dot_general(
         jnp.ones((8, LANES), jnp.float32),
@@ -382,18 +423,49 @@
     parts[...] = jnp.broadcast_to(jnp.where(last, line, gram[...])[None], parts.shape)
 
 
-def cross_call(basis, snaps, newest, gram, copies):
-    length = basis.shape[-1]
+def cross_call(merged, newest, gram, copies):
+    length = newest.shape[-1]
     return call(
         cross_kernel,
         f32(copies, 8, LANES),
-        (basis, snaps, newest, gram),
+        (merged, newest, gram),
         [pltpu.VMEM((32, 8, LANES), jnp.float32)],
-        in_specs=[WHOLE] * 4,
+        in_specs=[WHOLE] * 3,
         out_specs=WHOLE,
         flops=31 * 6 * 8 * length,
         nbytes=31 * 3 * 8 * length * 2,
     )
+
+
+def eliminated(work):
+    wide = (8, LANES)
+    blocks = [work[8 * i : 8 * i + 8] for i in range(4)]
+    row = row_ids()
+    done = []
+    for b in range(4):
+        columns = [
+            {i: jnp.broadcast_to(blocks[i][:, 8 * b + s : 8 * b + s + 1], wide) for i in range(b, 4)}
+            for s in range(8)
+        ]
+        rows = [jnp.broadcast_to(blocks[b][s : s + 1], wide) for s in range(8)]
+        result = jnp.zeros(wide, jnp.float32)
+        scaled = []
+        for t in range(8):
+            pivot = jnp.broadcast_to(columns[t][b][t : t + 1], wide)
+            inv = 1.0 / pivot
+            result = jnp.where(row == t, rows[t] / jnp.sqrt(pivot), result)
+            scaled.append(rows[t] * inv)
+            for s in range(t + 1, 8):
+                ratio = jnp.broadcast_to(columns[s][b][t : t + 1], wide) * inv
+                below = jnp.broadcast_to(columns[t][b][s : s + 1], wide)
+                rows[s] = rows[s] - below * scaled[t]
+                for i in range(b, 4):
+                    columns[s][i] = columns[s][i] - columns[t][i] * ratio
+        done.append(result)
+        for i in range(b + 1, 4):
+            for t in range(8):
+                blocks[i] = blocks[i] - columns[t][i] * scaled[t]
+    return jnp.concatenate(done, 0)
 
 
 def weights_of(weight, parts, scale, factor, high, low, diagonal):
@@ -408,15 +480,7 @@
     g = jnp.where(col == 31, line, g)
     g = g * (weight * s) * s_col
     eye = (row == col).astype(jnp.float32)
-    work = jnp.concatenate([g, eye, jnp.zeros((32, 64), jnp.float32)], 1)
-    rows128 = lax.broadcasted_iota(jnp.int32, (32, LANES), 0)
-    done = jnp.zeros((32, LANES), jnp.float32)
-    for j in range(32):
-        column = jnp.broadcast_to(work[:, j : j + 1], (32, LANES))
-        pivot_row = jnp.broadcast_to(work[j : j + 1], (32, LANES))
-        pivot = jnp.broadcast_to(column[j : j + 1], (32, LANES))
-        done = jnp.where(rows128 == j, pivot_row / jnp.sqrt(pivot), done)
-        work = work - column * (pivot_row / pivot)
+    done = eliminated(jnp.concatenate([g, eye, jnp.zeros((32, 64), jnp.float32)], 1))
     factor[...] = jnp.where(col >= row, done[:, :32], 0.0)
     l = jnp.where(col <= row, done[:, 32:64], 0.0)
     diagonal[...] = jnp.broadcast_to(l[31:32, 31:32], diagonal.shape)
@@ -434,44 +498,64 @@
         out[...] = jnp.where(keep, wide, 0.0).astype(jnp.bfloat16)
 
 
+MODES_WIDTH = 2048
+
+
 def modes_kernel(
-    weight, parts, scale, basis, snaps, newest, modes, factor, high, low, diagonal
+    weight,
+    parts,
+    scale,
+    merged,
+    newest,
+    modes,
+    factor,
+    out,
+    high,
+    low,
+    diagonal,
+    out_sems,
 ):
-    step = pl.program_id(0)
-
-    @pl.when(step == 0)
-    def _():
-        weights_of(weight, parts, scale, factor, high, low, diagonal)
-
-    width = modes.shape[-1]
-    at = pl.ds(pl.multiple_of(step * width, width), width)
-    for c in range(3):
-        rows = merged_rows(basis, snaps, c, at)
-        out = jnp.dot(high[...], rows, preferred_element_type=jnp.float32)
-        out = out + jnp.dot(low[...], rows, preferred_element_type=jnp.float32)
-        out = out.reshape(32, 8, width)
-        modes[:31, c] = out[:31].astype(jnp.bfloat16)
+    width = MODES_WIDTH
+    pieces = []
+    for i in range(newest.shape[-1] // width):
+        for c in range(3):
+            pieces.append((len(pieces), c, slice(i * width, (i + 1) * width)))
+    weights_of(weight, parts, scale, factor, high, low, diagonal)
+    stores = []
+    for n, c, at in pieces:
+        rows = merged[c, :, at]
+        value = jnp.dot(high[...], rows, preferred_element_type=jnp.float32)
+        value = value + jnp.dot(low[...], rows, preferred_element_type=jnp.float32)
+        value = value.reshape(32, 8, width)
+        out[:31, c, :, at] = value[:31].astype(jnp.bfloat16)
         own = diagonal[:, :1] * newest[c, :, at]
-        modes[31, c] = (out[31] + own).astype(jnp.bfloat16)
-
-
-def modes_call(parts, scale, basis, snaps, newest, weight, width=1024):
-    length = basis.shape[-1]
+        out[31, c, :, at] = (value[31] + own).astype(jnp.bfloat16)
+        store = pltpu.make_async_copy(
+            out.at[:, c, :, at], modes.at[:, c, :, at], out_sems.at[n]
+        )
+        store.start()
+        stores.append(store)
+    for store in stores:
+        store.wait()
+
+
+def modes_call(parts, scale, merged, newest, weight):
+    length = newest.shape[-1]
+    count = 3 * length // MODES_WIDTH
+    shape = (32, 3, 8, length)
     return call(
         functools.partial(modes_kernel, weight),
-        (jax.ShapeDtypeStruct((32, 3, 8, length), jnp.bfloat16), f32(32, 32)),
-        (parts, scale, basis, snaps, newest),
+        (jax.ShapeDtypeStruct(shape, jnp.bfloat16), f32(32, 32)),
+        (parts, scale, merged, newest),
         [
+            pltpu.VMEM(shape, jnp.bfloat16),
             pltpu.VMEM((256, 256), jnp.bfloat16),
             pltpu.VMEM((256, 256), jnp.bfloat16),
             pltpu.VMEM((8, LANES), jnp.float32),
+            pltpu.SemaphoreType.DMA((count,)),
         ],
-        grid=(length // width,),
-        in_specs=[WHOLE] * 5,
-        out_specs=[
-            pl.BlockSpec((32, 3, 8, width), lambda i: (0, 0, 0, i)),
-            pl.BlockSpec((32, 32), lambda i: (0, 0)),
-        ],
+        in_specs=[WHOLE] * 4,
+        out_specs=[pl.BlockSpec(memory_space=pltpu.HBM), WHOLE],
         flops=4 * 256 * 256 * 3 * length,
         nbytes=63 * 3 * 8 * length * 2,
     )
@@ -484,12 +568,14 @@
 
 
 def exchange(sends):
-    to_below, to_above, first_y, last_y = sends
-    above = shifted(to_below, "gx", -1)
-    below = shifted(to_above, "gx", 1)
+    to_far, to_near, first_y, last_y = sends
+    count = lax.axis_size("gx")
+    pairs = [(i, (i + 1) % count) for i in range(1, count, 2)]
+    far = lax.ppermute(to_far, "gx", pairs + [(j, i) for i, j in pairs])
+    near = lax.ppermute(to_near, "gx", [(i, i ^ 1) for i in range(count)])
     before = shifted(last_y, "gy", 1)
     after = shifted(first_y, "gy", -1)
-    return (above, below, before, after)
+    return (far, near, before, after)
 
 
 def local(density, momentum, energy, basis, scales, snapshots):
@@ -499,15 +585,20 @@
     fields = (density, momentum, energy)
     scale = jnp.concatenate([scales, jnp.ones((16,), jnp.float32)])[None]
 
-    halo = exchange(pack(fields))
-    gram = gram_call(basis, snapshots)
-    first = stage_call(0, fields, None, halo)
-    second = stage_call(1, first[:3], fields, exchange(first[3:]))
-    final = stage_call(2, second[:3], fields, exchange(second[3:]))
+    odd = (lax.axis_index("gx") % 2).astype(jnp.int32)[None]
+    fields, along_z, sends = pack(odd, fields)
+    halo = exchange(sends)
+    gram, merged = gram_call(basis, snapshots)
+    halo, gram, merged = lax.optimization_barrier((halo, gram, merged))
+    first = stage_call(0, odd, along_z, halo, fields, None)
+    halo = exchange(first[3:])
+    second = stage_call(1, odd, along_z, halo, first[:3], fields)
+    halo = exchange(second[3:])
+    final = stage_call(2, odd, along_z, halo, second[:3], fields)
     newest = final[3]
-    parts = cross_call(basis, snapshots, newest, gram, devices)
+    parts = cross_call(merged, newest, gram, devices)
     parts = lax.all_to_all(parts, ("gx", "gy"), 0, 0, tiled=True)
-    modes, factor = modes_call(parts, scale, basis, snapshots, newest, weight)
+    modes, factor = modes_call(parts, scale, merged, newest, weight)
     return (final[0], final[1], final[2], modes, factor)
 
 

time: 89.4 us -> 77.5 us (0.87)
  local copies, waits for them, and re-layouts: 8.44 us -> 2.8 us
  starting transfers between devices: 34.2 us -> 30 us
  Pallas kernels: 29 us -> 25.3 us
  waiting for transfers between devices: 16.5 us -> 18.3 us
    ppermute x12 -> x6, starting transfers between devices: 27 us -> 10.2 us  [shifted(): return lax.ppermute(block, axis, route)]
    ppermute x0 -> x6, starting transfers between devices: none -> 11.3 us  [the longest x3 8.26 us: exchange(): near = lax.ppermute(to_near, 'gx', [(i, i ^ 1) for i in range(count)])]
    unnamed x32 -> x6, local copies, waits for them, and re-layouts: 8.44 us -> 2.79 us
    pallas_call x7, Pallas kernels: 29 us -> 25.3 us  [call(): pl.pallas_call(kernel, out_shape=out_shape, scratch_shapes=list(scratch),...]
    all_to_all x1, starting transfers between devices: 7.19 us -> 8.46 us  [local(): parts = lax.all_to_all(parts, ('gx', 'gy'), 0, 0, tiled=True)]
    ppermute x12 -> x6, waiting for transfers between devices: 2.81 us -> 3.88 us  [shifted(): return lax.ppermute(block, axis, route)]
  transfers between devices with their start and end apart: 13 -> 13, of which waited for: 3 -> 4; matrix products, arithmetic and copies ran while one was open for 0% -> 0% of each run, Pallas kernels for 3% -> 7%
where the time goes in v2:
time: 77.5 us; the launch traced here: 77.3 us
  starting transfers between devices  30 us (39%)
  Pallas kernels  25.3 us (33%)
  waiting for transfers between devices  18.3 us (24%)
  local copies, waits for them, and re-layouts  2.8 us (4%)
  between operations  0.92 us (1%)
    pallas_call x7, Pallas kernels, call(): pl.pallas_call(kernel, out_shape=out_shape, scratch_shapes=list(scratch),...  25.3 us
    all_to_all x1, waiting for transfers between devices, local(): parts = lax.all_to_all(parts, ('gx', 'gy'), 0, 0, tiled=True)  13.7 us
    ppermute x6, starting transfers between devices, shifted(): return lax.ppermute(block, axis, route)  10.2 us
    all_to_all x1, starting transfers between devices, local(): parts = lax.all_to_all(parts, ('gx', 'gy'), 0, 0, tiled=True)  8.46 us
    ppermute x3, starting transfers between devices, exchange(): near = lax.ppermute(to_near, 'gx', [(i, i ^ 1) for i in range(count)])  8.26 us
    ppermute x6, waiting for transfers between devices, shifted(): return lax.ppermute(block, axis, route)  3.88 us
    ppermute x3, starting transfers between devices, exchange(): far = lax.ppermute(to_far, 'gx', pairs + [(j, i) for i, j in pairs])  3.04 us
    unnamed x6, local copies, waits for them, and re-layouts  2.79 us
  transfers between devices with their start and end apart: 13, of which 4 were waited for; matrix products, arithmetic and copies ran while one was open for 0% of the time, Pallas kernels for 7%

profile of v2, /device:TPU:1, one launch (start us, length us, event | category | flops | bytes accessed | tf_op | source)
XLA Modules:
  0.0 77.3 jit_solution(15834647868392736485)
XLA Ops:
  0.6 1.3 %shard_map.110 = (f32[8,4096]{1,0:T(8,128)S(1)}, f32[3,8,4096]{2,1,0:T(8,128)S(1)}, f32[8,4096]{1,0:T(8,128)S(1)}, bf16[2,256,256]{2,1,0:T(8,128)(2,1)S(1)}, f32...) custom-call(s32[1]{0:T(128)} %bitcast.odd.refs_0_, ...), custom_call_target="tpu_custom_call" | custom-call | bytes 1000000 | tf_op jit(solution)/shard_map/pallas_call | solution.py:251
  1.9 2.7 %collective-permute-start = (f32[5,8,2048]{2,1,0:T(8,128)S(1)}, f32[5,8,2048]{2,1,0:T(8,128)S(1)}, u32[]{:S(2)}, u32[]{:S(2)}) collective-permute-start(f32[5,8,2048]{2,1,0:T(8,128)S(1)} %get-tuple-element.42), channel_id=1, source_target_pairs={{4,8},{12,16},{20,24},{28,32},{36,40},{44,48},{52,56},{60,64},{68,... | collective-permute-start | bytes 983048 | tf_op jit(solution)/shard_map/ppermute | solution.py:574
  4.6 3.6 %collective-permute-start.1 = (f32[5,8,2048]{2,1,0:T(8,128)S(1)}, f32[5,8,2048]{2,1,0:T(8,128)S(1)}, u32[]{:S(2)}, u32[]{:S(2)}) collective-permute-start(f32[5,8,2048]{2,1,0:T(8,128)S(1)} %get-tuple-element.43), channel_id=1, source_target_pairs={{0,4},{4,0},{8,12},{12,8},{16,20},{20,16},{24,28},{28,24},{32,36},... | collective-permute-start | bytes 983048 | tf_op jit(solution)/shard_map/ppermute | solution.py:575
  8.2 1.6 %collective-permute-start.2 = (f32[5,8,256]{2,1,0:T(8,128)S(1)}, f32[5,8,256]{2,1,0:T(8,128)S(1)}, u32[]{:S(2)}, u32[]{:S(2)}) collective-permute-start(f32[5,8,256]{2,1,0:T(8,128)S(1)} %get-tuple-element.44), channel_id=1, source_target_pairs={{0,1},{1,2},{2,3},{3,0},{4,5},{5,6},{6,7},{7,4},{8,9},{9,10},{10,1... | collective-permute-start | bytes 122888 | tf_op jit(solution)/shard_map/ppermute | solution.py:567
  9.8 2.1 %collective-permute-start.3 = (f32[5,8,256]{2,1,0:T(8,128)S(1)}, f32[5,8,256]{2,1,0:T(8,128)S(1)}, u32[]{:S(2)}, u32[]{:S(2)}) collective-permute-start(f32[5,8,256]{2,1,0:T(8,128)S(1)} %get-tuple-element.45), channel_id=1, source_target_pairs={{0,3},{1,0},{2,1},{3,2},{4,7},{5,4},{6,5},{7,6},{8,11},{9,8},{10,9... | collective-permute-start | bytes 122888 | tf_op jit(solution)/shard_map/ppermute | solution.py:567
  11.9 5.6 %shard_map.111 = (f32[8,128]{1,0:T(8,128)S(1)}, bf16[3,256,4096]{2,1,0:T(8,128)(2,1)S(1)}) custom-call(bf16[16,3,8,4096]{3,2,1,0:T(8,128)(2,1)} %basis_h.1, bf16[15,3,8,4096]{3,2,1,0:T(8,128)(2,1)} %snaps_h.1), custom_call_target="tpu_custom_call" | custom-call | flops 1610612736 | bytes 6094848 | tf_op jit(solution)/shard_map/pallas_call | solution.py:251
  17.6 2.8 %shard_map.112 = (f32[8,4096]{1,0:T(8,128)S(1)}, f32[3,8,4096]{2,1,0:T(8,128)S(1)}, f32[8,4096]{1,0:T(8,128)S(1)}, f32[5,8,2048]{2,1,0:T(8,128)S(1)}, f32[5,8,20...) custom-call(s32[1]{0:T(128)} %bitcast.odd.refs_0_, ...), custom_call_target="tpu_custom_call" | custom-call | flops 22937600 | bytes 3000000 | tf_op jit(solution)/shard_map/pallas_call | solution.py:251
  20.4 0.9 %collective-permute-start.5 = (f32[5,8,2048]{2,1,0:T(8,128)S(1)}, f32[5,8,2048]{2,1,0:T(8,128)S(1)}, u32[]{:S(2)}, u32[]{:S(2)}) collective-permute-start(f32[5,8,2048]{2,1,0:T(8,128)S(1)} %get-tuple-element.56), channel_id=1, source_target_pairs={{0,4},{4,0},{8,12},{12,8},{16,20},{20,16},{24,28},{28,24},{32,36},... | collective-permute-start | bytes 983048 | tf_op jit(solution)/shard_map/ppermute | solution.py:575
  21.3 1.1 %collective-permute-start.6 = (f32[5,8,256]{2,1,0:T(8,128)S(1)}, f32[5,8,256]{2,1,0:T(8,128)S(1)}, u32[]{:S(2)}, u32[]{:S(2)}) collective-permute-start(f32[5,8,256]{2,1,0:T(8,128)S(1)} %get-tuple-element.57), channel_id=1, source_target_pairs={{0,1},{1,2},{2,3},{3,0},{4,5},{5,6},{6,7},{7,4},{8,9},{9,10},{10,1... | collective-permute-start | bytes 122888 | tf_op jit(solution)/shard_map/ppermute | solution.py:567
  22.5 2.1 %collective-permute-start.7 = (f32[5,8,256]{2,1,0:T(8,128)S(1)}, f32[5,8,256]{2,1,0:T(8,128)S(1)}, u32[]{:S(2)}, u32[]{:S(2)}) collective-permute-start(f32[5,8,256]{2,1,0:T(8,128)S(1)} %get-tuple-element.58), channel_id=1, source_target_pairs={{0,3},{1,0},{2,1},{3,2},{4,7},{5,4},{6,5},{7,6},{8,11},{9,8},{10,9... | collective-permute-start | bytes 122888 | tf_op jit(solution)/shard_map/ppermute | solution.py:567
  24.6 1.9 %collective-permute-done.6.refs_4_ = f32[5,8,256]{2,1,0:T(8,128)S(1)} collective-permute-done((f32[5,8,256]{2,1,0:T(8,128)S(1)}, f32[5,8,256]{2,1,0:T(8,128)S(1)}, u32[]{:S(2)}, u32[]{:S(2)}) %collective-permute-start.6) | collective-permute-done | bytes 40992 | tf_op jit(solution)/shard_map/ppermute | solution.py:567
  26.5 0.7 collective-permute-done.4.refs_2_
  27.2 2.8 %shard_map.113 = (f32[8,4096]{1,0:T(8,128)S(1)}, f32[3,8,4096]{2,1,0:T(8,128)S(1)}, f32[8,4096]{1,0:T(8,128)S(1)}, f32[5,8,2048]{2,1,0:T(8,128)S(1)}, f32[5,8,20...) custom-call(s32[1]{0:T(128)} %bitcast.odd.refs_0_, ...), custom_call_target="tpu_custom_call" | custom-call | flops 22937600 | bytes 3000000 | tf_op jit(solution)/shard_map/pallas_call | solution.py:251
  30.0 0.3 collective-permute-start.8
  30.3 3.8 %collective-permute-start.9 = (f32[5,8,2048]{2,1,0:T(8,128)S(1)}, f32[5,8,2048]{2,1,0:T(8,128)S(1)}, u32[]{:S(2)}, u32[]{:S(2)}) collective-permute-start(f32[5,8,2048]{2,1,0:T(8,128)S(1)} %get-tuple-element.63), channel_id=1, source_target_pairs={{0,4},{4,0},{8,12},{12,8},{16,20},{20,16},{24,28},{28,24},{32,36},... | collective-permute-start | bytes 983048 | tf_op jit(solution)/shard_map/ppermute | solution.py:575
  34.1 1.1 %collective-permute-start.10 = (f32[5,8,256]{2,1,0:T(8,128)S(1)}, f32[5,8,256]{2,1,0:T(8,128)S(1)}, u32[]{:S(2)}, u32[]{:S(2)}) collective-permute-start(f32[5,8,256]{2,1,0:T(8,128)S(1)} %get-tuple-element.64), channel_id=1, source_target_pairs={{0,1},{1,2},{2,3},{3,0},{4,5},{5,6},{6,7},{7,4},{8,9},{9,10},{10,1... | collective-permute-start | bytes 122888 | tf_op jit(solution)/shard_map/ppermute | solution.py:567
  35.2 2.1 %collective-permute-start.11 = (f32[5,8,256]{2,1,0:T(8,128)S(1)}, f32[5,8,256]{2,1,0:T(8,128)S(1)}, u32[]{:S(2)}, u32[]{:S(2)}) collective-permute-start(f32[5,8,256]{2,1,0:T(8,128)S(1)} %get-tuple-element.65), channel_id=1, source_target_pairs={{0,3},{1,0},{2,1},{3,2},{4,7},{5,4},{6,5},{7,6},{8,11},{9,8},{10,9... | collective-permute-start | bytes 122888 | tf_op jit(solution)/shard_map/ppermute | solution.py:567
  37.3 1.9 %collective-permute-done.10.refs_4_ = f32[5,8,256]{2,1,0:T(8,128)S(1)} collective-permute-done((f32[5,8,256]{2,1,0:T(8,128)S(1)}, f32[5,8,256]{2,1,0:T(8,128)S(1)}, u32[]{:S(2)}, u32[]{:S(2)}) %collective-permute-start.10) | collective-permute-done | bytes 40992 | tf_op jit(solution)/shard_map/ppermute | solution.py:567
  39.3 3.6 %shard_map.114 = (f32[8,4096]{1,0:T(8,128)}, f32[3,8,4096]{2,1,0:T(8,128)}, f32[8,4096]{1,0:T(8,128)}, f32[3,8,4096]{2,1,0:T(8,128)S(1)}) custom-call(s32[1]{0:T(128)} %bitcast.odd.refs_0_, bf16[2,256,256]{2,1,0:T(8,128)(2,1)S(1)} %get-tuple-element.41.refs_1_, f32[5,8,2048]{2,1,0:T(8,128)S(1)} %collective-permute-done.8.refs_2_, ...), custom_call_target="tpu_custom_call" | custom-call | flops 22937600 | bytes 3000000 | tf_op jit(solution)/shard_map/pallas_call | solution.py:251
  42.9 2.6 %shard_map.115 = f32[128,8,128]{2,1,0:T(8,128)} custom-call(bf16[3,256,4096]{2,1,0:T(8,128)(2,1)S(1)} %get-tuple-element.72.merged, f32[3,8,4096]{2,1,0:T(8,128)S(1)} %get-tuple-element.73.newest, f32[8,128]{1,0:T(8,128)S(1)} %get-tuple-element.74.gram), custom_call_target="tpu_custom_call" | custom-call | flops 6094848 | bytes 6094848 | tf_op jit(solution)/shard_map/pallas_call | solution.py:251
  45.5 8.5 %all-to-all-start = ((f32[128,8,128]{2,1,0:T(8,128)}), f32[128,8,128]{2,1,0:T(8,128)S(1)}, u32[]{:S(2)}, u32[]{:S(2)}) async-start(f32[128,8,128]{2,1,0:T(8,128)} %shard_map.115), calls=%async_computation | async-start | bytes 1048576 | tf_op jit(solution)/shard_map/all_to_all | solution.py:600
  54.0 13.7 %all-to-all-done.parts = f32[128,8,128]{2,1,0:T(8,128)S(1)} async-done(((f32[128,8,128]{2,1,0:T(8,128)}), f32[128,8,128]{2,1,0:T(8,128)S(1)}, u32[]{:S(2)}, u32[]{:S(2)}) %all-to-all-start) | async-done | bytes 524320 | tf_op jit(solution)/shard_map/all_to_all | solution.py:600
  67.7 2.8 %copy-done.1 = bf16[3,256,4096]{2,1,0:T(8,128)(2,1)S(1)} copy-done((bf16[3,256,4096]{2,1,0:T(8,128)(2,1)S(1)}, bf16[3,256,4096]{2,1,0:T(8,128)(2,1)}, u32[]{:S(2)}) %copy-start.1) | copy-done | bytes 6291480
  70.5 6.6 %shard_map.116 = (bf16[32,3,8,4096]{3,2,1,0:T(8,128)(2,1)}, f32[32,32]{1,0:T(8,128)}) custom-call(f32[128,8,128]{2,1,0:T(8,128)S(1)} %all-to-all-done.parts, f32[1,32]{1,0:T(1,128)S(1)} %pad_bitcast_fusion.scale, bf16[3,256,4096]{2,1,0:T(8,128)(2,1)S(1)} %copy-done.1, f32[3,8,4096]{2,1,0:T(8,128)S(1)} %get-tuple-element.73.newest), custom_call_target="tpu_custom_call" | custom-call | flops 3221225472 | bytes 12386304 | tf_op jit(solution)/shard_map/pallas_call | solution.py:251
  (16 shorter events, 0.1 us)
Async XLA Ops:
  1.9 15.6 %collective-permute-start = (f32[5,8,2048]{2,1,0:T(8,128)S(1)}, f32[5,8,2048]{2,1,0:T(8,128)S(1)}, u32[]{:S(2)}, u32[]{:S(2)}) collective-permute-start(f32[5,8,2048]{2,1,0:T(8,128)S(1)} %get-tuple-element.42), channel_id=1, source_target_pairs={{4,8},{12,16},{20,24},{28,32},{36,40},{44,48},{52,56},{60,64},{68,... | collective-permute-start | bytes 983048 | tf_op jit(solution)/shard_map/ppermute | solution.py:574
  4.6 12.9 %collective-permute-start.1 = (f32[5,8,2048]{2,1,0:T(8,128)S(1)}, f32[5,8,2048]{2,1,0:T(8,128)S(1)}, u32[]{:S(2)}, u32[]{:S(2)}) collective-permute-start(f32[5,8,2048]{2,1,0:T(8,128)S(1)} %get-tuple-element.43), channel_id=1, source_target_pairs={{0,4},{4,0},{8,12},{12,8},{16,20},{20,16},{24,28},{28,24},{32,36},... | collective-permute-start | bytes 983048 | tf_op jit(solution)/shard_map/ppermute | solution.py:575
  8.2 9.4 %collective-permute-start.2 = (f32[5,8,256]{2,1,0:T(8,128)S(1)}, f32[5,8,256]{2,1,0:T(8,128)S(1)}, u32[]{:S(2)}, u32[]{:S(2)}) collective-permute-start(f32[5,8,256]{2,1,0:T(8,128)S(1)} %get-tuple-element.44), channel_id=1, source_target_pairs={{0,1},{1,2},{2,3},{3,0},{4,5},{5,6},{6,7},{7,4},{8,9},{9,10},{10,1... | collective-permute-start | bytes 122888 | tf_op jit(solution)/shard_map/ppermute | solution.py:567
  9.8 7.7 %collective-permute-start.3 = (f32[5,8,256]{2,1,0:T(8,128)S(1)}, f32[5,8,256]{2,1,0:T(8,128)S(1)}, u32[]{:S(2)}, u32[]{:S(2)}) collective-permute-start(f32[5,8,256]{2,1,0:T(8,128)S(1)} %get-tuple-element.45), channel_id=1, source_target_pairs={{0,3},{1,0},{2,1},{3,2},{4,7},{5,4},{6,5},{7,6},{8,11},{9,8},{10,9... | collective-permute-start | bytes 122888 | tf_op jit(solution)/shard_map/ppermute | solution.py:567
  17.5 25.4 %copy-start = (bf16[3,256,4096]{2,1,0:T(8,128)(2,1)}, bf16[3,256,4096]{2,1,0:T(8,128)(2,1)S(1)}, u32[]{:S(2)}) copy-start(bf16[3,256,4096]{2,1,0:T(8,128)(2,1)S(1)} %get-tuple-element.72.merged) | copy-start | bytes 18874372
  20.3 6.9 %collective-permute-start.4 = (f32[5,8,2048]{2,1,0:T(8,128)S(1)}, f32[5,8,2048]{2,1,0:T(8,128)S(1)}, u32[]{:S(2)}, u32[]{:S(2)}) collective-permute-start(f32[5,8,2048]{2,1,0:T(8,128)S(1)} %get-tuple-element.55), channel_id=1, source_target_pairs={{4,8},{12,16},{20,24},{28,32},{36,40},{44,48},{52,56},{60,64},{68,... | collective-permute-start | bytes 983048 | tf_op jit(solution)/shard_map/ppermute | solution.py:574
  20.4 6.8 %collective-permute-start.5 = (f32[5,8,2048]{2,1,0:T(8,128)S(1)}, f32[5,8,2048]{2,1,0:T(8,128)S(1)}, u32[]{:S(2)}, u32[]{:S(2)}) collective-permute-start(f32[5,8,2048]{2,1,0:T(8,128)S(1)} %get-tuple-element.56), channel_id=1, source_target_pairs={{0,4},{4,0},{8,12},{12,8},{16,20},{20,16},{24,28},{28,24},{32,36},... | collective-permute-start | bytes 983048 | tf_op jit(solution)/shard_map/ppermute | solution.py:575
  21.3 5.2 %collective-permute-start.6 = (f32[5,8,256]{2,1,0:T(8,128)S(1)}, f32[5,8,256]{2,1,0:T(8,128)S(1)}, u32[]{:S(2)}, u32[]{:S(2)}) collective-permute-start(f32[5,8,256]{2,1,0:T(8,128)S(1)} %get-tuple-element.57), channel_id=1, source_target_pairs={{0,1},{1,2},{2,3},{3,0},{4,5},{5,6},{6,7},{7,4},{8,9},{9,10},{10,1... | collective-permute-start | bytes 122888 | tf_op jit(solution)/shard_map/ppermute | solution.py:567
  22.5 4.1 %collective-permute-start.7 = (f32[5,8,256]{2,1,0:T(8,128)S(1)}, f32[5,8,256]{2,1,0:T(8,128)S(1)}, u32[]{:S(2)}, u32[]{:S(2)}) collective-permute-start(f32[5,8,256]{2,1,0:T(8,128)S(1)} %get-tuple-element.58), channel_id=1, source_target_pairs={{0,3},{1,0},{2,1},{3,2},{4,7},{5,4},{6,5},{7,6},{8,11},{9,8},{10,9... | collective-permute-start | bytes 122888 | tf_op jit(solution)/shard_map/ppermute | solution.py:567
  27.2 26.8 %copy-start.2 = (f32[16]{0:T(128)S(1)}, f32[16]{0:T(128)}, u32[]{:S(2)}) copy-start(f32[16]{0:T(128)} %param.11) | copy-start | bytes 196
  30.0 9.2 %collective-permute-start.8 = (f32[5,8,2048]{2,1,0:T(8,128)S(1)}, f32[5,8,2048]{2,1,0:T(8,128)S(1)}, u32[]{:S(2)}, u32[]{:S(2)}) collective-permute-start(f32[5,8,2048]{2,1,0:T(8,128)S(1)} %get-tuple-element.62), channel_id=1, source_target_pairs={{4,8},{12,16},{20,24},{28,32},{36,40},{44,48},{52,56},{60,64},{68,... | collective-permute-start | bytes 983048 | tf_op jit(solution)/shard_map/ppermute | solution.py:574
  30.3 9.0 %collective-permute-start.9 = (f32[5,8,2048]{2,1,0:T(8,128)S(1)}, f32[5,8,2048]{2,1,0:T(8,128)S(1)}, u32[]{:S(2)}, u32[]{:S(2)}) collective-permute-start(f32[5,8,2048]{2,1,0:T(8,128)S(1)} %get-tuple-element.63), channel_id=1, source_target_pairs={{0,4},{4,0},{8,12},{12,8},{16,20},{20,16},{24,28},{28,24},{32,36},... | collective-permute-start | bytes 983048 | tf_op jit(solution)/shard_map/ppermute | solution.py:575
  34.1 5.2 %collective-permute-start.10 = (f32[5,8,256]{2,1,0:T(8,128)S(1)}, f32[5,8,256]{2,1,0:T(8,128)S(1)}, u32[]{:S(2)}, u32[]{:S(2)}) collective-permute-start(f32[5,8,256]{2,1,0:T(8,128)S(1)} %get-tuple-element.64), channel_id=1, source_target_pairs={{0,1},{1,2},{2,3},{3,0},{4,5},{5,6},{6,7},{7,4},{8,9},{9,10},{10,1... | collective-permute-start | bytes 122888 | tf_op jit(solution)/shard_map/ppermute | solution.py:567
  35.2 4.1 %collective-permute-start.11 = (f32[5,8,256]{2,1,0:T(8,128)S(1)}, f32[5,8,256]{2,1,0:T(8,128)S(1)}, u32[]{:S(2)}, u32[]{:S(2)}) collective-permute-start(f32[5,8,256]{2,1,0:T(8,128)S(1)} %get-tuple-element.65), channel_id=1, source_target_pairs={{0,3},{1,0},{2,1},{3,2},{4,7},{5,4},{6,5},{7,6},{8,11},{9,8},{10,9... | collective-permute-start | bytes 122888 | tf_op jit(solution)/shard_map/ppermute | solution.py:567
  45.5 22.2 %all-to-all-start = ((f32[128,8,128]{2,1,0:T(8,128)}), f32[128,8,128]{2,1,0:T(8,128)S(1)}, u32[]{:S(2)}, u32[]{:S(2)}) async-start(f32[128,8,128]{2,1,0:T(8,128)} %shard_map.115), calls=%async_computation | async-start | bytes 1048576 | tf_op jit(solution)/shard_map/all_to_all | solution.py:600
  67.7 2.8 %copy-start.1 = (bf16[3,256,4096]{2,1,0:T(8,128)(2,1)S(1)}, bf16[3,256,4096]{2,1,0:T(8,128)(2,1)}, u32[]{:S(2)}) copy-start(bf16[3,256,4096]{2,1,0:T(8,128)(2,1)} %copy-done) | copy-start | bytes 18874372

commit v3 on v2

--- a/solution.py
+++ b/solution.py
@@ -15,7 +15,7 @@
 FIRST = (0.8, -0.2, 4.0 / 105.0, -1.0 / 280.0)
 SECOND = (8.0 / 5.0, -0.2, 8.0 / 315.0, -1.0 / 560.0)
 CENTRAL = -205.0 / 72.0
-UNROLL = (16, 16, 35, 16, 2)
+UNROLL = (16, 16, 35, 16, 2, 4)
 VMEM_LIMIT = 20 * 1024 * 1024
 WHOLE = pl.BlockSpec(memory_space=pltpu.VMEM)
 SCALAR = pl.BlockSpec(memory_space=pltpu.SMEM)
@@ -106,62 +106,125 @@
     return jnp.asarray(np.stack(result))
 
 
-def stage_kernel(stage, refs):
-    odd, along_z, far, near, before, after, rho, mom, energy = refs[:9]
-    base = state_views(*refs[9:12]) if stage else None
-    rest = refs[12:] if stage else refs[9:]
+def values_along(fields, direction):
+    r, mx, my, mz, e = fields
+    u, v, w, p, t = primitives(r, mx, my, mz, e)
+    along = (u, v, w)[direction]
+    moved = [mx * along, my * along, mz * along]
+    moved[direction] = moved[direction] + p
+    mass = (mx, my, mz)[direction]
+    return (mass, *moved, (e + p) * along, u, v, w, t, p)
+
+
+def weighted(f, k, ahead, behind):
+    if f < 5:
+        return FIRST[k - 1] * (ahead - behind)
+    return SECOND[k - 1] * (ahead + behind)
+
+
+def half_step(here, following):
+    return pltpu.roll(jnp.where(lane_ids() < NZ, following, here), NZ, 1)
+
+
+def inner_kernel(along_z, rho, mom, energy, partial, ys, yh, zs, zd):
+    state = state_views(rho, mom, energy)
+    length = rho.shape[-1]
+    blocks = length // LANES
+    edge = 2 * LANES
+
+    def fill(j):
+        both = pl.ds(pl.multiple_of(j * edge, edge), edge)
+        at = pl.ds(pl.multiple_of(j * edge + edge, edge), edge)
+        place = pl.ds(pl.multiple_of(j * 16, 16), 16)
+        fields = [s[:, both] for s in state]
+        values = values_along(fields, 1)
+        for f in range(10):
+            ys[f, :, at] = values[f]
+        u, v, w, t, p = values[5:]
+        mx, my, mz, e = fields[1:]
+        across = (mz, mx * w, my * w, mz * w + p, (e + p) * w, u, v, w, t)
+        for f, value in enumerate(across):
+            tall = jnp.concatenate([value[:, :LANES], value[:, LANES:]], 0)
+            hi = tall.astype(jnp.bfloat16)
+            zs[f, place, :LANES] = hi
+            zs[f, place, LANES:] = (tall - hi.astype(jnp.float32)).astype(jnp.bfloat16)
+
+    loop(blocks // 2, fill, UNROLL[1])
+    for f in range(9):
+        wide = jnp.dot(
+            zs[f], along_z[0 if f < 5 else 1], preferred_element_type=jnp.float32
+        )
+        zd[f] = wide[:, :LANES] + wide[:, LANES:]
+    empty = jnp.zeros((10, 8, edge), jnp.float32)
+    ys[:, :, :edge] = empty
+    ys[:, :, length + edge :] = empty
+
+    def shift_half(j):
+        for f in range(9):
+            yh[f, :, lanes_at(j)] = half_step(ys[f, :, lanes_at(j)], ys[f, :, lanes_at(j + 1)])
+
+    loop(blocks + 3, shift_half, UNROLL[2])
+
+    def add(j):
+        for f in range(9):
+            total = zd[f, pl.ds(pl.multiple_of(j * 8, 8), 8), :]
+            if f >= 5:
+                total = total + (3.0 * CENTRAL) * ys[f, :, lanes_at(j + 2)]
+            for k in range(1, 5):
+                source = yh if k % 2 else ys
+                ahead = source[f, :, lanes_at(j + 2 + k // 2)]
+                behind = source[f, :, lanes_at(j + 2 - (k + 1) // 2)]
+                total = total + weighted(f, k, ahead, behind)
+            partial[f, :, lanes_at(j)] = total
+
+    loop(blocks, add, UNROLL[5])
+
+
+def outer_kernel(stage, refs):
+    odd, partial_in, ys, far, near, before, after, rho, mom, energy = refs[:10]
+    base = state_views(*refs[10:13]) if stage else None
+    rest = refs[13:] if stage else refs[10:]
+    rho_o, mom_o, energy_o, partial = rest[:4]
     if stage < 2:
-        rho_o, mom_o, energy_o = rest[:3]
-        sends = rest[3:7]
-        ys, yh, hx, zs, zd = rest[7:]
+        sends, hx = rest[4:8], rest[8]
     else:
-        rho_o, mom_o, energy_o, newest = rest[:4]
-        ys, yh, hx, zs, zd = rest[4:]
+        newest, hx = rest[4:]
     state = state_views(rho, mom, energy)
     outs = state_views(rho_o, mom_o, energy_o)
     length = rho.shape[-1]
     blocks = length // LANES
     half = blocks // 2
-    row, lane = row_ids(), lane_ids()
+    row = row_ids()
     low = low_rows(odd)
 
-    def fill(fields, at):
-        r, mx, my, mz, e = fields
-        u, v, w, p, t = primitives(r, mx, my, mz, e)
-        for f, value in enumerate(
-            (my, mx * v, my * v + p, mz * v, (e + p) * v, u, v, w, t, p)
-        ):
-            ys[f, :, at] = value
-        return (mz, mx * w, my * w, mz * w + p, (e + p) * w, u, v, w, t)
-
-    def fill_own(j):
-        both = pl.ds(pl.multiple_of(j * 2 * LANES, 2 * LANES), 2 * LANES)
-        at = pl.ds(pl.multiple_of(j * 2 * LANES + 2 * LANES, 2 * LANES), 2 * LANES)
-        place = pl.ds(pl.multiple_of(j * 16, 16), 16)
-        for f, value in enumerate(fill([s[:, both] for s in state], at)):
-            tall = jnp.concatenate([value[:, :LANES], value[:, LANES:]], 0)
-            hi = tall.astype(jnp.bfloat16)
-            zs[f, place, :LANES] = hi
-            zs[f, place, LANES:] = (tall - hi.astype(jnp.float32)).astype(jnp.bfloat16)
-
-    loop(blocks // 2, fill_own, UNROLL[1])
+    edges = []
+    for halo in (before, after):
+        edges.append(
+            [
+                values_along([halo[f, :, i * LANES : (i + 1) * LANES] for f in range(5)], 1)
+                for i in range(2)
+            ]
+        )
+    none = jnp.zeros((8, LANES), jnp.float32)
     for f in range(9):
-        wide = jnp.dot(
-            zs[f], along_z[0 if f < 5 else 1], preferred_element_type=jnp.float32
-        )
-        zd[f] = wide[:, :LANES] + wide[:, LANES:]
-    edge = 2 * LANES
-    fill([before[f] for f in range(5)], slice(0, edge))
-    fill([after[f] for f in range(5)], slice(length + edge, length + 2 * edge))
-
-    def shift_half(j):
-        for f in range(9):
-            here, following = ys[f, :, lanes_at(j)], ys[f, :, lanes_at(j + 1)]
-            yh[f, :, lanes_at(j)] = pltpu.roll(
-                jnp.where(lane < NZ, following, here), NZ, 1
-            )
-
-    loop(blocks + 3, shift_half, UNROLL[2])
+        b0, b1 = edges[0][0][f], edges[0][1][f]
+        a0, a1 = edges[1][0][f], edges[1][1][f]
+        into, out_of = half_step(b1, none), half_step(none, a0)
+        shares = {
+            0: weighted(f, 1, none, into)
+            + weighted(f, 2, none, b1)
+            + weighted(f, 3, none, half_step(b0, b1))
+            + weighted(f, 4, none, b0),
+            1: weighted(f, 3, none, into) + weighted(f, 4, none, b1),
+            blocks - 2: weighted(f, 3, out_of, none) + weighted(f, 4, a0, none),
+            blocks - 1: weighted(f, 1, out_of, none)
+            + weighted(f, 2, a0, none)
+            + weighted(f, 3, half_step(a0, a1), none)
+            + weighted(f, 4, a1, none),
+        }
+        for j, share in shares.items():
+            at = slice(j * LANES, (j + 1) * LANES)
+            partial[f, :, at] = partial_in[f, :, at] + share
 
     def unpack(j):
         for f in range(5):
@@ -176,43 +239,15 @@
         own = [s[:, at] for s in state]
         r, mx, my, mz, e = own
         u, v, w, t, p = [ys[5 + f, :, lanes_at(j + 2)] for f in range(5)]
-        energy_p = e + p
-        hr, hmx, hmy, hmz, he = [hx[f, :, at] for f in range(5)]
-        hu, hv, hw, hp, ht = primitives(hr, hmx, hmy, hmz, he)
-        fx = (mx, mx * u + p, my * u, mz * u, energy_p * u, u, v, w, t)
-        hfx = (hmx, hmx * hu + hp, hmy * hu, hmz * hu, (he + hp) * hu, hu, hv, hw, ht)
-        here = pl.ds(pl.multiple_of(j * 8, 8), 8)
+        fx = (mx, mx * u + p, my * u, mz * u, (e + p) * u, u, v, w, t)
+        hfx = values_along([hx[f, :, at] for f in range(5)], 0)
         result = []
         for f in range(9):
-            total = zd[f, here, :]
-            if f >= 5:
-                total = total + (3.0 * CENTRAL) * fx[f]
+            total = partial[f, :, at]
             for k in range(1, 5):
-                pairs = [
-                    (
-                        pltpu.roll(jnp.where(row < k, hfx[f], fx[f]), 8 - k, 0),
-                        pltpu.roll(jnp.where(row >= 8 - k, hfx[f], fx[f]), k, 0),
-                    ),
-                ]
-                if k % 2:
-                    up, down = (k - 1) // 2, -(k + 1) // 2
-                    pairs.append(
-                        (yh[f, :, lanes_at(j + 2 + up)], yh[f, :, lanes_at(j + 2 + down)])
-                    )
-                else:
-                    pairs.append(
-                        (
-                            ys[f, :, lanes_at(j + 2 + k // 2)],
-                            ys[f, :, lanes_at(j + 2 - k // 2)],
-                        )
-                    )
-                if f < 5:
-                    s = sum(a - b for a, b in pairs)
-                    term = FIRST[k - 1] * s
-                else:
-                    s = sum(a + b for a, b in pairs)
-                    term = SECOND[k - 1] * s
-                total = total + term
+                ahead = pltpu.roll(jnp.where(row < k, hfx[f], fx[f]), 8 - k, 0)
+                behind = pltpu.roll(jnp.where(row >= 8 - k, hfx[f], fx[f]), k, 0)
+                total = total + weighted(f, k, ahead, behind)
             result.append(total)
         visc = 0.08 * t
         lap = result[5:]
@@ -292,28 +327,42 @@
     return out[:3], out[3], out[4:]
 
 
-def stage_call(stage, odd, along_z, halo, state, base):
+def inner_call(along_z, state):
     rows, length = state[0].shape
-    out = state_shapes(rows, length)
+    padded = length + 8 * NZ
+    return call(
+        inner_kernel,
+        (f32(9, rows, length), f32(10, rows, padded)),
+        (along_z, *state),
+        [
+            pltpu.VMEM((9, rows, padded), jnp.float32),
+            pltpu.VMEM((9, length // 16, 2 * LANES), jnp.bfloat16),
+            pltpu.VMEM((9, length // 16, LANES), jnp.float32),
+        ],
+        in_specs=[WHOLE] * 4,
+        out_specs=[WHOLE] * 2,
+        flops=32768 * 400,
+        nbytes=3 * 10**6,
+    )
+
+
+def outer_call(stage, odd, inner, halo, state, base):
+    rows, length = state[0].shape
+    out = state_shapes(rows, length) + (f32(9, rows, length),)
     out += send_shapes(rows, length) if stage < 2 else (f32(3, rows, length),)
-    args = (odd, along_z, *halo, *state) + (tuple(base) if stage else ())
-    scratch = [
-        pltpu.VMEM((10, rows, length + 8 * NZ), jnp.float32),
-        pltpu.VMEM((9, rows, length + 8 * NZ), jnp.float32),
-        pltpu.VMEM((5, rows, length), jnp.float32),
-        pltpu.VMEM((9, length // 16, 2 * LANES), jnp.bfloat16),
-        pltpu.VMEM((9, length // 16, LANES), jnp.float32),
-    ]
-    return call(
-        lambda *refs: stage_kernel(stage, refs),
+    args = (odd, *inner, *halo, *state) + (tuple(base) if stage else ())
+    out = call(
+        lambda *refs: outer_kernel(stage, refs),
         out,
         args,
-        scratch,
+        [pltpu.VMEM((5, rows, length), jnp.float32)],
         in_specs=[SCALAR] + [WHOLE] * (len(args) - 1),
         out_specs=[WHOLE] * len(out),
-        flops=32768 * 700,
+        input_output_aliases={1: 3},
+        flops=32768 * 400,
         nbytes=3 * 10**6,
     )
+    return out[:3], out[4:]
 
 
 def merged_rows(basis, snaps, c, at):
@@ -343,15 +392,18 @@
 GRAM_WIDTH = 1024
 
 
-def gram_kernel(basis_h, snaps_h, gram, merged, basis, snaps, total, sems):
+def gram_kernel(part, basis_h, snaps_h, gram, merged, basis, snaps, total, sems):
     width = GRAM_WIDTH
-    places = [slice(i, i + width) for i in range(0, basis_h.shape[-1], width)]
+    start = part * merged.shape[-1]
+    places = [slice(i, i + width) for i in range(0, merged.shape[-1], width)]
     loads = []
     for n, at in enumerate(places):
         for m, (source, held) in enumerate(((basis_h, basis), (snaps_h, snaps))):
             loads.append(
                 pltpu.make_async_copy(
-                    source.at[:, :, :, at], held.at[:, :, :, at], sems.at[n, m]
+                    source.at[:, :, :, start + at.start : start + at.stop],
+                    held.at[:, :, :, at],
+                    sems.at[n, m],
                 )
             )
             loads[-1].start()
@@ -373,16 +425,16 @@
     gram[...] = pack_square(small)
 
 
-def gram_call(basis, snaps):
-    length = basis.shape[-1]
+def gram_call(basis, snaps, part):
+    length = basis.shape[-1] // 2
     hbm = pl.BlockSpec(memory_space=pltpu.HBM)
     return call(
-        gram_kernel,
+        functools.partial(gram_kernel, part),
         (f32(8, LANES), pltpu.VMEM((3, 256, length), jnp.bfloat16)),
         in_hbm(basis, snaps),
         [
-            pltpu.VMEM(basis.shape, jnp.bfloat16),
-            pltpu.VMEM(snaps.shape, jnp.bfloat16),
+            pltpu.VMEM((*basis.shape[:-1], length), jnp.bfloat16),
+            pltpu.VMEM((*snaps.shape[:-1], length), jnp.bfloat16),
             pltpu.VMEM((256, 256), jnp.float32),
             pltpu.SemaphoreType.DMA((length // GRAM_WIDTH, 2)),
         ],
@@ -393,15 +445,19 @@
     )
 
 
-def cross_kernel(merged, newest, gram, parts, total):
+def cross_kernel(merged_a, merged_b, newest, gram_a, gram_b, parts, total):
     blocks = newest.shape[-1] // LANES
+    half = blocks // 2
 
     def add(i):
         pair = pl.ds(pl.multiple_of(i * 16, 16), 16)
         sums = [jnp.zeros((2, 8, LANES), jnp.float32) for _ in range(4)]
         for n in range(3 * blocks):
             c, at = n % 3, slice(n // 3 * LANES, (n // 3 + 1) * LANES)
-            rows = merged[c, pair, at].astype(jnp.float32).reshape(2, 8, LANES)
+            merged = merged_a if n // 3 < half else merged_b
+            first = n // 3 % half * LANES
+            rows = merged[c, pair, first : first + LANES]
+            rows = rows.astype(jnp.float32).reshape(2, 8, LANES)
             sums[n % 4] = sums[n % 4] + rows * newest[c, :, at]
         total[pl.ds(i * 2, 2)] = (sums[0] + sums[1]) + (sums[2] + sums[3])
 
@@ -420,17 +476,17 @@
     )
     line = jnp.concatenate([jnp.zeros((8, 96), jnp.float32), line], 1)
     last = (row_ids() == 7) & (lane_ids() >= 96)
-    parts[...] = jnp.broadcast_to(jnp.where(last, line, gram[...])[None], parts.shape)
-
-
-def cross_call(merged, newest, gram, copies):
+    parts[...] = jnp.where(last, line, gram_a[...] + gram_b[...])
+
+
+def cross_call(merged, newest, grams):
     length = newest.shape[-1]
     return call(
         cross_kernel,
-        f32(copies, 8, LANES),
-        (merged, newest, gram),
+        f32(8, LANES),
+        (*merged, newest, *grams),
         [pltpu.VMEM((32, 8, LANES), jnp.float32)],
-        in_specs=[WHOLE] * 3,
+        in_specs=[WHOLE] * 5,
         out_specs=WHOLE,
         flops=31 * 6 * 8 * length,
         nbytes=31 * 3 * 8 * length * 2,
@@ -498,32 +554,39 @@
         out[...] = jnp.where(keep, wide, 0.0).astype(jnp.bfloat16)
 
 
-MODES_WIDTH = 2048
-
-
 def modes_kernel(
     weight,
     parts,
     scale,
-    merged,
+    merged_a,
+    merged_b,
     newest,
     modes,
     factor,
+    merged,
     out,
     high,
     low,
     diagonal,
+    in_sems,
     out_sems,
 ):
-    width = MODES_WIDTH
-    pieces = []
-    for i in range(newest.shape[-1] // width):
-        for c in range(3):
-            pieces.append((len(pieces), c, slice(i * width, (i + 1) * width)))
+    width = newest.shape[-1] // 2
+    pieces = [(3 * i + c, i, c) for i in range(2) for c in range(3)]
+    loads = [
+        pltpu.make_async_copy((merged_a, merged_b)[i].at[c], merged.at[n], in_sems.at[n])
+        for n, i, c in pieces
+    ]
+    for load in loads[:3]:
+        load.start()
     weights_of(weight, parts, scale, factor, high, low, diagonal)
+    for load in loads[3:]:
+        load.start()
     stores = []
-    for n, c, at in pieces:
-        rows = merged[c, :, at]
+    for n, i, c in pieces:
+        loads[n].wait()
+        at = slice(i * width, (i + 1) * width)
+        rows = merged[n]
         value = jnp.dot(high[...], rows, preferred_element_type=jnp.float32)
         value = value + jnp.dot(low[...], rows, preferred_element_type=jnp.float32)
         value = value.reshape(32, 8, width)
@@ -541,21 +604,23 @@
 
 def modes_call(parts, scale, merged, newest, weight):
     length = newest.shape[-1]
-    count = 3 * length // MODES_WIDTH
     shape = (32, 3, 8, length)
+    hbm = pl.BlockSpec(memory_space=pltpu.HBM)
     return call(
         functools.partial(modes_kernel, weight),
         (jax.ShapeDtypeStruct(shape, jnp.bfloat16), f32(32, 32)),
-        (parts, scale, merged, newest),
+        (parts, scale, *in_hbm(*merged), newest),
         [
+            pltpu.VMEM((6, 256, length // 2), jnp.bfloat16),
             pltpu.VMEM(shape, jnp.bfloat16),
             pltpu.VMEM((256, 256), jnp.bfloat16),
             pltpu.VMEM((256, 256), jnp.bfloat16),
             pltpu.VMEM((8, LANES), jnp.float32),
-            pltpu.SemaphoreType.DMA((count,)),
+            pltpu.SemaphoreType.DMA((6,)),
+            pltpu.SemaphoreType.DMA((6,)),
         ],
-        in_specs=[WHOLE] * 4,
-        out_specs=[pl.BlockSpec(memory_space=pltpu.HBM), WHOLE],
+        in_specs=[WHOLE, WHOLE, hbm, hbm, WHOLE],
+        out_specs=[hbm, WHOLE],
         flops=4 * 256 * 256 * 3 * length,
         nbytes=63 * 3 * 8 * length * 2,
     )
@@ -578,6 +643,18 @@
     return (far, near, before, after)
 
 
+def total_parts(part):
+    count, other = lax.axis_size("gx"), lax.axis_size("gy")
+    part = part + lax.ppermute(part, "gx", [(i, i ^ 1) for i in range(count)])
+    groups = [
+        [i for i in range(count * other) if i // other % 2 == core] for core in range(2)
+    ]
+    copies = jnp.broadcast_to(part[None], (count * other // 2, *part.shape))
+    return lax.all_to_all(
+        copies, ("gx", "gy"), 0, 0, tiled=True, axis_index_groups=groups
+    )
+
+
 def local(density, momentum, energy, basis, scales, snapshots):
     rows, length = density.shape
     devices = lax.axis_size("gx") * lax.axis_size("gy")
@@ -587,17 +664,17 @@
 
     odd = (lax.axis_index("gx") % 2).astype(jnp.int32)[None]
     fields, along_z, sends = pack(odd, fields)
-    halo = exchange(sends)
-    gram, merged = gram_call(basis, snapshots)
-    halo, gram, merged = lax.optimization_barrier((halo, gram, merged))
-    first = stage_call(0, odd, along_z, halo, fields, None)
-    halo = exchange(first[3:])
-    second = stage_call(1, odd, along_z, halo, first[:3], fields)
-    halo = exchange(second[3:])
-    final = stage_call(2, odd, along_z, halo, second[:3], fields)
-    newest = final[3]
-    parts = cross_call(merged, newest, gram, devices)
-    parts = lax.all_to_all(parts, ("gx", "gy"), 0, 0, tiled=True)
+    halo, inner = exchange(sends), inner_call(along_z, fields)
+    state, sends = outer_call(0, odd, inner, halo, fields, None)
+    old = []
+    for stage in (1, 2):
+        halo, inner = exchange(sends), inner_call(along_z, state)
+        old.append(gram_call(basis, snapshots, stage - 1))
+        halo, inner, old = lax.optimization_barrier((halo, inner, old))
+        state, sends = outer_call(stage, odd, inner, halo, state, fields)
+    final, (newest,) = state, sends
+    grams, merged = zip(*old)
+    parts = total_parts(cross_call(merged, newest, grams))
     modes, factor = modes_call(parts, scale, merged, newest, weight)
     return (final[0], final[1], final[2], modes, factor)
 

time: 77.5 us -> 72.4 us (0.934)
  waiting for transfers between devices: 18.3 us -> 10.8 us
  Pallas kernels: 25.3 us -> 30 us
  local copies, waits for them, and re-layouts: 2.8 us -> 0.74 us
    pallas_call x7 -> x11, Pallas kernels: 25.3 us -> 30 us  [call(): pl.pallas_call(kernel, out_shape=out_shape, scratch_shapes=list(scratch),...]
    all_to_all x1, waiting for transfers between devices: 13.7 us -> 9.73 us  [total_parts(): lax.all_to_all(copies, ('gx', 'gy'), 0, 0, tiled=True, axis_index_groups=...]
    ppermute x6, waiting for transfers between devices: 3.88 us -> 0.21 us  [shifted(): return lax.ppermute(block, axis, route)]
    unnamed x6, local copies, waits for them, and re-layouts: 2.79 us -> 0.01 us
    all_to_all x1, starting transfers between devices: 8.46 us -> 6.78 us  [total_parts(): lax.all_to_all(copies, ('gx', 'gy'), 0, 0, tiled=True, axis_index_groups=...]
    ppermute x6, starting transfers between devices: 10.2 us -> 11.3 us  [shifted(): return lax.ppermute(block, axis, route)]
    ppermute x0 -> x1, waiting for transfers between devices: none -> 0.88 us  [total_parts(): part = part + lax.ppermute(part, 'gx', [(i, i ^ 1) for i in range(count)])]
  transfers between devices with their start and end apart: 13 -> 14, of which waited for: 4 -> 3; matrix products, arithmetic and copies ran while one was open for 0% -> 0% of each run, Pallas kernels for 7% -> 18%
where the time goes in v3:
time: 72.4 us; the launch traced here: 72 us
  Pallas kernels  30 us (41%)
  starting transfers between devices  29.4 us (41%)
  waiting for transfers between devices  10.8 us (15%)
  between operations  1 us (1%)
  local copies, waits for them, and re-layouts  0.74 us (1%)
    pallas_call x11, Pallas kernels, call(): pl.pallas_call(kernel, out_shape=out_shape, scratch_shapes=list(scratch),...  30 us
    ppermute x6, starting transfers between devices, shifted(): return lax.ppermute(block, axis, route)  11.3 us
    all_to_all x1, waiting for transfers between devices, total_parts(): lax.all_to_all(copies, ('gx', 'gy'), 0, 0, tiled=True, axis_index_groups=...  9.73 us
    ppermute x3, starting transfers between devices, exchange(): near = lax.ppermute(to_near, 'gx', [(i, i ^ 1) for i in range(count)])  8.17 us
    all_to_all x1, starting transfers between devices, total_parts(): lax.all_to_all(copies, ('gx', 'gy'), 0, 0, tiled=True, axis_index_groups=...  6.78 us
    ppermute x3, starting transfers between devices, exchange(): far = lax.ppermute(to_far, 'gx', pairs + [(j, i) for i, j in pairs])  2.85 us
  transfers between devices with their start and end apart: 14, of which 3 were waited for; matrix products, arithmetic and copies ran while one was open for 0% of the time, Pallas kernels for 18%

profile of v3, /device:TPU:1, one launch (start us, length us, event | category | flops | bytes accessed | tf_op | source)
XLA Modules:
  0.0 72.0 jit_solution(16303978405104148326)
XLA Ops:
  0.6 1.3 %shard_map.110 = (f32[8,4096]{1,0:T(8,128)S(1)}, f32[3,8,4096]{2,1,0:T(8,128)S(1)}, f32[8,4096]{1,0:T(8,128)S(1)}, bf16[2,256,256]{2,1,0:T(8,128)(2,1)S(1)}, f32...) custom-call(s32[1]{0:T(128)} %bitcast.odd.refs_0_, ...), custom_call_target="tpu_custom_call" | custom-call | bytes 1000000 | tf_op jit(solution)/shard_map/pallas_call | solution.py:286
  1.9 2.7 %collective-permute-start = (f32[5,8,2048]{2,1,0:T(8,128)S(1)}, f32[5,8,2048]{2,1,0:T(8,128)S(1)}, u32[]{:S(2)}, u32[]{:S(2)}) collective-permute-start(f32[5,8,2048]{2,1,0:T(8,128)S(1)} %get-tuple-element.67), channel_id=1, source_target_pairs={{4,8},{12,16},{20,24},{28,32},{36,40},{44,48},{52,56},{60,64},{68,... | collective-permute-start | bytes 983048 | tf_op jit(solution)/shard_map/ppermute | solution.py:639
  4.6 3.6 %collective-permute-start.1 = (f32[5,8,2048]{2,1,0:T(8,128)S(1)}, f32[5,8,2048]{2,1,0:T(8,128)S(1)}, u32[]{:S(2)}, u32[]{:S(2)}) collective-permute-start(f32[5,8,2048]{2,1,0:T(8,128)S(1)} %get-tuple-element.68), channel_id=1, source_target_pairs={{0,4},{4,0},{8,12},{12,8},{16,20},{20,16},{24,28},{28,24},{32,36},... | collective-permute-start | bytes 983048 | tf_op jit(solution)/shard_map/ppermute | solution.py:640
  8.2 1.6 %collective-permute-start.2 = (f32[5,8,256]{2,1,0:T(8,128)S(1)}, f32[5,8,256]{2,1,0:T(8,128)S(1)}, u32[]{:S(2)}, u32[]{:S(2)}) collective-permute-start(f32[5,8,256]{2,1,0:T(8,128)S(1)} %get-tuple-element.69), channel_id=1, source_target_pairs={{0,1},{1,2},{2,3},{3,0},{4,5},{5,6},{6,7},{7,4},{8,9},{9,10},{10,1... | collective-permute-start | bytes 122888 | tf_op jit(solution)/shard_map/ppermute | solution.py:632
  9.8 2.1 %collective-permute-start.3 = (f32[5,8,256]{2,1,0:T(8,128)S(1)}, f32[5,8,256]{2,1,0:T(8,128)S(1)}, u32[]{:S(2)}, u32[]{:S(2)}) collective-permute-start(f32[5,8,256]{2,1,0:T(8,128)S(1)} %get-tuple-element.70), channel_id=1, source_target_pairs={{0,3},{1,0},{2,1},{3,2},{4,7},{5,4},{6,5},{7,6},{8,11},{9,8},{10,9... | collective-permute-start | bytes 122888 | tf_op jit(solution)/shard_map/ppermute | solution.py:632
  11.9 1.7 %shard_map.111 = (f32[9,8,4096]{2,1,0:T(8,128)S(1)}, f32[10,8,4608]{2,1,0:T(8,128)S(1)}) custom-call(bf16[2,256,256]{2,1,0:T(8,128)(2,1)S(1)} %get-tuple-element.61.along_z, f32[8,4096]{1,0:T(8,128)S(1)} %get-tuple-element.62.rho.refs_7_.refs_10_, f32[3,8,4096]{2,1,0:T(8,128)S(1)} %get-tuple-element.63.mom.refs_8_.refs_11_, ...), custom_call_target="tpu_custom_call" | custom-call | flops 13107200 | bytes 3000000 | tf_op jit(solution)/shard_map/pallas_call | solution.py:286
  13.9 1.7 %shard_map.112 = (f32[8,4096]{1,0:T(8,128)S(1)}, f32[3,8,4096]{2,1,0:T(8,128)S(1)}, f32[8,4096]{1,0:T(8,128)S(1)}, f32[9,8,4096]{2,1,0:T(8,128)S(1)}, f32[5,8,20...) custom-call(s32[1]{0:T(128)} %bitcast.odd.refs_0_, ...), custom_call_target="tpu_custom_call", output_to_operand_aliasing={{3}: (1, {})} | custom-call | flops 13107200 | bytes 3000000 | tf_op jit(solution)/shard_map/pallas_call | solution.py:286
  15.7 4.1 %collective-permute-start.5 = (f32[5,8,2048]{2,1,0:T(8,128)S(1)}, f32[5,8,2048]{2,1,0:T(8,128)S(1)}, u32[]{:S(2)}, u32[]{:S(2)}) collective-permute-start(f32[5,8,2048]{2,1,0:T(8,128)S(1)} %get-tuple-element.72), channel_id=1, source_target_pairs={{0,4},{4,0},{8,12},{12,8},{16,20},{20,16},{24,28},{28,24},{32,36},... | collective-permute-start | bytes 983048 | tf_op jit(solution)/shard_map/ppermute | solution.py:640
  19.8 1.6 %collective-permute-start.6 = (f32[5,8,256]{2,1,0:T(8,128)S(1)}, f32[5,8,256]{2,1,0:T(8,128)S(1)}, u32[]{:S(2)}, u32[]{:S(2)}) collective-permute-start(f32[5,8,256]{2,1,0:T(8,128)S(1)} %get-tuple-element.73), channel_id=1, source_target_pairs={{0,1},{1,2},{2,3},{3,0},{4,5},{5,6},{6,7},{7,4},{8,9},{9,10},{10,1... | collective-permute-start | bytes 122888 | tf_op jit(solution)/shard_map/ppermute | solution.py:632
  21.4 2.1 %collective-permute-start.7 = (f32[5,8,256]{2,1,0:T(8,128)S(1)}, f32[5,8,256]{2,1,0:T(8,128)S(1)}, u32[]{:S(2)}, u32[]{:S(2)}) collective-permute-start(f32[5,8,256]{2,1,0:T(8,128)S(1)} %get-tuple-element.74), channel_id=1, source_target_pairs={{0,3},{1,0},{2,1},{3,2},{4,7},{5,4},{6,5},{7,6},{8,11},{9,8},{10,9... | collective-permute-start | bytes 122888 | tf_op jit(solution)/shard_map/ppermute | solution.py:632
  23.6 3.7 %shard_map.114 = (f32[8,128]{1,0:T(8,128)S(1)}, bf16[3,256,2048]{2,1,0:T(8,128)(2,1)S(1)}) custom-call(bf16[16,3,8,4096]{3,2,1,0:T(8,128)(2,1)} %basis_h.3, bf16[15,3,8,4096]{3,2,1,0:T(8,128)(2,1)} %snaps_h.3), custom_call_target="tpu_custom_call" | custom-call | flops 805306368 | bytes 3047424 | tf_op jit(solution)/shard_map/pallas_call | solution.py:286
  27.3 1.7 %shard_map.113 = (f32[9,8,4096]{2,1,0:T(8,128)S(1)}, f32[10,8,4608]{2,1,0:T(8,128)S(1)}) custom-call(bf16[2,256,256]{2,1,0:T(8,128)(2,1)S(1)} %get-tuple-element.61.along_z, f32[8,4096]{1,0:T(8,128)S(1)} %get-tuple-element.75.rho.refs_7_, f32[3,8,4096]{2,1,0:T(8,128)S(1)} %get-tuple-element.76.mom.refs_8_, f32[8,4096]{1,0:T(8,128)S(1)} %get-tuple-element.77.energy.refs_9_), custom_call_target="tpu_custom_call" | custom-call | flops 13107200 | bytes 3000000 | tf_op jit(solution)/shard_map/pallas_call | solution.py:286
  29.1 1.8 %shard_map.115 = (f32[8,4096]{1,0:T(8,128)S(1)}, f32[3,8,4096]{2,1,0:T(8,128)S(1)}, f32[8,4096]{1,0:T(8,128)S(1)}, f32[9,8,4096]{2,1,0:T(8,128)S(1)}, f32[5,8,20...) custom-call(s32[1]{0:T(128)} %bitcast.odd.refs_0_, ...), custom_call_target="tpu_custom_call", output_to_operand_aliasing={{3}: (1, {})} | custom-call | flops 13107200 | bytes 3000000 | tf_op jit(solution)/shard_map/pallas_call | solution.py:286
  31.5 1.6 %collective-permute-start.10 = (f32[5,8,256]{2,1,0:T(8,128)S(1)}, f32[5,8,256]{2,1,0:T(8,128)S(1)}, u32[]{:S(2)}, u32[]{:S(2)}) collective-permute-start(f32[5,8,256]{2,1,0:T(8,128)S(1)} %get-tuple-element.90), channel_id=1, source_target_pairs={{0,1},{1,2},{2,3},{3,0},{4,5},{5,6},{6,7},{7,4},{8,9},{9,10},{10,1... | collective-permute-start | bytes 122888 | tf_op jit(solution)/shard_map/ppermute | solution.py:632
  33.2 2.1 %collective-permute-start.11 = (f32[5,8,256]{2,1,0:T(8,128)S(1)}, f32[5,8,256]{2,1,0:T(8,128)S(1)}, u32[]{:S(2)}, u32[]{:S(2)}) collective-permute-start(f32[5,8,256]{2,1,0:T(8,128)S(1)} %get-tuple-element.91), channel_id=1, source_target_pairs={{0,3},{1,0},{2,1},{3,2},{4,7},{5,4},{6,5},{7,6},{8,11},{9,8},{10,9... | collective-permute-start | bytes 122888 | tf_op jit(solution)/shard_map/ppermute | solution.py:632
  35.3 3.7 %shard_map.117 = (f32[8,128]{1,0:T(8,128)S(1)}, bf16[3,256,2048]{2,1,0:T(8,128)(2,1)S(1)}) custom-call(bf16[16,3,8,4096]{3,2,1,0:T(8,128)(2,1)} %basis_h.3, bf16[15,3,8,4096]{3,2,1,0:T(8,128)(2,1)} %snaps_h.3), custom_call_target="tpu_custom_call" | custom-call | flops 805306368 | bytes 3047424 | tf_op jit(solution)/shard_map/pallas_call | solution.py:286
  39.1 1.7 %shard_map.116 = (f32[9,8,4096]{2,1,0:T(8,128)S(1)}, f32[10,8,4608]{2,1,0:T(8,128)S(1)}) custom-call(bf16[2,256,256]{2,1,0:T(8,128)(2,1)S(1)} %get-tuple-element.61.along_z, f32[8,4096]{1,0:T(8,128)S(1)} %get-tuple-element.92.rho.refs_7_, f32[3,8,4096]{2,1,0:T(8,128)S(1)} %get-tuple-element.93.mom.refs_8_, f32[8,4096]{1,0:T(8,128)S(1)} %get-tuple-element.94.energy.refs_9_), custom_call_target="tpu_custom_call" | custom-call | flops 13107200 | bytes 3000000 | tf_op jit(solution)/shard_map/pallas_call | solution.py:286
  40.8 2.6 %shard_map.118 = (f32[8,4096]{1,0:T(8,128)}, f32[3,8,4096]{2,1,0:T(8,128)}, f32[8,4096]{1,0:T(8,128)}, f32[9,8,4096]{2,1,0:T(8,128)S(1)}, f32[3,8,4096]{2,1,0:T(8,128)S(1)}) custom-call(s32[1]{0:T(128)} %bitcast.odd.refs_0_, f32[9,8,4096]{2,1,0:T(8,128)S(1)} %get-tuple-element.101.refs_1_, ...), custom_call_target="tpu_custom_call", output_to_operand_aliasing={{3}: (1, {})} | custom-call | flops 13107200 | bytes 3000000 | tf_op jit(solution)/shard_map/pallas_call | solution.py:286
  43.4 1.8 %shard_map.119 = f32[8,128]{1,0:T(8,128)S(1)} custom-call(bf16[3,256,2048]{2,1,0:T(8,128)(2,1)S(1)} %get-tuple-element.110.merged_a, bf16[3,256,2048]{2,1,0:T(8,128)(2,1)S(1)} %get-tuple-element.111.merged_b, f32[3,8,4096]{2,1,0:T(8,128)S(1)} %get-tuple-element.112.newest, f32[8,128]{1,0:T(8,128)S(1)} %get-tuple-element.113.gram_a, ...), custom_call_target="tpu_custom_call" | custom-call | flops 6094848 | bytes 6094848 | tf_op jit(solution)/shard_map/pallas_call | solution.py:286
  45.5 0.9 %collective-permute-done.12 = f32[8,128]{1,0:T(8,128)S(1)} collective-permute-done((f32[8,128]{1,0:T(8,128)S(1)}, f32[8,128]{1,0:T(8,128)S(1)}, u32[]{:S(2)}, u32[]{:S(2)}) %collective-permute-start.12) | collective-permute-done | bytes 4128 | tf_op jit(solution)/shard_map/ppermute | solution.py:648
  46.4 0.7 %broadcast_in_dim.13 = f32[64,8,128]{2,1,0:T(8,128)} broadcast(f32[8,128]{1,0:T(8,128)S(1)} %add.10), dimensions={1,2} | broadcast | bytes 266240 | tf_op jit(solution)/shard_map/broadcast_in_dim | solution.py:652
  47.1 6.8 %all-to-all-start = ((f32[64,8,128]{2,1,0:T(8,128)}), f32[64,8,128]{2,1,0:T(8,128)S(1)}, u32[]{:S(2)}, u32[]{:S(2)}) async-start(f32[64,8,128]{2,1,0:T(8,128)} %broadcast_in_dim.13), calls=%async_computation | async-start | bytes 524288 | tf_op jit(solution)/shard_map/all_to_all | solution.py:653
  53.9 9.7 %all-to-all-done.parts = f32[64,8,128]{2,1,0:T(8,128)S(1)} async-done(((f32[64,8,128]{2,1,0:T(8,128)}), f32[64,8,128]{2,1,0:T(8,128)S(1)}, u32[]{:S(2)}, u32[]{:S(2)}) %all-to-all-start) | async-done | bytes 262176 | tf_op jit(solution)/shard_map/all_to_all | solution.py:653
  63.6 8.2 %shard_map.120 = (bf16[32,3,8,4096]{3,2,1,0:T(8,128)(2,1)}, f32[32,32]{1,0:T(8,128)}) custom-call(f32[64,8,128]{2,1,0:T(8,128)S(1)} %all-to-all-done.parts, f32[1,32]{1,0:T(1,128)S(1)} %pad_bitcast_fusion.scale, bf16[3,256,2048]{2,1,0:T(8,128)(2,1)} %copy-done, bf16[3,256,2048]{2,1,0:T(8,128)(2,1)} %copy-done.1, f32[3,8,4096]{2,1,0:T(8,128)S(1)} %get-tuple-element.112.newest), custom_call_target="tpu_custom_call" | custom-call | flops 3221225472 | bytes 12386304 | tf_op jit(solution)/shard_map/pallas_call | solution.py:286
  (24 shorter events, 1.2 us)
Async XLA Ops:
  1.9 11.9 %collective-permute-start = (f32[5,8,2048]{2,1,0:T(8,128)S(1)}, f32[5,8,2048]{2,1,0:T(8,128)S(1)}, u32[]{:S(2)}, u32[]{:S(2)}) collective-permute-start(f32[5,8,2048]{2,1,0:T(8,128)S(1)} %get-tuple-element.67), channel_id=1, source_target_pairs={{4,8},{12,16},{20,24},{28,32},{36,40},{44,48},{52,56},{60,64},{68,... | collective-permute-start | bytes 983048 | tf_op jit(solution)/shard_map/ppermute | solution.py:639
  4.6 9.3 %collective-permute-start.1 = (f32[5,8,2048]{2,1,0:T(8,128)S(1)}, f32[5,8,2048]{2,1,0:T(8,128)S(1)}, u32[]{:S(2)}, u32[]{:S(2)}) collective-permute-start(f32[5,8,2048]{2,1,0:T(8,128)S(1)} %get-tuple-element.68), channel_id=1, source_target_pairs={{0,4},{4,0},{8,12},{12,8},{16,20},{20,16},{24,28},{28,24},{32,36},... | collective-permute-start | bytes 983048 | tf_op jit(solution)/shard_map/ppermute | solution.py:640
  8.2 5.7 %collective-permute-start.2 = (f32[5,8,256]{2,1,0:T(8,128)S(1)}, f32[5,8,256]{2,1,0:T(8,128)S(1)}, u32[]{:S(2)}, u32[]{:S(2)}) collective-permute-start(f32[5,8,256]{2,1,0:T(8,128)S(1)} %get-tuple-element.69), channel_id=1, source_target_pairs={{0,1},{1,2},{2,3},{3,0},{4,5},{5,6},{6,7},{7,4},{8,9},{9,10},{10,1... | collective-permute-start | bytes 122888 | tf_op jit(solution)/shard_map/ppermute | solution.py:632
  9.8 4.1 %collective-permute-start.3 = (f32[5,8,256]{2,1,0:T(8,128)S(1)}, f32[5,8,256]{2,1,0:T(8,128)S(1)}, u32[]{:S(2)}, u32[]{:S(2)}) collective-permute-start(f32[5,8,256]{2,1,0:T(8,128)S(1)} %get-tuple-element.70), channel_id=1, source_target_pairs={{0,3},{1,0},{2,1},{3,2},{4,7},{5,4},{6,5},{7,6},{8,11},{9,8},{10,9... | collective-permute-start | bytes 122888 | tf_op jit(solution)/shard_map/ppermute | solution.py:632
  15.6 13.5 %collective-permute-start.4 = (f32[5,8,2048]{2,1,0:T(8,128)S(1)}, f32[5,8,2048]{2,1,0:T(8,128)S(1)}, u32[]{:S(2)}, u32[]{:S(2)}) collective-permute-start(f32[5,8,2048]{2,1,0:T(8,128)S(1)} %get-tuple-element.71), channel_id=1, source_target_pairs={{4,8},{12,16},{20,24},{28,32},{36,40},{44,48},{52,56},{60,64},{68,... | collective-permute-start | bytes 983048 | tf_op jit(solution)/shard_map/ppermute | solution.py:639
  15.7 13.4 %collective-permute-start.5 = (f32[5,8,2048]{2,1,0:T(8,128)S(1)}, f32[5,8,2048]{2,1,0:T(8,128)S(1)}, u32[]{:S(2)}, u32[]{:S(2)}) collective-permute-start(f32[5,8,2048]{2,1,0:T(8,128)S(1)} %get-tuple-element.72), channel_id=1, source_target_pairs={{0,4},{4,0},{8,12},{12,8},{16,20},{20,16},{24,28},{28,24},{32,36},... | collective-permute-start | bytes 983048 | tf_op jit(solution)/shard_map/ppermute | solution.py:640
  19.8 9.2 %collective-permute-start.6 = (f32[5,8,256]{2,1,0:T(8,128)S(1)}, f32[5,8,256]{2,1,0:T(8,128)S(1)}, u32[]{:S(2)}, u32[]{:S(2)}) collective-permute-start(f32[5,8,256]{2,1,0:T(8,128)S(1)} %get-tuple-element.73), channel_id=1, source_target_pairs={{0,1},{1,2},{2,3},{3,0},{4,5},{5,6},{6,7},{7,4},{8,9},{9,10},{10,1... | collective-permute-start | bytes 122888 | tf_op jit(solution)/shard_map/ppermute | solution.py:632
  21.4 7.6 %collective-permute-start.7 = (f32[5,8,256]{2,1,0:T(8,128)S(1)}, f32[5,8,256]{2,1,0:T(8,128)S(1)}, u32[]{:S(2)}, u32[]{:S(2)}) collective-permute-start(f32[5,8,256]{2,1,0:T(8,128)S(1)} %get-tuple-element.74), channel_id=1, source_target_pairs={{0,3},{1,0},{2,1},{3,2},{4,7},{5,4},{6,5},{7,6},{8,11},{9,8},{10,9... | collective-permute-start | bytes 122888 | tf_op jit(solution)/shard_map/ppermute | solution.py:632
  27.3 16.1 %copy-start = (bf16[3,256,2048]{2,1,0:T(8,128)(2,1)}, bf16[3,256,2048]{2,1,0:T(8,128)(2,1)S(1)}, u32[]{:S(2)}) copy-start(bf16[3,256,2048]{2,1,0:T(8,128)(2,1)S(1)} %get-tuple-element.110.merged_a) | copy-start | bytes 9437188
  30.9 9.9 %collective-permute-start.8 = (f32[5,8,2048]{2,1,0:T(8,128)S(1)}, f32[5,8,2048]{2,1,0:T(8,128)S(1)}, u32[]{:S(2)}, u32[]{:S(2)}) collective-permute-start(f32[5,8,2048]{2,1,0:T(8,128)S(1)} %get-tuple-element.88), channel_id=1, source_target_pairs={{4,8},{12,16},{20,24},{28,32},{36,40},{44,48},{52,56},{60,64},{68,... | collective-permute-start | bytes 983048 | tf_op jit(solution)/shard_map/ppermute | solution.py:639
  31.0 9.8 %collective-permute-start.9 = (f32[5,8,2048]{2,1,0:T(8,128)S(1)}, f32[5,8,2048]{2,1,0:T(8,128)S(1)}, u32[]{:S(2)}, u32[]{:S(2)}) collective-permute-start(f32[5,8,2048]{2,1,0:T(8,128)S(1)} %get-tuple-element.89), channel_id=1, source_target_pairs={{0,4},{4,0},{8,12},{12,8},{16,20},{20,16},{24,28},{28,24},{32,36},... | collective-permute-start | bytes 983048 | tf_op jit(solution)/shard_map/ppermute | solution.py:640
  31.5 9.2 %collective-permute-start.10 = (f32[5,8,256]{2,1,0:T(8,128)S(1)}, f32[5,8,256]{2,1,0:T(8,128)S(1)}, u32[]{:S(2)}, u32[]{:S(2)}) collective-permute-start(f32[5,8,256]{2,1,0:T(8,128)S(1)} %get-tuple-element.90), channel_id=1, source_target_pairs={{0,1},{1,2},{2,3},{3,0},{4,5},{5,6},{6,7},{7,4},{8,9},{9,10},{10,1... | collective-permute-start | bytes 122888 | tf_op jit(solution)/shard_map/ppermute | solution.py:632
  33.2 7.6 %collective-permute-start.11 = (f32[5,8,256]{2,1,0:T(8,128)S(1)}, f32[5,8,256]{2,1,0:T(8,128)S(1)}, u32[]{:S(2)}, u32[]{:S(2)}) collective-permute-start(f32[5,8,256]{2,1,0:T(8,128)S(1)} %get-tuple-element.91), channel_id=1, source_target_pairs={{0,3},{1,0},{2,1},{3,2},{4,7},{5,4},{6,5},{7,6},{8,11},{9,8},{10,9... | collective-permute-start | bytes 122888 | tf_op jit(solution)/shard_map/ppermute | solution.py:632
  39.0 4.4 %copy-start.1 = (bf16[3,256,2048]{2,1,0:T(8,128)(2,1)}, bf16[3,256,2048]{2,1,0:T(8,128)(2,1)S(1)}, u32[]{:S(2)}) copy-start(bf16[3,256,2048]{2,1,0:T(8,128)(2,1)S(1)} %get-tuple-element.111.merged_b) | copy-start | bytes 9437188
  43.4 10.5 %copy-start.2 = (f32[16]{0:T(128)S(1)}, f32[16]{0:T(128)}, u32[]{:S(2)}) copy-start(f32[16]{0:T(128)} %param.11) | copy-start | bytes 196
  45.2 1.2 %collective-permute-start.12 = (f32[8,128]{1,0:T(8,128)S(1)}, f32[8,128]{1,0:T(8,128)S(1)}, u32[]{:S(2)}, u32[]{:S(2)}) collective-permute-start(f32[8,128]{1,0:T(8,128)S(1)} %shard_map.119), channel_id=1, source_target_pairs={{0,4},{4,0},{8,12},{12,8},{16,20},{20,16},{24,28},{28,24},{32,36},... | collective-permute-start | bytes 12296 | tf_op jit(solution)/shard_map/ppermute | solution.py:648
  47.1 16.5 %all-to-all-start = ((f32[64,8,128]{2,1,0:T(8,128)}), f32[64,8,128]{2,1,0:T(8,128)S(1)}, u32[]{:S(2)}, u32[]{:S(2)}) async-start(f32[64,8,128]{2,1,0:T(8,128)} %broadcast_in_dim.13), calls=%async_computation | async-start | bytes 524288 | tf_op jit(solution)/shard_map/all_to_all | solution.py:653

commit v4 on v3

--- a/solution.py
+++ b/solution.py
@@ -15,7 +15,7 @@
 FIRST = (0.8, -0.2, 4.0 / 105.0, -1.0 / 280.0)
 SECOND = (8.0 / 5.0, -0.2, 8.0 / 315.0, -1.0 / 560.0)
 CENTRAL = -205.0 / 72.0
-UNROLL = (16, 16, 35, 16, 2, 4)
+UNROLL = (16, 16, 35, 16, 8, 16)
 VMEM_LIMIT = 20 * 1024 * 1024
 WHOLE = pl.BlockSpec(memory_space=pltpu.VMEM)
 SCALAR = pl.BlockSpec(memory_space=pltpu.SMEM)
@@ -554,6 +554,9 @@
         out[...] = jnp.where(keep, wide, 0.0).astype(jnp.bfloat16)
 
 
+EARLY = 6
+
+
 def modes_kernel(
     weight,
     parts,
@@ -577,10 +580,10 @@
         pltpu.make_async_copy((merged_a, merged_b)[i].at[c], merged.at[n], in_sems.at[n])
         for n, i, c in pieces
     ]
-    for load in loads[:3]:
+    for load in loads[:EARLY]:
         load.start()
     weights_of(weight, parts, scale, factor, high, low, diagonal)
-    for load in loads[3:]:
+    for load in loads[EARLY:]:
         load.start()
     stores = []
     for n, i, c in pieces:
@@ -664,13 +667,12 @@
 
     odd = (lax.axis_index("gx") % 2).astype(jnp.int32)[None]
     fields, along_z, sends = pack(odd, fields)
-    halo, inner = exchange(sends), inner_call(along_z, fields)
-    state, sends = outer_call(0, odd, inner, halo, fields, None)
-    old = []
-    for stage in (1, 2):
+    state, old = fields, []
+    for stage in range(3):
         halo, inner = exchange(sends), inner_call(along_z, state)
-        old.append(gram_call(basis, snapshots, stage - 1))
-        halo, inner, old = lax.optimization_barrier((halo, inner, old))
+        if stage < 2:
+            old.append(gram_call(basis, snapshots, stage))
+            halo, inner, old = lax.optimization_barrier((halo, inner, old))
         state, sends = outer_call(stage, odd, inner, halo, state, fields)
     final, (newest,) = state, sends
     grams, merged = zip(*old)

time: 72.4 us -> 71.4 us (0.986)
  Pallas kernels: 30 us -> 29 us
    ppermute x1, starting transfers between devices: 0.29 us -> 2.19 us  [total_parts(): part = part + lax.ppermute(part, 'gx', [(i, i ^ 1) for i in range(count)])]
    ppermute x6, starting transfers between devices: 11.3 us -> 9.98 us  [shifted(): return lax.ppermute(block, axis, route)]
    pallas_call x11, Pallas kernels: 30 us -> 29 us  [call(): pl.pallas_call(kernel, out_shape=out_shape, scratch_shapes=list(scratch),...]
  transfers between devices with their start and end apart: 14 -> 14, of which waited for: 3 -> 3; matrix products, arithmetic and copies ran while one was open for 0% -> 0% of each run, Pallas kernels for 18% -> 17%
where the time goes in v4:
time: 71.4 us; the launch traced here: 71.1 us
  starting transfers between devices  29.4 us (41%)
  Pallas kernels  29 us (41%)
  waiting for transfers between devices  11.1 us (16%)
  between operations  0.99 us (1%)
  local copies, waits for them, and re-layouts  0.74 us (1%)
    pallas_call x11, Pallas kernels, call(): pl.pallas_call(kernel, out_shape=out_shape, scratch_shapes=list(scratch),...  29 us
    all_to_all x1, waiting for transfers between devices, total_parts(): lax.all_to_all(copies, ('gx', 'gy'), 0, 0, tiled=True, axis_index_groups=...  10.1 us
    ppermute x6, starting transfers between devices, shifted(): return lax.ppermute(block, axis, route)  9.98 us
    ppermute x3, starting transfers between devices, exchange(): near = lax.ppermute(to_near, 'gx', [(i, i ^ 1) for i in range(count)])  7.51 us
    all_to_all x1, starting transfers between devices, total_parts(): lax.all_to_all(copies, ('gx', 'gy'), 0, 0, tiled=True, axis_index_groups=...  6.33 us
    ppermute x3, starting transfers between devices, exchange(): far = lax.ppermute(to_far, 'gx', pairs + [(j, i) for i, j in pairs])  3.36 us
    ppermute x1, starting transfers between devices, total_parts(): part = part + lax.ppermute(part, 'gx', [(i, i ^ 1) for i in range(count)])  2.19 us
  transfers between devices with their start and end apart: 14, of which 3 were waited for; matrix products, arithmetic and copies ran while one was open for 0% of the time, Pallas kernels for 17%

profile of v4, /device:TPU:1, one launch (start us, length us, event | category | flops | bytes accessed | tf_op | source)
XLA Modules:
  0.0 71.1 jit_solution(5462156041216591119)
XLA Ops:
  0.6 1.3 %shard_map.110 = (f32[8,4096]{1,0:T(8,128)S(1)}, f32[3,8,4096]{2,1,0:T(8,128)S(1)}, f32[8,4096]{1,0:T(8,128)S(1)}, bf16[2,256,256]{2,1,0:T(8,128)(2,1)S(1)}, f32...) custom-call(s32[1]{0:T(128)} %bitcast.odd.refs_0_, ...), custom_call_target="tpu_custom_call" | custom-call | bytes 1000000 | tf_op jit(solution)/shard_map/pallas_call | solution.py:286
  1.9 2.7 %collective-permute-start = (f32[5,8,2048]{2,1,0:T(8,128)S(1)}, f32[5,8,2048]{2,1,0:T(8,128)S(1)}, u32[]{:S(2)}, u32[]{:S(2)}) collective-permute-start(f32[5,8,2048]{2,1,0:T(8,128)S(1)} %get-tuple-element.62), channel_id=1, source_target_pairs={{4,8},{12,16},{20,24},{28,32},{36,40},{44,48},{52,56},{60,64},{68,... | collective-permute-start | bytes 983048 | tf_op jit(solution)/shard_map/ppermute | solution.py:642
  4.6 3.6 %collective-permute-start.1 = (f32[5,8,2048]{2,1,0:T(8,128)S(1)}, f32[5,8,2048]{2,1,0:T(8,128)S(1)}, u32[]{:S(2)}, u32[]{:S(2)}) collective-permute-start(f32[5,8,2048]{2,1,0:T(8,128)S(1)} %get-tuple-element.63), channel_id=1, source_target_pairs={{0,4},{4,0},{8,12},{12,8},{16,20},{20,16},{24,28},{28,24},{32,36},... | collective-permute-start | bytes 983048 | tf_op jit(solution)/shard_map/ppermute | solution.py:643
  8.2 1.6 %collective-permute-start.2 = (f32[5,8,256]{2,1,0:T(8,128)S(1)}, f32[5,8,256]{2,1,0:T(8,128)S(1)}, u32[]{:S(2)}, u32[]{:S(2)}) collective-permute-start(f32[5,8,256]{2,1,0:T(8,128)S(1)} %get-tuple-element.64), channel_id=1, source_target_pairs={{0,1},{1,2},{2,3},{3,0},{4,5},{5,6},{6,7},{7,4},{8,9},{9,10},{10,1... | collective-permute-start | bytes 122888 | tf_op jit(solution)/shard_map/ppermute | solution.py:635
  9.8 2.1 %collective-permute-start.3 = (f32[5,8,256]{2,1,0:T(8,128)S(1)}, f32[5,8,256]{2,1,0:T(8,128)S(1)}, u32[]{:S(2)}, u32[]{:S(2)}) collective-permute-start(f32[5,8,256]{2,1,0:T(8,128)S(1)} %get-tuple-element.65), channel_id=1, source_target_pairs={{0,3},{1,0},{2,1},{3,2},{4,7},{5,4},{6,5},{7,6},{8,11},{9,8},{10,9... | collective-permute-start | bytes 122888 | tf_op jit(solution)/shard_map/ppermute | solution.py:635
  11.9 1.5 %shard_map.111 = (f32[9,8,4096]{2,1,0:T(8,128)S(1)}, f32[10,8,4608]{2,1,0:T(8,128)S(1)}) custom-call(bf16[2,256,256]{2,1,0:T(8,128)(2,1)S(1)} %get-tuple-element.61.along_z, f32[8,4096]{1,0:T(8,128)S(1)} %get-tuple-element.66.rho.refs_7_.refs_10_, f32[3,8,4096]{2,1,0:T(8,128)S(1)} %get-tuple-element.67.mom.refs_8_.refs_11_, ...), custom_call_target="tpu_custom_call" | custom-call | flops 13107200 | bytes 3000000 | tf_op jit(solution)/shard_map/pallas_call | solution.py:286
  13.5 3.7 %shard_map.112 = (f32[8,128]{1,0:T(8,128)S(1)}, bf16[3,256,2048]{2,1,0:T(8,128)(2,1)S(1)}) custom-call(bf16[16,3,8,4096]{3,2,1,0:T(8,128)(2,1)} %basis_h.3, bf16[15,3,8,4096]{3,2,1,0:T(8,128)(2,1)} %snaps_h.3), custom_call_target="tpu_custom_call" | custom-call | flops 805306368 | bytes 3047424 | tf_op jit(solution)/shard_map/pallas_call | solution.py:286
  17.3 1.6 %shard_map.113 = (f32[8,4096]{1,0:T(8,128)S(1)}, f32[3,8,4096]{2,1,0:T(8,128)S(1)}, f32[8,4096]{1,0:T(8,128)S(1)}, f32[9,8,4096]{2,1,0:T(8,128)S(1)}, f32[5,8,20...) custom-call(s32[1]{0:T(128)} %bitcast.odd.refs_0_, ...), custom_call_target="tpu_custom_call", output_to_operand_aliasing={{3}: (1, {})} | custom-call | flops 13107200 | bytes 3000000 | tf_op jit(solution)/shard_map/pallas_call | solution.py:286
  19.0 0.9 %collective-permute-start.5 = (f32[5,8,2048]{2,1,0:T(8,128)S(1)}, f32[5,8,2048]{2,1,0:T(8,128)S(1)}, u32[]{:S(2)}, u32[]{:S(2)}) collective-permute-start(f32[5,8,2048]{2,1,0:T(8,128)S(1)} %get-tuple-element.80), channel_id=1, source_target_pairs={{0,4},{4,0},{8,12},{12,8},{16,20},{20,16},{24,28},{28,24},{32,36},... | collective-permute-start | bytes 983048 | tf_op jit(solution)/shard_map/ppermute | solution.py:643
  19.9 1.4 %collective-permute-start.6 = (f32[5,8,256]{2,1,0:T(8,128)S(1)}, f32[5,8,256]{2,1,0:T(8,128)S(1)}, u32[]{:S(2)}, u32[]{:S(2)}) collective-permute-start(f32[5,8,256]{2,1,0:T(8,128)S(1)} %get-tuple-element.81), channel_id=1, source_target_pairs={{0,1},{1,2},{2,3},{3,0},{4,5},{5,6},{6,7},{7,4},{8,9},{9,10},{10,1... | collective-permute-start | bytes 122888 | tf_op jit(solution)/shard_map/ppermute | solution.py:635
  21.3 2.1 %collective-permute-start.7 = (f32[5,8,256]{2,1,0:T(8,128)S(1)}, f32[5,8,256]{2,1,0:T(8,128)S(1)}, u32[]{:S(2)}, u32[]{:S(2)}) collective-permute-start(f32[5,8,256]{2,1,0:T(8,128)S(1)} %get-tuple-element.82), channel_id=1, source_target_pairs={{0,3},{1,0},{2,1},{3,2},{4,7},{5,4},{6,5},{7,6},{8,11},{9,8},{10,9... | collective-permute-start | bytes 122888 | tf_op jit(solution)/shard_map/ppermute | solution.py:635
  23.4 3.7 %shard_map.115 = (f32[8,128]{1,0:T(8,128)S(1)}, bf16[3,256,2048]{2,1,0:T(8,128)(2,1)S(1)}) custom-call(bf16[16,3,8,4096]{3,2,1,0:T(8,128)(2,1)} %basis_h.3, bf16[15,3,8,4096]{3,2,1,0:T(8,128)(2,1)} %snaps_h.3), custom_call_target="tpu_custom_call" | custom-call | flops 805306368 | bytes 3047424 | tf_op jit(solution)/shard_map/pallas_call | solution.py:286
  27.2 1.5 %shard_map.114 = (f32[9,8,4096]{2,1,0:T(8,128)S(1)}, f32[10,8,4608]{2,1,0:T(8,128)S(1)}) custom-call(bf16[2,256,256]{2,1,0:T(8,128)(2,1)S(1)} %get-tuple-element.61.along_z, f32[8,4096]{1,0:T(8,128)S(1)} %get-tuple-element.83.rho.refs_7_, f32[3,8,4096]{2,1,0:T(8,128)S(1)} %get-tuple-element.84.mom.refs_8_, f32[8,4096]{1,0:T(8,128)S(1)} %get-tuple-element.85.energy.refs_9_), custom_call_target="tpu_custom_call" | custom-call | flops 13107200 | bytes 3000000 | tf_op jit(solution)/shard_map/pallas_call | solution.py:286
  28.8 1.7 %shard_map.116 = (f32[8,4096]{1,0:T(8,128)S(1)}, f32[3,8,4096]{2,1,0:T(8,128)S(1)}, f32[8,4096]{1,0:T(8,128)S(1)}, f32[9,8,4096]{2,1,0:T(8,128)S(1)}, f32[5,8,20...) custom-call(s32[1]{0:T(128)} %bitcast.odd.refs_0_, ...), custom_call_target="tpu_custom_call", output_to_operand_aliasing={{3}: (1, {})} | custom-call | flops 13107200 | bytes 3000000 | tf_op jit(solution)/shard_map/pallas_call | solution.py:286
  31.0 3.0 %collective-permute-start.9 = (f32[5,8,2048]{2,1,0:T(8,128)S(1)}, f32[5,8,2048]{2,1,0:T(8,128)S(1)}, u32[]{:S(2)}, u32[]{:S(2)}) collective-permute-start(f32[5,8,2048]{2,1,0:T(8,128)S(1)} %get-tuple-element.104), channel_id=1, source_target_pairs={{0,4},{4,0},{8,12},{12,8},{16,20},{20,16},{24,28},{28,24},{32,36},... | collective-permute-start | bytes 983048 | tf_op jit(solution)/shard_map/ppermute | solution.py:643
  34.0 2.7 %collective-permute-start.11 = (f32[5,8,256]{2,1,0:T(8,128)S(1)}, f32[5,8,256]{2,1,0:T(8,128)S(1)}, u32[]{:S(2)}, u32[]{:S(2)}) collective-permute-start(f32[5,8,256]{2,1,0:T(8,128)S(1)} %get-tuple-element.106), channel_id=1, source_target_pairs={{0,3},{1,0},{2,1},{3,2},{4,7},{5,4},{6,5},{7,6},{8,11},{9,8},{10,9... | collective-permute-start | bytes 122888 | tf_op jit(solution)/shard_map/ppermute | solution.py:635
  36.7 1.5 %shard_map.117 = (f32[9,8,4096]{2,1,0:T(8,128)S(1)}, f32[10,8,4608]{2,1,0:T(8,128)S(1)}) custom-call(bf16[2,256,256]{2,1,0:T(8,128)(2,1)S(1)} %get-tuple-element.61.along_z, f32[8,4096]{1,0:T(8,128)S(1)} %get-tuple-element.98.rho.refs_7_, f32[3,8,4096]{2,1,0:T(8,128)S(1)} %get-tuple-element.99.mom.refs_8_, f32[8,4096]{1,0:T(8,128)S(1)} %get-tuple-element.100.energy.refs_9_), custom_call_target="tpu_custom_call" | custom-call | flops 13107200 | bytes 3000000 | tf_op jit(solution)/shard_map/pallas_call | solution.py:286
  38.4 2.4 %shard_map.118 = (f32[8,4096]{1,0:T(8,128)}, f32[3,8,4096]{2,1,0:T(8,128)}, f32[8,4096]{1,0:T(8,128)}, f32[9,8,4096]{2,1,0:T(8,128)S(1)}, f32[3,8,4096]{2,1,0:T(8,128)S(1)}) custom-call(s32[1]{0:T(128)} %bitcast.odd.refs_0_, f32[9,8,4096]{2,1,0:T(8,128)S(1)} %get-tuple-element.101.refs_1_, ...), custom_call_target="tpu_custom_call", output_to_operand_aliasing={{3}: (1, {})} | custom-call | flops 13107200 | bytes 3000000 | tf_op jit(solution)/shard_map/pallas_call | solution.py:286
  40.9 1.8 %shard_map.119 = f32[8,128]{1,0:T(8,128)S(1)} custom-call(bf16[3,256,2048]{2,1,0:T(8,128)(2,1)S(1)} %get-tuple-element.110.merged_a, bf16[3,256,2048]{2,1,0:T(8,128)(2,1)S(1)} %get-tuple-element.111.merged_b, f32[3,8,4096]{2,1,0:T(8,128)S(1)} %get-tuple-element.112.newest, f32[8,128]{1,0:T(8,128)S(1)} %get-tuple-element.113.gram_a, ...), custom_call_target="tpu_custom_call" | custom-call | flops 6094848 | bytes 6094848 | tf_op jit(solution)/shard_map/pallas_call | solution.py:286
  42.6 2.2 %collective-permute-start.12 = (f32[8,128]{1,0:T(8,128)S(1)}, f32[8,128]{1,0:T(8,128)S(1)}, u32[]{:S(2)}, u32[]{:S(2)}) collective-permute-start(f32[8,128]{1,0:T(8,128)S(1)} %shard_map.119), channel_id=1, source_target_pairs={{0,4},{4,0},{8,12},{12,8},{16,20},{20,16},{24,28},{28,24},{32,36},... | collective-permute-start | bytes 12296 | tf_op jit(solution)/shard_map/ppermute | solution.py:651
  44.8 0.8 %collective-permute-done.12 = f32[8,128]{1,0:T(8,128)S(1)} collective-permute-done((f32[8,128]{1,0:T(8,128)S(1)}, f32[8,128]{1,0:T(8,128)S(1)}, u32[]{:S(2)}, u32[]{:S(2)}) %collective-permute-start.12) | collective-permute-done | bytes 4128 | tf_op jit(solution)/shard_map/ppermute | solution.py:651
  46.4 6.3 %all-to-all-start = ((f32[64,8,128]{2,1,0:T(8,128)}), f32[64,8,128]{2,1,0:T(8,128)S(1)}, u32[]{:S(2)}, u32[]{:S(2)}) async-start(f32[64,8,128]{2,1,0:T(8,128)} %broadcast_in_dim.13), calls=%async_computation | async-start | bytes 524288 | tf_op jit(solution)/shard_map/all_to_all | solution.py:656
  52.7 10.1 %all-to-all-done.parts = f32[64,8,128]{2,1,0:T(8,128)S(1)} async-done(((f32[64,8,128]{2,1,0:T(8,128)}), f32[64,8,128]{2,1,0:T(8,128)S(1)}, u32[]{:S(2)}, u32[]{:S(2)}) %all-to-all-start) | async-done | bytes 262176 | tf_op jit(solution)/shard_map/all_to_all | solution.py:656
  62.8 8.2 %shard_map.120 = (bf16[32,3,8,4096]{3,2,1,0:T(8,128)(2,1)}, f32[32,32]{1,0:T(8,128)}) custom-call(f32[64,8,128]{2,1,0:T(8,128)S(1)} %all-to-all-done.parts, f32[1,32]{1,0:T(1,128)S(1)} %pad_bitcast_fusion.scale, bf16[3,256,2048]{2,1,0:T(8,128)(2,1)} %copy-done, bf16[3,256,2048]{2,1,0:T(8,128)(2,1)} %copy-done.1, f32[3,8,4096]{2,1,0:T(8,128)S(1)} %get-tuple-element.112.newest), custom_call_target="tpu_custom_call" | custom-call | flops 3221225472 | bytes 12386304 | tf_op jit(solution)/shard_map/pallas_call | solution.py:286
  (24 shorter events, 1.6 us)
Async XLA Ops:
  1.9 15.3 %collective-permute-start = (f32[5,8,2048]{2,1,0:T(8,128)S(1)}, f32[5,8,2048]{2,1,0:T(8,128)S(1)}, u32[]{:S(2)}, u32[]{:S(2)}) collective-permute-start(f32[5,8,2048]{2,1,0:T(8,128)S(1)} %get-tuple-element.62), channel_id=1, source_target_pairs={{4,8},{12,16},{20,24},{28,32},{36,40},{44,48},{52,56},{60,64},{68,... | collective-permute-start | bytes 983048 | tf_op jit(solution)/shard_map/ppermute | solution.py:642
  4.6 12.6 %collective-permute-start.1 = (f32[5,8,2048]{2,1,0:T(8,128)S(1)}, f32[5,8,2048]{2,1,0:T(8,128)S(1)}, u32[]{:S(2)}, u32[]{:S(2)}) collective-permute-start(f32[5,8,2048]{2,1,0:T(8,128)S(1)} %get-tuple-element.63), channel_id=1, source_target_pairs={{0,4},{4,0},{8,12},{12,8},{16,20},{20,16},{24,28},{28,24},{32,36},... | collective-permute-start | bytes 983048 | tf_op jit(solution)/shard_map/ppermute | solution.py:643
  8.2 9.1 %collective-permute-start.2 = (f32[5,8,256]{2,1,0:T(8,128)S(1)}, f32[5,8,256]{2,1,0:T(8,128)S(1)}, u32[]{:S(2)}, u32[]{:S(2)}) collective-permute-start(f32[5,8,256]{2,1,0:T(8,128)S(1)} %get-tuple-element.64), channel_id=1, source_target_pairs={{0,1},{1,2},{2,3},{3,0},{4,5},{5,6},{6,7},{7,4},{8,9},{9,10},{10,1... | collective-permute-start | bytes 122888 | tf_op jit(solution)/shard_map/ppermute | solution.py:635
  9.8 7.4 %collective-permute-start.3 = (f32[5,8,256]{2,1,0:T(8,128)S(1)}, f32[5,8,256]{2,1,0:T(8,128)S(1)}, u32[]{:S(2)}, u32[]{:S(2)}) collective-permute-start(f32[5,8,256]{2,1,0:T(8,128)S(1)} %get-tuple-element.65), channel_id=1, source_target_pairs={{0,3},{1,0},{2,1},{3,2},{4,7},{5,4},{6,5},{7,6},{8,11},{9,8},{10,9... | collective-permute-start | bytes 122888 | tf_op jit(solution)/shard_map/ppermute | solution.py:635
  17.2 23.6 %copy-start = (bf16[3,256,2048]{2,1,0:T(8,128)(2,1)}, bf16[3,256,2048]{2,1,0:T(8,128)(2,1)S(1)}, u32[]{:S(2)}) copy-start(bf16[3,256,2048]{2,1,0:T(8,128)(2,1)S(1)} %get-tuple-element.110.merged_a) | copy-start | bytes 9437188
  18.9 9.9 %collective-permute-start.4 = (f32[5,8,2048]{2,1,0:T(8,128)S(1)}, f32[5,8,2048]{2,1,0:T(8,128)S(1)}, u32[]{:S(2)}, u32[]{:S(2)}) collective-permute-start(f32[5,8,2048]{2,1,0:T(8,128)S(1)} %get-tuple-element.79), channel_id=1, source_target_pairs={{4,8},{12,16},{20,24},{28,32},{36,40},{44,48},{52,56},{60,64},{68,... | collective-permute-start | bytes 983048 | tf_op jit(solution)/shard_map/ppermute | solution.py:642
  19.0 9.8 %collective-permute-start.5 = (f32[5,8,2048]{2,1,0:T(8,128)S(1)}, f32[5,8,2048]{2,1,0:T(8,128)S(1)}, u32[]{:S(2)}, u32[]{:S(2)}) collective-permute-start(f32[5,8,2048]{2,1,0:T(8,128)S(1)} %get-tuple-element.80), channel_id=1, source_target_pairs={{0,4},{4,0},{8,12},{12,8},{16,20},{20,16},{24,28},{28,24},{32,36},... | collective-permute-start | bytes 983048 | tf_op jit(solution)/shard_map/ppermute | solution.py:643
  19.9 8.8 %collective-permute-start.6 = (f32[5,8,256]{2,1,0:T(8,128)S(1)}, f32[5,8,256]{2,1,0:T(8,128)S(1)}, u32[]{:S(2)}, u32[]{:S(2)}) collective-permute-start(f32[5,8,256]{2,1,0:T(8,128)S(1)} %get-tuple-element.81), channel_id=1, source_target_pairs={{0,1},{1,2},{2,3},{3,0},{4,5},{5,6},{6,7},{7,4},{8,9},{9,10},{10,1... | collective-permute-start | bytes 122888 | tf_op jit(solution)/shard_map/ppermute | solution.py:635
  21.3 7.4 %collective-permute-start.7 = (f32[5,8,256]{2,1,0:T(8,128)S(1)}, f32[5,8,256]{2,1,0:T(8,128)S(1)}, u32[]{:S(2)}, u32[]{:S(2)}) collective-permute-start(f32[5,8,256]{2,1,0:T(8,128)S(1)} %get-tuple-element.82), channel_id=1, source_target_pairs={{0,3},{1,0},{2,1},{3,2},{4,7},{5,4},{6,5},{7,6},{8,11},{9,8},{10,9... | collective-permute-start | bytes 122888 | tf_op jit(solution)/shard_map/ppermute | solution.py:635
  27.2 13.7 %copy-start.1 = (bf16[3,256,2048]{2,1,0:T(8,128)(2,1)}, bf16[3,256,2048]{2,1,0:T(8,128)(2,1)S(1)}, u32[]{:S(2)}) copy-start(bf16[3,256,2048]{2,1,0:T(8,128)(2,1)S(1)} %get-tuple-element.111.merged_b) | copy-start | bytes 9437188
  30.4 8.0 %collective-permute-start.8 = (f32[5,8,2048]{2,1,0:T(8,128)S(1)}, f32[5,8,2048]{2,1,0:T(8,128)S(1)}, u32[]{:S(2)}, u32[]{:S(2)}) collective-permute-start(f32[5,8,2048]{2,1,0:T(8,128)S(1)} %get-tuple-element.103), channel_id=1, source_target_pairs={{4,8},{12,16},{20,24},{28,32},{36,40},{44,48},{52,56},{60,64},{68,... | collective-permute-start | bytes 983048 | tf_op jit(solution)/shard_map/ppermute | solution.py:642
  31.0 7.4 %collective-permute-start.9 = (f32[5,8,2048]{2,1,0:T(8,128)S(1)}, f32[5,8,2048]{2,1,0:T(8,128)S(1)}, u32[]{:S(2)}, u32[]{:S(2)}) collective-permute-start(f32[5,8,2048]{2,1,0:T(8,128)S(1)} %get-tuple-element.104), channel_id=1, source_target_pairs={{0,4},{4,0},{8,12},{12,8},{16,20},{20,16},{24,28},{28,24},{32,36},... | collective-permute-start | bytes 983048 | tf_op jit(solution)/shard_map/ppermute | solution.py:643
  34.0 4.4 %collective-permute-start.10 = (f32[5,8,256]{2,1,0:T(8,128)S(1)}, f32[5,8,256]{2,1,0:T(8,128)S(1)}, u32[]{:S(2)}, u32[]{:S(2)}) collective-permute-start(f32[5,8,256]{2,1,0:T(8,128)S(1)} %get-tuple-element.105), channel_id=1, source_target_pairs={{0,1},{1,2},{2,3},{3,0},{4,5},{5,6},{6,7},{7,4},{8,9},{9,10},{10,1... | collective-permute-start | bytes 122888 | tf_op jit(solution)/shard_map/ppermute | solution.py:635
  34.0 4.4 %collective-permute-start.11 = (f32[5,8,256]{2,1,0:T(8,128)S(1)}, f32[5,8,256]{2,1,0:T(8,128)S(1)}, u32[]{:S(2)}, u32[]{:S(2)}) collective-permute-start(f32[5,8,256]{2,1,0:T(8,128)S(1)} %get-tuple-element.106), channel_id=1, source_target_pairs={{0,3},{1,0},{2,1},{3,2},{4,7},{5,4},{6,5},{7,6},{8,11},{9,8},{10,9... | collective-permute-start | bytes 122888 | tf_op jit(solution)/shard_map/ppermute | solution.py:635
  40.9 11.8 %copy-start.2 = (f32[16]{0:T(128)S(1)}, f32[16]{0:T(128)}, u32[]{:S(2)}) copy-start(f32[16]{0:T(128)} %param.11) | copy-start | bytes 196
  42.6 3.0 %collective-permute-start.12 = (f32[8,128]{1,0:T(8,128)S(1)}, f32[8,128]{1,0:T(8,128)S(1)}, u32[]{:S(2)}, u32[]{:S(2)}) collective-permute-start(f32[8,128]{1,0:T(8,128)S(1)} %shard_map.119), channel_id=1, source_target_pairs={{0,4},{4,0},{8,12},{12,8},{16,20},{20,16},{24,28},{28,24},{32,36},... | collective-permute-start | bytes 12296 | tf_op jit(solution)/shard_map/ppermute | solution.py:651
  46.4 16.4 %all-to-all-start = ((f32[64,8,128]{2,1,0:T(8,128)}), f32[64,8,128]{2,1,0:T(8,128)S(1)}, u32[]{:S(2)}, u32[]{:S(2)}) async-start(f32[64,8,128]{2,1,0:T(8,128)} %broadcast_in_dim.13), calls=%async_computation | async-start | bytes 524288 | tf_op jit(solution)/shard_map/all_to_all | solution.py:656
